TPU v7x, 32 devices: a whole 2x2x4 slice. The times are simulated.
32 devices in a mesh: groups: 2 (over y), wide: 4 (over z), narrow: 4 (over x, core).
Axes of the slice: x: 2, y: 2, z: 4, core: 2. Of those that a mesh axis runs over, the one named last changes fastest.
Arguments:
- tokens: bfloat16 [128, 8192], P(('groups', 'wide'), 'narrow'), parts along dimension 0, may hold values from -60 to 60
- signs: int32 [128, 8192], P(('groups', 'wide'), 'narrow'), parts along dimension 0, may hold values 0 or 1
- magnitude: float32 [128, 8192], P(('groups', 'wide'), 'narrow'), parts along dimension 0, may hold values from 0.05 to 0.5
- target: bfloat16 [128, 8192], P(('groups', 'wide'), 'narrow'), parts along dimension 0, may hold values from -6 to 6
- norm_gain: float32 [8192], P('narrow'), may hold values from 0.1 to 1.9
- gate_weight: bfloat16 [8192, 20480], P('narrow', 'wide'), may hold values from -0.0625 to 0.0625
- up_weight: bfloat16 [8192, 20480], P('narrow', 'wide'), may hold values from -0.0625 to 0.0625
- down_weight: bfloat16 [20480, 8192], P('wide', 'narrow'), may hold values from -0.0390625 to 0.0390625
Outputs:
- new_delta: float32 [128, 8192], P(('groups', 'wide'), 'narrow'), parts along dimension 0
There are 2 independent parts, one for each index of `groups`. A program takes and returns all parts, laid end to end along the dimension named above; an argument that names none is the same for every part. Nothing has to cross between parts.
All inputs are finite; a program needn't handle non-finite values. No bound on the sum of `signs` on one device may be relied on, other than what follows from the above.
Results may differ from a plain program's by a relative error of at most 0.0034.
Values may be sent and summed in bfloat16 or wider, within the bound.
No kernel may reach another device: no remote copies, remote signals or barrier semaphores. Data moves between devices by JAX's collectives and lax.ppermute only.
A program may use at most 192 MiB of HBM per device.

v0:
```python
import jax
import jax.numpy as jnp
from jax import lax
from jax.sharding import PartitionSpec as P

D = 8192


EPS = 1e-05
ASCENT = 0.5


def gate_terms(sums, hidden_width):
    gate = sums[:, :hidden_width]
    up = sums[:, hidden_width : 2 * hidden_width]
    back_hidden = sums[:, 2 * hidden_width :]
    sig = jax.nn.sigmoid(gate)
    back_gate = back_hidden * up * sig * (1.0 + gate * (1.0 - sig))
    back_up = back_hidden * gate * sig
    return jnp.concatenate([back_gate, back_up], axis=1).astype(jnp.bfloat16)


def on_device(tokens, signs, magnitude, target, norm_gain, gate_weight, up_weight, down_weight):
    hidden_width = gate_weight.shape[1]
    delta = (2 * signs - 1).astype(jnp.float32) * magnitude
    latent = tokens.astype(jnp.float32) + delta
    squares = lax.psum(jnp.sum(latent * latent, axis=1), "narrow")
    scale = lax.rsqrt(squares[:, None] / D + EPS)
    unit = latent * scale
    normed = (unit * norm_gain).astype(jnp.bfloat16)
    both_weights = jnp.concatenate([gate_weight, up_weight], axis=1)
    stacked = jnp.stack([normed, target], axis=0)
    piece = lax.all_gather(stacked, "wide", axis=1, tiled=True)
    forward = jnp.dot(piece[0], both_weights, preferred_element_type=jnp.float32)
    backward = lax.dot_general(
        piece[1], down_weight, (((1,), (1,)), ((), ())), preferred_element_type=jnp.float32
    )
    partial_value = jnp.concatenate([forward, backward], axis=1)
    shares = lax.psum_scatter(partial_value, "narrow", scatter_dimension=0, tiled=True)
    back_share = gate_terms(shares, hidden_width)
    back_both = lax.all_gather(back_share, "narrow", axis=0, tiled=True)
    piece = back_both
    back_normed = lax.psum_scatter(
        lax.dot_general(
            piece, both_weights, (((1,), (1,)), ((), ())), preferred_element_type=jnp.float32
        ),
        "wide",
        scatter_dimension=0,
        tiled=True,
    )
    scaled = back_normed * norm_gain
    inner = lax.psum(jnp.sum(scaled * unit, axis=1), "narrow")
    back_latent = scale * (scaled - unit * (inner[:, None] / D))
    return delta + ASCENT * (target.astype(jnp.float32) + back_latent)


def solution(mesh):
    in_specs = (
        P(("groups", "wide"), "narrow"),
        P(("groups", "wide"), "narrow"),
        P(("groups", "wide"), "narrow"),
        P(("groups", "wide"), "narrow"),
        P("narrow"),
        P("narrow", "wide"),
        P("narrow", "wide"),
        P("wide", "narrow"),
    )
    out_specs = P(("groups", "wide"), "narrow")
    return jax.shard_map(
        on_device, mesh=mesh, in_specs=in_specs, out_specs=out_specs, check_vma=False
    )
```

profile of v0, /device:TPU:0, one launch (start us, length us, event | category | flops | bytes accessed | tf_op | source)
XLA Modules:
  0.0 213.0 jit_solution(7017977959071597468)
XLA Ops:
  6.5 0.0 reduce-scatter.3.cloned.1.call-start
  6.5 1.1 multiply_reduce_fusion.1
  7.7 8.3 %psum.14 = f32[16]{0:T(128)S(1)} all-reduce(f32[16]{0:T(128)S(1)} %get-tuple-element.5), channel_id=1, replica_groups=mesh['groups'=2,'wide'=4,'narrow'=4] {'narrow'}, use_global_device_ids=true, to_apply=%region_1.0 | all-reduce | flops 16 | bytes 128 | tf_op jit(solution)/shard_map/psum | solution.py:27
  16.0 0.9 fusion.5
  17.0 0.9 pad_maximum_fusion.2
  17.8 0.0 slice-start
  17.8 15.6 %all_gather.6 = bf16[2,64,2048]{2,1,0:T(8,128)(2,1)S(1)} all-gather(bf16[2,16,2048]{2,1,0:T(8,128)(2,1)S(1)} %pad_maximum_fusion.2), channel_id=1, replica_groups=mesh['groups'=2,'wide'=4,'narrow'=4] {'wide'}, dimensions={1}, use_global_device_ids=true | all-gather | bytes 655360 | tf_op jit(solution)/shard_map/all_gather | solution.py:33
  33.5 0.0 slice-start.1
  33.5 0.0 slice-start.2
  33.5 0.0 slice-start.3
  33.5 0.0 slice-start.4
  33.5 20.3 %constant_dynamic-update-slice_fusion.1 = bf16[2048,10240]{1,0:T(8,128)(2,1)} fusion(bf16[2048,5120]{1,0:T(8,128)(2,1)} %param.13), kind=kLoop, calls=%fused_computation.21 | loop fusion | bytes 41943040
  53.7 0.0 slice-done
  53.7 0.0 slice-done.1
  53.7 0.0 slice-done.2
  53.7 0.0 slice-done.3
  53.8 0.0 slice-done.4
  53.8 8.5 %constant_dynamic-update-slice_fusion = bf16[2048,10240]{1,0:T(8,128)(2,1)} fusion(bf16[2048,10240]{1,0:T(8,128)(2,1)} %constant_dynamic-update-slice_fusion.1, bf16[2048,5120]{1,0:T(8,128)(2,1)S(1)} %bitcast.14), kind=kLoop, calls=%fused_computation.20 | loop fusion | bytes 41943040 | tf_op jit(solution)/shard_map/concatenate | solution.py:31
  62.3 16.7 %fusion.4 = f32[64,10240]{1,0:T(8,128)S(1)} fusion(bf16[2048,10240]{1,0:T(8,128)(2,1)} %constant_dynamic-update-slice_fusion, bf16[2,64,2048]{2,1,0:T(8,128)(2,1)S(1)} %all_gather.6), kind=kOutput, calls=%fused_computation.11 | convolution fusion | flops 2684354560 | bytes 44826624 | tf_op jit(solution)/shard_map/dot_general | solution.py:34
  79.1 10.6 %fusion.3 = f32[64,5120]{1,0:T(8,128)S(1)} fusion(bf16[5120,2048]{1,0:T(8,128)(2,1)} %param.15, bf16[2,64,2048]{2,1,0:T(8,128)(2,1)S(1)} %all_gather.6), kind=kOutput, calls=%fused_computation.9 | convolution fusion | flops 1342177280 | bytes 22544384 | tf_op jit(solution)/shard_map/dot_general | solution.py:35
  89.6 2.1 %pad_maximum_fusion = f32[64,15360]{1,0:T(8,128)} fusion(f32[64,5120]{1,0:T(8,128)S(1)} %fusion.3, f32[64,10240]{1,0:T(8,128)S(1)} %fusion.4), kind=kLoop, calls=%fused_computation | loop fusion | flops 983040 | bytes 7864320 | tf_op jit(solution)/shard_map/concatenate | solution.py:38
  91.8 0.0 reduce-scatter.3.cloned.1.call-update
  91.8 0.0 all-gather.2.cloned.1.call-start
  91.9 44.1 %reduce-scatter.3.cloned.1.call-done = f32[16,15360]{1,0:T(8,128)} async-done(((f32[64,15360]{1,0:T(8,128)}), f32[16,15360]{1,0:T(8,128)}) %reduce-scatter.3.cloned.1.call-update) | async-done | bytes 983056 | tf_op jit(solution)/shard_map/reduce_scatter | solution.py:39
  136.0 1.3 fusion.2
  137.3 0.8 pad_maximum_fusion.1
  138.1 0.0 all-gather.2.cloned.1.call-update
  138.1 0.0 copy-start
  138.1 0.0 copy-start.2
  138.1 0.0 copy-start.1
  138.1 0.0 reduce-scatter.5.cloned.1.call-start
  138.2 18.2 %all-gather.2.cloned.1.call-done = bf16[64,10240]{1,0:T(8,128)(2,1)} async-done(((bf16[16,10240]{1,0:T(8,128)(2,1)}), bf16[64,10240]{1,0:T(8,128)(2,1)}) %all-gather.2.cloned.1.call-update) | async-done | bytes 1310736 | tf_op jit(solution)/shard_map/all_gather | solution.py:41
  156.4 19.8 %fusion.6 = f32[64,2048]{1,0:T(8,128)} fusion(bf16[64,10240]{1,0:T(8,128)(2,1)} %all-gather.2.cloned.1.call-done, bf16[2048,10240]{1,0:T(8,128)(2,1)} %constant_dynamic-update-slice_fusion), kind=kOutput, calls=%fused_computation.24 | convolution fusion | flops 2684354560 | bytes 43778048 | tf_op jit(solution)/shard_map/dot_general | solution.py:44
  176.2 0.0 reduce-scatter.5.cloned.1.call-update
  176.2 21.8 %reduce-scatter.5.cloned.1.call-done = f32[16,2048]{1,0:T(8,128)} async-done(((f32[64,2048]{1,0:T(8,128)}), f32[16,2048]{1,0:T(8,128)}) %reduce-scatter.5.cloned.1.call-update) | async-done | bytes 131088 | tf_op jit(solution)/shard_map/reduce_scatter | solution.py:43
  198.0 0.0 copy-done
  198.0 0.0 copy-done.2
  198.0 1.1 multiply_reduce_fusion
  199.1 5.7 %psum.15 = f32[16]{0:T(128)S(1)} all-reduce(f32[16]{0:T(128)S(1)} %multiply_reduce_fusion), channel_id=1, replica_groups=mesh['groups'=2,'wide'=4,'narrow'=4] {'narrow'}, use_global_device_ids=true, to_apply=%region_5.0 | all-reduce | flops 16 | bytes 128 | tf_op jit(solution)/shard_map/psum | solution.py:52
  204.8 0.0 copy-done.1
  204.8 1.7 multiply_add_fusion
  (3 shorter events, 0.0 us)
Async XLA Ops:
  6.5 129.5 %reduce-scatter.3.cloned.1.call-start = ((), (), s32[]{:S(2)}) async-start(), calls=%async_computation.2 | async-start | bytes 4915200 | tf_op jit(solution)/shard_map/reduce_scatter | solution.py:39
  17.8 35.9 %slice-start = ((s8[20971520]{0:T(1024)(128)(4,1)}), s8[4194304]{0:T(1024)(128)(4,1)S(1)}, s32[]{:S(2)}) async-start(s8[20971520]{0:T(1024)(128)(4,1)} %bitcast.13), calls=%async_computation.5 | async-start | bytes 8388608
  33.5 20.3 %slice-start.1 = ((s8[20971520]{0:T(1024)(128)(4,1)}), s8[4194304]{0:T(1024)(128)(4,1)S(1)}, s32[]{:S(2)}) async-start(s8[20971520]{0:T(1024)(128)(4,1)} %bitcast.13), calls=%async_computation.6 | async-start | bytes 8388608
  33.5 20.3 %slice-start.2 = ((s8[20971520]{0:T(1024)(128)(4,1)}), s8[4194304]{0:T(1024)(128)(4,1)S(1)}, s32[]{:S(2)}) async-start(s8[20971520]{0:T(1024)(128)(4,1)} %bitcast.13), calls=%async_computation.7 | async-start | bytes 8388608
  33.5 20.3 %slice-start.3 = ((s8[20971520]{0:T(1024)(128)(4,1)}), s8[4194304]{0:T(1024)(128)(4,1)S(1)}, s32[]{:S(2)}) async-start(s8[20971520]{0:T(1024)(128)(4,1)} %bitcast.13), calls=%async_computation.8 | async-start | bytes 8388608
  33.5 20.3 %slice-start.4 = ((s8[20971520]{0:T(1024)(128)(4,1)}), s8[4194304]{0:T(1024)(128)(4,1)S(1)}, s32[]{:S(2)}) async-start(s8[20971520]{0:T(1024)(128)(4,1)} %bitcast.13), calls=%async_computation.9 | async-start | bytes 8388608
  91.8 64.6 %all-gather.2.cloned.1.call-start = ((), (), s32[]{:S(2)}) async-start(), calls=%async_computation.3 | async-start | bytes 1638400 | tf_op jit(solution)/shard_map/all_gather | solution.py:41
  138.1 59.9 %copy-start = (bf16[16,2048]{1,0:T(8,128)(2,1)S(1)}, bf16[16,2048]{1,0:T(8,128)(2,1)}, u32[]{:S(2)}) copy-start(bf16[16,2048]{1,0:T(8,128)(2,1)} %param.8) | copy-start | bytes 196612
  138.1 59.9 %copy-start.2 = (f32[2048]{0:T(1024)S(1)}, f32[2048]{0:T(1024)}, u32[]{:S(2)}) copy-start(f32[2048]{0:T(1024)} %param.12) | copy-start | bytes 24580
  138.1 66.7 %copy-start.1 = (bf16[16,2048]{1,0:T(8,128)(2,1)S(1)}, bf16[16,2048]{1,0:T(8,128)(2,1)}, u32[]{:S(2)}) copy-start(bf16[16,2048]{1,0:T(8,128)(2,1)} %param.11) | copy-start | bytes 196612
  138.1 59.9 %reduce-scatter.5.cloned.1.call-start = ((), (), s32[]{:S(2)}) async-start(), calls=%async_computation.4 | async-start | bytes 655360 | tf_op jit(solution)/shard_map/reduce_scatter | solution.py:43
Sparse Core Ops, SparseCore 0:
  91.9 44.0 reduce-scatter.2
  138.2 18.1 all-gather.1
  176.4 21.6 reduce-scatter.4
where the time goes:
time: 213 us
  waiting for transfers between devices  84.2 us (40%)
  matrix products  47.1 us (22%)
  blocking collectives  29.6 us (14%)
  local copies, waits for them, and re-layouts  28.8 us (14%)
  between operations  13.2 us (6%)
  other arithmetic  9.93 us (5%)
    reduce_scatter x1, waiting for transfers between devices, on_device(): lax.psum_scatter(partial_value, 'narrow', scatter_dimension=0, tiled=True)  44.1 us
    reduce_scatter x1, waiting for transfers between devices, on_device(): lax.psum_scatter(lax.dot_general(piece, both_weights, (((1,), (1,)), ((),...  21.8 us
    unnamed x17, local copies, waits for them, and re-layouts  20.3 us
    dot_general x1, matrix products, on_device(): lax.dot_general(piece, both_weights, (((1,), (1,)), ((), ())), preferred_...  19.8 us
    all_gather x1, waiting for transfers between devices, on_device(): back_both = lax.all_gather(back_share, 'narrow', axis=0, tiled=True)  18.2 us
    dot_general x1, matrix products, on_device(): jnp.dot(piece[0], both_weights, preferred_element_type=jnp.float32)  16.7 us
    all_gather x1, blocking collectives, on_device(): piece = lax.all_gather(stacked, 'wide', axis=1, tiled=True)  15.6 us
    dot_general x1, matrix products, on_device(): lax.dot_general(piece[1], down_weight, (((1,), (1,)), ((), ())), preferre...  10.6 us
  transfers between devices with their start and end apart: 3, of which 3 were waited for; matrix products, arithmetic and copies ran while one was open for 0% of the time, Pallas kernels for 0%

commit v1 on v0

v1 whole, which is shorter than its diff:
```python
import jax
import jax.numpy as jnp
from jax import lax
from jax.experimental import pallas as pl
from jax.experimental.pallas import tpu as pltpu
from jax.sharding import PartitionSpec as P

EPS = 1e-05
ASCENT = 0.5
LAST_SHARE = 0.3
STEP = 512
PAIR = 64
SCOPED_BYTES = 44 << 20

NN = (((1,), (0,)), ((), ()))
NT = (((1,), (1,)), ((), ()))
VMEM = pl.BlockSpec(memory_space=pltpu.VMEM)
HBM = pl.BlockSpec(memory_space=pltpu.HBM)
ANY = pl.BlockSpec(memory_space=pl.ANY)
SMEM = pl.BlockSpec(memory_space=pltpu.SMEM)
F32 = jnp.float32
BF16 = jnp.bfloat16


def dot(a, b, dims):
    return lax.dot_general(a, b, dims, preferred_element_type=F32)


def reversed_bits(value, count):
    out = 0 * value
    bit = 1
    while bit < count:
        out = 2 * out + value // bit % 2
        bit *= 2
    return out


def steps(length):
    return [(at, min(STEP, length - at)) for at in range(0, length, STEP)]


def cost(*products):
    flops = sum(2 * m * k * n for m, k, n in products)
    size = sum(2 * k * n for _, k, n in products)
    return pl.CostEstimate(flops=flops, bytes_accessed=size, transcendentals=0)


def split(x):
    high = x.astype(BF16)
    low = (x - high.astype(F32)).astype(BF16)
    return jnp.concatenate([jnp.broadcast_to(y, (x.shape[0], PAIR)) for y in (high, low)], axis=1)


def joined(x):
    return x[:, :1].astype(F32) + x[:, PAIR : PAIR + 1].astype(F32)


def params():
    return pltpu.CompilerParams(vmem_limit_bytes=SCOPED_BYTES)


def assemble(mirror_ref, blocks, rows_ref, narrow):
    size = blocks[0].shape[0]
    share = len(blocks) // narrow
    for p, block in enumerate(blocks):
        place = (reversed_bits(p // share, narrow) ^ mirror_ref[0]) * share + p % share
        rows_ref[pl.ds(pl.multiple_of(place * size, size), size), :] = block[...]


def forward(mirror, blocks, weights, span, dims, narrow, after, name):
    tokens = sum(b.shape[0] for b in blocks)
    width = blocks[0].shape[1]
    begin, hidden = span
    total = hidden * len(weights)
    half = tokens // 2
    parts = [(i, at, size) for at, size in steps(hidden) for i in range(len(weights))]
    held = (width, hidden) if dims is NN else (hidden, width)

    def cut(ref, at, size):
        return ref.at[:, pl.ds(at, size)] if dims is NN else ref.at[pl.ds(at, size), :]

    def kernel(*refs):
        mirror_ref, refs = refs[0], refs[1:]
        block_refs, refs = refs[: len(blocks)], refs[len(blocks) :]
        weight_refs, refs = refs[: len(weights)], refs[len(weights) + len(after) :]
        keep_ref, send_ref, rows_ref, sems, *held_refs = refs
        copies = [
            pltpu.make_async_copy(cut(weight_refs[i], begin + at, size), cut(held_refs[i], at, size), sems.at[j])
            for j, (i, at, size) in enumerate(parts)
        ]
        for copy in copies:
            copy.start()
        assemble(mirror_ref, block_refs, rows_ref, narrow)
        for copy, (i, at, size) in zip(copies, parts):
            copy.wait()
            part = dot(rows_ref[...], cut(held_refs[i], at, size)[...], dims)
            here = pl.ds(i * hidden + at, size)
            keep_ref[:, here] = part[:half]
            send_ref[:, here] = part[half:].astype(BF16)

    return pl.pallas_call(
        kernel,
        in_specs=[SMEM] + [VMEM] * len(blocks) + [HBM] * len(weights) + [ANY] * len(after),
        out_specs=[VMEM] * 2,
        out_shape=[jax.ShapeDtypeStruct((half, total), F32), jax.ShapeDtypeStruct((half, total), BF16)],
        scratch_shapes=[pltpu.VMEM((tokens, width), BF16), pltpu.SemaphoreType.DMA((len(parts),))]
        + [pltpu.VMEM(held, BF16)] * len(weights),
        compiler_params=params(),
        cost_estimate=cost((tokens, width, total)),
        name=name,
    )(mirror, *blocks, *weights, *after)


def backward(index, blocks, weights, span, before, pieces, name):
    n = len(blocks)
    begin, hidden = span
    share = blocks[0].shape[0]
    tokens = share * n
    width = weights[0].shape[0]
    size = tokens // pieces
    parts = [(i, at, count) for at, count in steps(width) for i in range(len(weights))]
    extra = [] if before is None else [before]

    def kernel(*refs):
        index_ref, refs = refs[0], refs[1:]
        block_refs, refs = refs[:n], refs[n:]
        weight_refs, refs = refs[: len(weights)], refs[len(weights) :]
        before_refs, refs = refs[: len(extra)], refs[len(extra) :]
        out_refs, refs = refs[:pieces], refs[pieces:]
        rows_ref, sems, *held_refs = refs
        copies = [
            pltpu.make_async_copy(
                weight_refs[i].at[pl.ds(at, count), pl.ds(begin, hidden)],
                held_refs[i].at[pl.ds(at, count), :],
                sems.at[j],
            )
            for j, (i, at, count) in enumerate(parts)
        ]
        for copy in copies:
            copy.start()
        for j, block in enumerate(block_refs):
            place = (reversed_bits(j, n) ^ index_ref[0]) * share
            rows_ref[pl.ds(pl.multiple_of(place, share), share), :] = block[...]
        inner = joined(rows_ref[:, pl.ds(2 * hidden, 2 * PAIR)])
        for b in before_refs:
            inner += b[:, pl.ds(width, 1)]
        for i, out in enumerate(out_refs):
            mine = inner[i * size : (i + 1) * size]
            out[:, pl.ds(width, 2 * PAIR)] = split(mine) if i else jnp.broadcast_to(mine, (size, 2 * PAIR))
        for copy, (i, at, count) in zip(copies, parts):
            copy.wait()
            here = pl.ds(at, count)
            product = dot(rows_ref[:, pl.ds(i * hidden, hidden)], held_refs[i][here, :], NT)
            part = part + product if i else product
            if i + 1 == len(weights):
                for b in before_refs:
                    part += b[:, here]
                for j, out in enumerate(out_refs):
                    out[:, here] = part[j * size : (j + 1) * size].astype(out.dtype)

    return pl.pallas_call(
        kernel,
        in_specs=[SMEM] + [VMEM] * n + [HBM] * len(weights) + [VMEM] * len(extra),
        out_specs=[VMEM] * pieces,
        out_shape=[jax.ShapeDtypeStruct((size, width + 2 * PAIR), BF16 if i else F32) for i in range(pieces)],
        scratch_shapes=[
            pltpu.VMEM((tokens, 2 * hidden + 2 * PAIR), BF16),
            pltpu.SemaphoreType.DMA((len(parts),)),
        ]
        + [pltpu.VMEM((width, hidden), BF16)] * len(weights),
        compiler_params=params(),
        cost_estimate=cost((tokens, 2 * hidden, width)),
        name=name,
    )(index, *blocks, *weights, *extra)


def solution(mesh):
    wide, narrow = mesh.shape["wide"], mesh.shape["narrow"]
    share = wide // narrow
    bits = [1 << i for i in range(narrow.bit_length() - 1)]

    def swap(x, axis, k):
        return lax.ppermute(x, axis, [(i, i ^ k) for i in range(mesh.shape[axis])])

    def over_narrow(x):
        return x + sum(swap(x, "narrow", k) for k in range(1, narrow))

    def scatter(keep, send):
        first = None
        for i, bit in enumerate(bits):
            got = swap(send, "narrow", bit)
            first = got if first is None else first
            half = keep.shape[0] // 2
            if i + 1 < len(bits):
                send = (keep[half:] + got[half:].astype(F32)).astype(BF16)
                keep, got = keep[:half], got[:half]
            keep = keep + got.astype(F32)
        return keep, first

    def gather(block):
        blocks = [block]
        for bit in reversed(bits):
            blocks = blocks + [swap(b, "narrow", bit) for b in blocks]
        return blocks

    def gate_terms(sums, back_hidden):
        hidden = sums.shape[1] // 2
        gate, up = sums[:, :hidden], sums[:, hidden:]
        sig = jax.nn.sigmoid(gate)
        back_gate = (back_hidden * up * sig * (1.0 + gate * (1.0 - sig))).astype(BF16)
        back_up = (back_hidden * gate * sig).astype(BF16)
        inner = jnp.sum(back_gate.astype(F32) * gate + back_up.astype(F32) * up, axis=1, keepdims=True)
        return jnp.concatenate([back_gate, back_up, split(inner)], axis=1)

    def on_device(tokens, signs, magnitude, target, norm_gain, gate_weight, up_weight, down_weight):
        width, hidden = gate_weight.shape
        features = width * narrow
        last = max(128, int(hidden * LAST_SHARE) // STEP * STEP)
        span_a, span_b = (0, hidden - last), (hidden - last, last)
        index = lax.axis_index("narrow").astype(jnp.int32).reshape(1)
        mirror = reversed_bits(index, narrow)
        pair = [gate_weight, up_weight]

        targets = [target] + [swap(target, "wide", k) for k in range(1, wide)]
        delta = (2 * signs - 1).astype(F32) * magnitude
        latent = tokens.astype(F32) + delta
        squares = over_narrow(jnp.sum(latent * latent, axis=1, keepdims=True))
        scale = lax.rsqrt(squares / features + EPS)
        unit = latent * scale
        normed = (unit * norm_gain).astype(BF16)
        normeds = [normed] + [swap(normed, "wide", k) for k in range(1, wide)]

        keep, send = forward(mirror, targets, [down_weight], (0, hidden), NT, narrow, [], "back_hidden")
        back_hidden, first = scatter(keep, send)
        keep, send = forward(mirror, normeds, pair, span_a, NN, narrow, [first], "gate_up_a")
        sums_a, first = scatter(keep, send)
        keep, send = forward(mirror, normeds, pair, span_b, NN, narrow, [first], "gate_up_b")
        sums_b, _ = scatter(keep, send)
        blocks_a = gather(gate_terms(sums_a, back_hidden[:, : span_a[1]]))
        blocks_b = gather(gate_terms(sums_b, back_hidden[:, span_b[0] :]))
        (before,) = backward(index, blocks_a, pair, span_a, None, 1, "back_a")
        pieces = backward(index, blocks_b, pair, span_b, before, wide, "back_b")
        back_normed, inner = pieces[0][:, :width], pieces[0][:, width : width + 1]
        for k in range(1, wide):
            got = swap(pieces[k], "wide", k)
            back_normed = back_normed + got[:, :width].astype(F32)
            inner = inner + joined(got[:, width:])
        scaled = back_normed * norm_gain
        back_latent = scale * (scaled - unit * (inner / features))
        return delta + ASCENT * (target.astype(F32) + back_latent)

    rows = P(("groups", "wide"), "narrow")
    in_specs = (rows, rows, rows, rows, P("narrow"), P("narrow", "wide"), P("narrow", "wide"), P("wide", "narrow"))
    return jax.shard_map(on_device, mesh=mesh, in_specs=in_specs, out_specs=rows, check_vma=False)
```

time: 213 us -> 105 us (0.49)
  waiting for transfers between devices: 84.2 us -> 30.5 us
  matrix products: 47.1 us -> 0 us
  Pallas kernels: 0 us -> 44.9 us
  blocking collectives: 29.6 us -> 0 us
  local copies, waits for them, and re-layouts: 28.8 us -> 1.43 us
  starting transfers between devices: 0.09 us -> 25.1 us
  between operations: 13.2 us -> 0.18 us
  other arithmetic: 9.93 us -> 3.05 us
    reduce_scatter x2 -> x0, waiting for transfers between devices: 65.9 us -> none  [the longest x1 44.1 us: on_device(): lax.psum_scatter(partial_value, 'narrow', scatter_dimension=0, tiled=True)]
    dot_general x3 -> x0, matrix products: 47.1 us -> none  [the longest x1 19.8 us: on_device(): lax.dot_general(piece, both_weights, (((1,), (1,)), ((), ())), preferred_...]
    pallas_call x0 -> x5, Pallas kernels: none -> 44.9 us  [the longest x3 24.8 us: forward(): pl.pallas_call(kernel, in_specs=[SMEM] + [VMEM] * len(blocks) + [HBM] * l...]
    ppermute x0 -> x24, waiting for transfers between devices: none -> 30.5 us  [swap(): return lax.ppermute(x, axis, [(i, i ^ k) for i in range(mesh.shape[axis])])]
    ppermute x0 -> x24, starting transfers between devices: none -> 25.1 us  [swap(): return lax.ppermute(x, axis, [(i, i ^ k) for i in range(mesh.shape[axis])])]
    unnamed x17 -> x12, local copies, waits for them, and re-layouts: 20.3 us -> 0.86 us
    all_gather x1 -> x0, waiting for transfers between devices: 18.2 us -> none  [on_device(): back_both = lax.all_gather(back_share, 'narrow', axis=0, tiled=True)]
    all_gather x1 -> x0, blocking collectives: 15.6 us -> none  [on_device(): piece = lax.all_gather(stacked, 'wide', axis=1, tiled=True)]
  transfers between devices with their start and end apart: 3 -> 24, of which waited for: 3 -> 11; matrix products, arithmetic and copies ran while one was open for 0% -> 1% of each run, Pallas kernels for 0% -> 23%
where the time goes in v1:
time: 105 us
  Pallas kernels  44.9 us (43%)
  waiting for transfers between devices  30.5 us (29%)
  starting transfers between devices  25.1 us (24%)
  other arithmetic  3.05 us (3%)
  local copies, waits for them, and re-layouts  1.43 us (1%)
    ppermute x24, waiting for transfers between devices, swap(): return lax.ppermute(x, axis, [(i, i ^ k) for i in range(mesh.shape[axis])])  30.5 us
    ppermute x24, starting transfers between devices, swap(): return lax.ppermute(x, axis, [(i, i ^ k) for i in range(mesh.shape[axis])])  25.1 us
    pallas_call x3, Pallas kernels, forward(): pl.pallas_call(kernel, in_specs=[SMEM] + [VMEM] * len(blocks) + [HBM] * l...  24.8 us
    pallas_call x2, Pallas kernels, backward(): pl.pallas_call(kernel, in_specs=[SMEM] + [VMEM] * n + [HBM] * len(weights...  20.1 us
  transfers between devices with their start and end apart: 24, of which 11 were waited for; matrix products, arithmetic and copies ran while one was open for 1% of the time, Pallas kernels for 23%

profile of v1, /device:TPU:0, one launch (start us, length us, event | category | flops | bytes accessed | tf_op | source)
XLA Modules:
  0.0 105.1 jit_solution(12178099847063463441)
XLA Ops:
  0.0 1.2 %multiply_reduce_fusion = f32[16]{0:T(128)S(1)} fusion(bf16[16,2048]{1,0:T(8,128)(2,1)} %param.8, f32[16,2048]{1,0:T(8,128)} %param.10, s32[16,2048]{1,0:T(8,128)} %param.9), kind=kLoop, calls=%fused_computation.12 | loop fusion | flops 262128 | bytes 327744 | tf_op jit(solution)/shard_map/reduce_sum | solution.py:227
  1.2 0.1 copy.16
  1.3 2.4 %collective-permute-start.2 = (f32[16,1]{1,0:T(8,128)S(1)}, f32[16,1]{1,0:T(8,128)S(1)}, u32[]{:S(2)}, u32[]{:S(2)}) collective-permute-start(f32[16,1]{1,0:T(8,128)S(1)} %copy.16), channel_id=1, source_target_pairs={{0,3},{1,2},{2,1},{3,0},{4,7},{5,6},{6,5},{7,4},{8,11},{9,10},{10,... | collective-permute-start | bytes 200 | tf_op jit(solution)/shard_map/ppermute | solution.py:183
  3.7 0.6 collective-permute-start.1
  4.4 2.8 %collective-permute-start.4 = (bf16[16,2048]{1,0:T(8,128)(2,1)}, bf16[16,2048]{1,0:T(8,128)(2,1)S(1)}, u32[]{:S(2)}, u32[]{:S(2)}) collective-permute-start(bf16[16,2048]{1,0:T(8,128)(2,1)} %refs_1_.1), channel_id=1, source_target_pairs={{0,8},{4,12},{8,0},{12,4},{1,9},{5,13},{9,1},{13,5},{2,10},{6,14},... | collective-permute-start | bytes 196616 | tf_op jit(solution)/shard_map/ppermute | solution.py:183
  7.2 1.6 %collective-permute-start.3 = (bf16[16,2048]{1,0:T(8,128)(2,1)}, bf16[16,2048]{1,0:T(8,128)(2,1)S(1)}, u32[]{:S(2)}, u32[]{:S(2)}) collective-permute-start(bf16[16,2048]{1,0:T(8,128)(2,1)} %refs_1_.1), channel_id=1, source_target_pairs={{0,4},{4,0},{8,12},{12,8},{1,5},{5,1},{9,13},{13,9},{2,6},{6,2},{1... | collective-permute-start | bytes 196616 | tf_op jit(solution)/shard_map/ppermute | solution.py:183
  8.8 0.7 collective-permute-start.5
  9.5 0.1 rsqrt_reduce_fusion
  9.6 1.4 %collective-permute-done.4.refs_3_ = bf16[16,2048]{1,0:T(8,128)(2,1)S(1)} collective-permute-done((bf16[16,2048]{1,0:T(8,128)(2,1)}, bf16[16,2048]{1,0:T(8,128)(2,1)S(1)}, u32[]{:S(2)}, u32[]{:S(2)}) %collective-permute-start.4) | collective-permute-done | bytes 65568 | tf_op jit(solution)/shard_map/ppermute | solution.py:183
  11.0 0.7 collective-permute-done.3.refs_2_
  11.7 3.4 %collective-permute-done.5.refs_4_ = bf16[16,2048]{1,0:T(8,128)(2,1)S(1)} collective-permute-done((bf16[16,2048]{1,0:T(8,128)(2,1)}, bf16[16,2048]{1,0:T(8,128)(2,1)S(1)}, u32[]{:S(2)}, u32[]{:S(2)}) %collective-permute-start.5) | collective-permute-done | bytes 65568 | tf_op jit(solution)/shard_map/ppermute | solution.py:183
  15.1 0.8 copy-done
  15.9 9.3 %back_hidden.1 = (f32[32,5120]{1,0:T(8,128)S(1)}, bf16[32,5120]{1,0:T(8,128)(2,1)S(1)}) custom-call(s32[1]{0:T(128)S(6)} %add.116.refs_0_, bf16[16,2048]{1,0:T(8,128)(2,1)S(1)} %copy-done, bf16[16,2048]{1,0:T(8,128)(2,1)S(1)} %collective-permute-done.3.refs_2_, bf16[16,2048]{1,0:T(8,128)(2,1)S(1)} %collective-permute-done.4.refs_3_, ...), custom_call_target="tpu_custom_call" | custom-call | flops 1342177280 | bytes 20971520 | tf_op jit(solution)/shard_map/back_hidden/pallas_call | solution.py:101
  25.3 0.1 multiply_convert_fusion.2.refs_1_
  25.4 1.4 %collective-permute-start.10 = (bf16[16,2048]{1,0:T(8,128)(2,1)S(1)}, bf16[16,2048]{1,0:T(8,128)(2,1)S(1)}, u32[]{:S(2)}, u32[]{:S(2)}) collective-permute-start(bf16[16,2048]{1,0:T(8,128)(2,1)S(1)} %multiply_convert_fusion.2.refs_1_), channel_id=1, source_target_pairs={{0,12},{4,8},{8,4},{12,0},{1,13},{5,9},{9,5},{13,1},{2,14},{6,10},... | collective-permute-start | bytes 196616 | tf_op jit(solution)/shard_map/ppermute | solution.py:183
  26.7 0.4 collective-permute-start.9
  27.2 2.6 %collective-permute-start.8 = (bf16[16,2048]{1,0:T(8,128)(2,1)S(1)}, bf16[16,2048]{1,0:T(8,128)(2,1)S(1)}, u32[]{:S(2)}, u32[]{:S(2)}) collective-permute-start(bf16[16,2048]{1,0:T(8,128)(2,1)S(1)} %multiply_convert_fusion.2.refs_1_), channel_id=1, source_target_pairs={{0,4},{4,0},{8,12},{12,8},{1,5},{5,1},{9,13},{13,9},{2,6},{6,2},{1... | collective-permute-start | bytes 196616 | tf_op jit(solution)/shard_map/ppermute | solution.py:183
  29.9 1.6 %collective-permute-start.7 = (bf16[16,5120]{1,0:T(8,128)(2,1)S(1)}, bf16[16,5120]{1,0:T(8,128)(2,1)S(1)}, u32[]{:S(2)}, u32[]{:S(2)}) collective-permute-start(bf16[16,5120]{1,0:T(8,128)(2,1)S(1)} %add_convert_fusion.1), channel_id=1, source_target_pairs={{0,2},{1,3},{2,0},{3,1},{4,6},{5,7},{6,4},{7,5},{8,10},{9,11},{10,... | collective-permute-start | bytes 491528 | tf_op jit(solution)/shard_map/ppermute | solution.py:183
  31.4 0.8 collective-permute-done.10.refs_4_
  32.2 2.3 %collective-permute-done.9.refs_3_ = bf16[16,2048]{1,0:T(8,128)(2,1)S(1)} collective-permute-done((bf16[16,2048]{1,0:T(8,128)(2,1)S(1)}, bf16[16,2048]{1,0:T(8,128)(2,1)S(1)}, u32[]{:S(2)}, u32[]{:S(2)}) %collective-permute-start.9) | collective-permute-done | bytes 65568 | tf_op jit(solution)/shard_map/ppermute | solution.py:183
  34.5 10.2 %gate_up_a.1 = (f32[32,7168]{1,0:T(8,128)S(1)}, bf16[32,7168]{1,0:T(8,128)(2,1)S(1)}) custom-call(s32[1]{0:T(128)S(6)} %add.116.refs_0_, bf16[16,2048]{1,0:T(8,128)(2,1)S(1)} %multiply_convert_fusion.2.refs_1_, bf16[16,2048]{1,0:T(8,128)(2,1)S(1)} %collective-permute-done.8.refs_2_, bf16[16,2048]{1,0:T(8,128)(2,1)S(1)} %collective-permute-done.9.refs_3_, ...), custom_call_target="tpu_custom_call" | custom-call | flops 1879048192 | bytes 29360128 | tf_op jit(solution)/shard_map/gate_up_a/pallas_call | solution.py:101
  44.8 0.1 collective-permute-start.11
  44.9 1.7 %collective-permute-done.11.refs_7_ = bf16[32,7168]{1,0:T(8,128)(2,1)S(1)} collective-permute-done((bf16[32,7168]{1,0:T(8,128)(2,1)S(1)}, bf16[32,7168]{1,0:T(8,128)(2,1)S(1)}, u32[]{:S(2)}, u32[]{:S(2)}) %collective-permute-start.11) | collective-permute-done | bytes 458784 | tf_op jit(solution)/shard_map/ppermute | solution.py:183
  46.6 5.3 %gate_up_b.1 = (f32[32,3072]{1,0:T(8,128)S(1)}, bf16[32,3072]{1,0:T(8,128)(2,1)S(1)}) custom-call(s32[1]{0:T(128)S(6)} %add.116.refs_0_, bf16[16,2048]{1,0:T(8,128)(2,1)S(1)} %multiply_convert_fusion.2.refs_1_, bf16[16,2048]{1,0:T(8,128)(2,1)S(1)} %collective-permute-done.8.refs_2_, bf16[16,2048]{1,0:T(8,128)(2,1)S(1)} %collective-permute-done.9.refs_3_, ...), custom_call_target="tpu_custom_call" | custom-call | flops 805306368 | bytes 12582912 | tf_op jit(solution)/shard_map/gate_up_b/pallas_call | solution.py:101
  51.9 0.2 collective-permute-start.12
  52.2 1.6 %collective-permute-start.17 = (bf16[16,7168]{1,0:T(8,128)(2,1)S(1)}, bf16[16,7168]{1,0:T(8,128)(2,1)S(1)}, u32[]{:S(2)}, u32[]{:S(2)}) collective-permute-start(bf16[16,7168]{1,0:T(8,128)(2,1)S(1)} %add_convert_fusion), channel_id=1, source_target_pairs={{0,2},{1,3},{2,0},{3,1},{4,6},{5,7},{6,4},{7,5},{8,10},{9,11},{10,... | collective-permute-start | bytes 688136 | tf_op jit(solution)/shard_map/ppermute | solution.py:183
  53.8 1.2 %collective-permute-start.13 = (bf16[16,3072]{1,0:T(8,128)(2,1)S(1)}, bf16[16,3072]{1,0:T(8,128)(2,1)S(1)}, u32[]{:S(2)}, u32[]{:S(2)}) collective-permute-start(bf16[16,3072]{1,0:T(8,128)(2,1)S(1)} %add_convert_fusion.2), channel_id=1, source_target_pairs={{0,2},{1,3},{2,0},{3,1},{4,6},{5,7},{6,4},{7,5},{8,10},{9,11},{10,... | collective-permute-start | bytes 294920 | tf_op jit(solution)/shard_map/ppermute | solution.py:183
  55.0 5.7 %collective-permute-done.17 = bf16[16,7168]{1,0:T(8,128)(2,1)S(1)} collective-permute-done((bf16[16,7168]{1,0:T(8,128)(2,1)S(1)}, bf16[16,7168]{1,0:T(8,128)(2,1)S(1)}, u32[]{:S(2)}, u32[]{:S(2)}) %collective-permute-start.17) | collective-permute-done | bytes 229408 | tf_op jit(solution)/shard_map/ppermute | solution.py:183
  60.7 0.3 add_reduce_fusion
  61.0 0.1 broadcast_in_dim.14
  61.1 0.1 broadcast_in_dim.13
  61.2 0.1 concatenate.7.refs_1_
  61.3 1.6 %collective-permute-start.18 = (bf16[16,7296]{1,0:T(8,128)(2,1)S(1)}, bf16[16,7296]{1,0:T(8,128)(2,1)S(1)}, u32[]{:S(2)}, u32[]{:S(2)}) collective-permute-start(bf16[16,7296]{1,0:T(8,128)(2,1)S(1)} %concatenate.7.refs_1_), channel_id=1, source_target_pairs={{0,2},{1,3},{2,0},{3,1},{4,6},{5,7},{6,4},{7,5},{8,10},{9,11},{10,... | collective-permute-start | bytes 700424 | tf_op jit(solution)/shard_map/ppermute | solution.py:183
  62.9 0.2 add_reduce_fusion.1
  63.1 6.3 %collective-permute-done.18.refs_2_ = bf16[16,7296]{1,0:T(8,128)(2,1)S(1)} collective-permute-done((bf16[16,7296]{1,0:T(8,128)(2,1)S(1)}, bf16[16,7296]{1,0:T(8,128)(2,1)S(1)}, u32[]{:S(2)}, u32[]{:S(2)}) %collective-permute-start.18) | collective-permute-done | bytes 233504 | tf_op jit(solution)/shard_map/ppermute | solution.py:183
  69.4 0.1 broadcast_in_dim.12
  69.6 0.1 concatenate.6.refs_1_
  69.7 1.5 %collective-permute-start.14 = (bf16[16,3200]{1,0:T(8,128)(2,1)S(1)}, bf16[16,3200]{1,0:T(8,128)(2,1)S(1)}, u32[]{:S(2)}, u32[]{:S(2)}) collective-permute-start(bf16[16,3200]{1,0:T(8,128)(2,1)S(1)} %concatenate.6.refs_1_), channel_id=1, source_target_pairs={{0,2},{1,3},{2,0},{3,1},{4,6},{5,7},{6,4},{7,5},{8,10},{9,11},{10,... | collective-permute-start | bytes 307208 | tf_op jit(solution)/shard_map/ppermute | solution.py:183
  71.2 0.2 collective-permute-start.15
  71.4 3.6 %collective-permute-done.14.refs_2_ = bf16[16,3200]{1,0:T(8,128)(2,1)S(1)} collective-permute-done((bf16[16,3200]{1,0:T(8,128)(2,1)S(1)}, bf16[16,3200]{1,0:T(8,128)(2,1)S(1)}, u32[]{:S(2)}, u32[]{:S(2)}) %collective-permute-start.14) | collective-permute-done | bytes 102432 | tf_op jit(solution)/shard_map/ppermute | solution.py:183
  75.0 13.5 %back_a.1.refs_7_ = f32[64,2176]{1,0:T(8,128)S(1)} custom-call(s32[1]{0:T(128)} %bitcast.1.refs_0_, bf16[16,7296]{1,0:T(8,128)(2,1)S(1)} %concatenate.7.refs_1_, bf16[16,7296]{1,0:T(8,128)(2,1)S(1)} %collective-permute-done.18.refs_2_, bf16[16,7296]{1,0:T(8,128)(2,1)S(1)} %collective-permute-done.19.refs_3_, ...), custom_call_target="tpu_custom_call" | custom-call | flops 1879048192 | bytes 29360128 | tf_op jit(solution)/shard_map/back_a/pallas_call | solution.py:161
  88.5 6.6 %back_b.1 = (f32[16,2176]{1,0:T(8,128)S(1)}, bf16[16,2176]{1,0:T(8,128)(2,1)S(1)}, bf16[16,2176]{1,0:T(8,128)(2,1)S(1)}, bf16[16,2176]{1,0:T(8,128)(2,1)S(1)}) custom-call(s32[1]{0:T(128)} %bitcast.1.refs_0_, bf16[16,3200]{1,0:T(8,128)(2,1)S(1)} %concatenate.6.refs_1_, bf16[16,3200]{1,0:T(8,128)(2,1)S(1)} %collective-permute-done.14.refs_2_, ...), custom_call_target="tpu_custom_call" | custom-call | flops 805306368 | bytes 12582912 | tf_op jit(solution)/shard_map/back_b/pallas_call | solution.py:161
  95.2 2.7 %collective-permute-start.22 = (bf16[16,2176]{1,0:T(8,128)(2,1)S(1)}, bf16[16,2176]{1,0:T(8,128)(2,1)S(1)}, u32[]{:S(2)}, u32[]{:S(2)}) collective-permute-start(bf16[16,2176]{1,0:T(8,128)(2,1)S(1)} %get-tuple-element.23), channel_id=1, source_target_pairs={{0,8},{4,12},{8,0},{12,4},{1,9},{5,13},{9,1},{13,5},{2,10},{6,14},... | collective-permute-start | bytes 208904 | tf_op jit(solution)/shard_map/ppermute | solution.py:183
  97.9 1.7 %collective-permute-start.23 = (bf16[16,2176]{1,0:T(8,128)(2,1)S(1)}, bf16[16,2176]{1,0:T(8,128)(2,1)S(1)}, u32[]{:S(2)}, u32[]{:S(2)}) collective-permute-start(bf16[16,2176]{1,0:T(8,128)(2,1)S(1)} %get-tuple-element.24), channel_id=1, source_target_pairs={{0,12},{4,8},{8,4},{12,0},{1,13},{5,9},{9,5},{13,1},{2,14},{6,10},... | collective-permute-start | bytes 208904 | tf_op jit(solution)/shard_map/ppermute | solution.py:183
  99.6 1.3 %collective-permute-done.21 = bf16[16,2176]{1,0:T(8,128)(2,1)S(1)} collective-permute-done((bf16[16,2176]{1,0:T(8,128)(2,1)S(1)}, bf16[16,2176]{1,0:T(8,128)(2,1)S(1)}, u32[]{:S(2)}, u32[]{:S(2)}) %collective-permute-start.21) | collective-permute-done | bytes 69664 | tf_op jit(solution)/shard_map/ppermute | solution.py:183
  100.9 3.3 %collective-permute-done.22 = bf16[16,2176]{1,0:T(8,128)(2,1)S(1)} collective-permute-done((bf16[16,2176]{1,0:T(8,128)(2,1)S(1)}, bf16[16,2176]{1,0:T(8,128)(2,1)S(1)}, u32[]{:S(2)}, u32[]{:S(2)}) %collective-permute-start.22) | collective-permute-done | bytes 69664 | tf_op jit(solution)/shard_map/ppermute | solution.py:183
  104.2 0.2 multiply_reduce_fusion.1
  104.4 0.8 multiply_add_fusion
  (39 shorter events, 0.6 us)
Async XLA Ops:
  0.0 25.2 %copy-start.2 = (f32[16,2048]{1,0:T(8,128)S(1)}, f32[16,2048]{1,0:T(8,128)}, u32[]{:S(2)}) copy-start(f32[16,2048]{1,0:T(8,128)} %param.10) | copy-start | bytes 393220
  0.0 25.3 %copy-start.3 = (s32[16,2048]{1,0:T(8,128)S(1)}, s32[16,2048]{1,0:T(8,128)}, u32[]{:S(2)}) copy-start(s32[16,2048]{1,0:T(8,128)} %param.9) | copy-start | bytes 393220
  0.0 25.3 %copy-start.4 = (bf16[16,2048]{1,0:T(8,128)(2,1)S(1)}, bf16[16,2048]{1,0:T(8,128)(2,1)}, u32[]{:S(2)}) copy-start(bf16[16,2048]{1,0:T(8,128)(2,1)} %param.8) | copy-start | bytes 196612
  0.0 25.3 %copy-start.5 = (f32[2048]{0:T(1024)S(1)}, f32[2048]{0:T(1024)}, u32[]{:S(2)}) copy-start(f32[2048]{0:T(1024)} %param.12) | copy-start | bytes 24580
  1.3 7.5 %collective-permute-start.2 = (f32[16,1]{1,0:T(8,128)S(1)}, f32[16,1]{1,0:T(8,128)S(1)}, u32[]{:S(2)}, u32[]{:S(2)}) collective-permute-start(f32[16,1]{1,0:T(8,128)S(1)} %copy.16), channel_id=1, source_target_pairs={{0,3},{1,2},{2,1},{3,0},{4,7},{5,6},{6,5},{7,4},{8,11},{9,10},{10,... | collective-permute-start | bytes 200 | tf_op jit(solution)/shard_map/ppermute | solution.py:183
  3.7 5.8 %collective-permute-start.1 = (f32[16,1]{1,0:T(8,128)S(1)}, f32[16,1]{1,0:T(8,128)S(1)}, u32[]{:S(2)}, u32[]{:S(2)}) collective-permute-start(f32[16,1]{1,0:T(8,128)S(1)} %copy.16), channel_id=1, source_target_pairs={{0,2},{1,3},{2,0},{3,1},{4,6},{5,7},{6,4},{7,5},{8,10},{9,11},{10,... | collective-permute-start | bytes 200 | tf_op jit(solution)/shard_map/ppermute | solution.py:183
  4.3 5.2 %collective-permute-start = (f32[16,1]{1,0:T(8,128)S(1)}, f32[16,1]{1,0:T(8,128)S(1)}, u32[]{:S(2)}, u32[]{:S(2)}) collective-permute-start(f32[16,1]{1,0:T(8,128)S(1)} %copy.16), channel_id=1, source_target_pairs={{0,1},{1,0},{2,3},{3,2},{4,5},{5,4},{6,7},{7,6},{8,9},{9,8},{10,11... | collective-permute-start | bytes 200 | tf_op jit(solution)/shard_map/ppermute | solution.py:183
  4.4 6.6 %collective-permute-start.4 = (bf16[16,2048]{1,0:T(8,128)(2,1)}, bf16[16,2048]{1,0:T(8,128)(2,1)S(1)}, u32[]{:S(2)}, u32[]{:S(2)}) collective-permute-start(bf16[16,2048]{1,0:T(8,128)(2,1)} %refs_1_.1), channel_id=1, source_target_pairs={{0,8},{4,12},{8,0},{12,4},{1,9},{5,13},{9,1},{13,5},{2,10},{6,14},... | collective-permute-start | bytes 196616 | tf_op jit(solution)/shard_map/ppermute | solution.py:183
  7.2 4.5 %collective-permute-start.3 = (bf16[16,2048]{1,0:T(8,128)(2,1)}, bf16[16,2048]{1,0:T(8,128)(2,1)S(1)}, u32[]{:S(2)}, u32[]{:S(2)}) collective-permute-start(bf16[16,2048]{1,0:T(8,128)(2,1)} %refs_1_.1), channel_id=1, source_target_pairs={{0,4},{4,0},{8,12},{12,8},{1,5},{5,1},{9,13},{13,9},{2,6},{6,2},{1... | collective-permute-start | bytes 196616 | tf_op jit(solution)/shard_map/ppermute | solution.py:183
  8.8 6.3 %collective-permute-start.5 = (bf16[16,2048]{1,0:T(8,128)(2,1)}, bf16[16,2048]{1,0:T(8,128)(2,1)S(1)}, u32[]{:S(2)}, u32[]{:S(2)}) collective-permute-start(bf16[16,2048]{1,0:T(8,128)(2,1)} %refs_1_.1), channel_id=1, source_target_pairs={{0,12},{4,8},{8,4},{12,0},{1,13},{5,9},{9,5},{13,1},{2,14},{6,10},... | collective-permute-start | bytes 196616 | tf_op jit(solution)/shard_map/ppermute | solution.py:183
  15.1 0.8 copy-start
  25.2 4.7 %collective-permute-start.6 = (bf16[32,5120]{1,0:T(8,128)(2,1)S(1)}, bf16[32,5120]{1,0:T(8,128)(2,1)S(1)}, u32[]{:S(2)}, u32[]{:S(2)}) collective-permute-start(bf16[32,5120]{1,0:T(8,128)(2,1)S(1)} %get-tuple-element.16), channel_id=1, source_target_pairs={{0,1},{1,0},{2,3},{3,2},{4,5},{5,4},{6,7},{7,6},{8,9},{9,8},{10,11... | collective-permute-start | bytes 983048 | tf_op jit(solution)/shard_map/ppermute | solution.py:183
  25.4 6.9 %collective-permute-start.10 = (bf16[16,2048]{1,0:T(8,128)(2,1)S(1)}, bf16[16,2048]{1,0:T(8,128)(2,1)S(1)}, u32[]{:S(2)}, u32[]{:S(2)}) collective-permute-start(bf16[16,2048]{1,0:T(8,128)(2,1)S(1)} %multiply_convert_fusion.2.refs_1_), channel_id=1, source_target_pairs={{0,12},{4,8},{8,4},{12,0},{1,13},{5,9},{9,5},{13,1},{2,14},{6,10},... | collective-permute-start | bytes 196616 | tf_op jit(solution)/shard_map/ppermute | solution.py:183
  26.7 7.8 %collective-permute-start.9 = (bf16[16,2048]{1,0:T(8,128)(2,1)S(1)}, bf16[16,2048]{1,0:T(8,128)(2,1)S(1)}, u32[]{:S(2)}, u32[]{:S(2)}) collective-permute-start(bf16[16,2048]{1,0:T(8,128)(2,1)S(1)} %multiply_convert_fusion.2.refs_1_), channel_id=1, source_target_pairs={{0,8},{4,12},{8,0},{12,4},{1,9},{5,13},{9,1},{13,5},{2,10},{6,14},... | collective-permute-start | bytes 196616 | tf_op jit(solution)/shard_map/ppermute | solution.py:183
  27.2 7.3 %collective-permute-start.8 = (bf16[16,2048]{1,0:T(8,128)(2,1)S(1)}, bf16[16,2048]{1,0:T(8,128)(2,1)S(1)}, u32[]{:S(2)}, u32[]{:S(2)}) collective-permute-start(bf16[16,2048]{1,0:T(8,128)(2,1)S(1)} %multiply_convert_fusion.2.refs_1_), channel_id=1, source_target_pairs={{0,4},{4,0},{8,12},{12,8},{1,5},{5,1},{9,13},{13,9},{2,6},{6,2},{1... | collective-permute-start | bytes 196616 | tf_op jit(solution)/shard_map/ppermute | solution.py:183
  29.9 15.0 %collective-permute-start.7 = (bf16[16,5120]{1,0:T(8,128)(2,1)S(1)}, bf16[16,5120]{1,0:T(8,128)(2,1)S(1)}, u32[]{:S(2)}, u32[]{:S(2)}) collective-permute-start(bf16[16,5120]{1,0:T(8,128)(2,1)S(1)} %add_convert_fusion.1), channel_id=1, source_target_pairs={{0,2},{1,3},{2,0},{3,1},{4,6},{5,7},{6,4},{7,5},{8,10},{9,11},{10,... | collective-permute-start | bytes 491528 | tf_op jit(solution)/shard_map/ppermute | solution.py:183
  44.8 1.9 %collective-permute-start.11 = (bf16[32,7168]{1,0:T(8,128)(2,1)S(1)}, bf16[32,7168]{1,0:T(8,128)(2,1)S(1)}, u32[]{:S(2)}, u32[]{:S(2)}) collective-permute-start(bf16[32,7168]{1,0:T(8,128)(2,1)S(1)} %get-tuple-element.17), channel_id=1, source_target_pairs={{0,1},{1,0},{2,3},{3,2},{4,5},{5,4},{6,7},{7,6},{8,9},{9,8},{10,11... | collective-permute-start | bytes 1376264 | tf_op jit(solution)/shard_map/ppermute | solution.py:183
  51.9 1.8 %collective-permute-start.12 = (bf16[32,3072]{1,0:T(8,128)(2,1)S(1)}, bf16[32,3072]{1,0:T(8,128)(2,1)S(1)}, u32[]{:S(2)}, u32[]{:S(2)}) collective-permute-start(bf16[32,3072]{1,0:T(8,128)(2,1)S(1)} %get-tuple-element.19), channel_id=1, source_target_pairs={{0,1},{1,0},{2,3},{3,2},{4,5},{5,4},{6,7},{7,6},{8,9},{9,8},{10,11... | collective-permute-start | bytes 589832 | tf_op jit(solution)/shard_map/ppermute | solution.py:183
  52.2 8.5 %collective-permute-start.17 = (bf16[16,7168]{1,0:T(8,128)(2,1)S(1)}, bf16[16,7168]{1,0:T(8,128)(2,1)S(1)}, u32[]{:S(2)}, u32[]{:S(2)}) collective-permute-start(bf16[16,7168]{1,0:T(8,128)(2,1)S(1)} %add_convert_fusion), channel_id=1, source_target_pairs={{0,2},{1,3},{2,0},{3,1},{4,6},{5,7},{6,4},{7,5},{8,10},{9,11},{10,... | collective-permute-start | bytes 688136 | tf_op jit(solution)/shard_map/ppermute | solution.py:183
  53.8 9.1 %collective-permute-start.13 = (bf16[16,3072]{1,0:T(8,128)(2,1)S(1)}, bf16[16,3072]{1,0:T(8,128)(2,1)S(1)}, u32[]{:S(2)}, u32[]{:S(2)}) collective-permute-start(bf16[16,3072]{1,0:T(8,128)(2,1)S(1)} %add_convert_fusion.2), channel_id=1, source_target_pairs={{0,2},{1,3},{2,0},{3,1},{4,6},{5,7},{6,4},{7,5},{8,10},{9,11},{10,... | collective-permute-start | bytes 294920 | tf_op jit(solution)/shard_map/ppermute | solution.py:183
  61.3 13.7 %collective-permute-start.19 = (bf16[16,7296]{1,0:T(8,128)(2,1)S(1)}, bf16[16,7296]{1,0:T(8,128)(2,1)S(1)}, u32[]{:S(2)}, u32[]{:S(2)}) collective-permute-start(bf16[16,7296]{1,0:T(8,128)(2,1)S(1)} %concatenate.7.refs_1_), channel_id=1, source_target_pairs={{0,1},{1,0},{2,3},{3,2},{4,5},{5,4},{6,7},{7,6},{8,9},{9,8},{10,11... | collective-permute-start | bytes 700424 | tf_op jit(solution)/shard_map/ppermute | solution.py:183
  61.3 8.1 %collective-permute-start.18 = (bf16[16,7296]{1,0:T(8,128)(2,1)S(1)}, bf16[16,7296]{1,0:T(8,128)(2,1)S(1)}, u32[]{:S(2)}, u32[]{:S(2)}) collective-permute-start(bf16[16,7296]{1,0:T(8,128)(2,1)S(1)} %concatenate.7.refs_1_), channel_id=1, source_target_pairs={{0,2},{1,3},{2,0},{3,1},{4,6},{5,7},{6,4},{7,5},{8,10},{9,11},{10,... | collective-permute-start | bytes 700424 | tf_op jit(solution)/shard_map/ppermute | solution.py:183
  69.4 5.6 %collective-permute-start.20 = (bf16[16,7296]{1,0:T(8,128)(2,1)S(1)}, bf16[16,7296]{1,0:T(8,128)(2,1)S(1)}, u32[]{:S(2)}, u32[]{:S(2)}) collective-permute-start(bf16[16,7296]{1,0:T(8,128)(2,1)S(1)} %collective-permute-done.18.refs_2_), channel_id=1, source_target_pairs={{0,1},{1,0},{2,3},{3,2},{4,5},{5,4},{6,7},{7,6},{8,9},{9,8},{10,11... | collective-permute-start | bytes 700424 | tf_op jit(solution)/shard_map/ppermute | solution.py:183
  69.7 5.3 %collective-permute-start.14 = (bf16[16,3200]{1,0:T(8,128)(2,1)S(1)}, bf16[16,3200]{1,0:T(8,128)(2,1)S(1)}, u32[]{:S(2)}, u32[]{:S(2)}) collective-permute-start(bf16[16,3200]{1,0:T(8,128)(2,1)S(1)} %concatenate.6.refs_1_), channel_id=1, source_target_pairs={{0,2},{1,3},{2,0},{3,1},{4,6},{5,7},{6,4},{7,5},{8,10},{9,11},{10,... | collective-permute-start | bytes 307208 | tf_op jit(solution)/shard_map/ppermute | solution.py:183
  71.2 17.4 %collective-permute-start.15 = (bf16[16,3200]{1,0:T(8,128)(2,1)S(1)}, bf16[16,3200]{1,0:T(8,128)(2,1)S(1)}, u32[]{:S(2)}, u32[]{:S(2)}) collective-permute-start(bf16[16,3200]{1,0:T(8,128)(2,1)S(1)} %concatenate.6.refs_1_), channel_id=1, source_target_pairs={{0,1},{1,0},{2,3},{3,2},{4,5},{5,4},{6,7},{7,6},{8,9},{9,8},{10,11... | collective-permute-start | bytes 307208 | tf_op jit(solution)/shard_map/ppermute | solution.py:183
  75.0 13.6 %collective-permute-start.16 = (bf16[16,3200]{1,0:T(8,128)(2,1)S(1)}, bf16[16,3200]{1,0:T(8,128)(2,1)S(1)}, u32[]{:S(2)}, u32[]{:S(2)}) collective-permute-start(bf16[16,3200]{1,0:T(8,128)(2,1)S(1)} %collective-permute-done.14.refs_2_), channel_id=1, source_target_pairs={{0,1},{1,0},{2,3},{3,2},{4,5},{5,4},{6,7},{7,6},{8,9},{9,8},{10,11... | collective-permute-start | bytes 307208 | tf_op jit(solution)/shard_map/ppermute | solution.py:183
  88.5 15.9 %copy-start.1 = (bf16[16,2048]{1,0:T(8,128)(2,1)S(1)}, bf16[16,2048]{1,0:T(8,128)(2,1)}, u32[]{:S(2)}) copy-start(bf16[16,2048]{1,0:T(8,128)(2,1)} %refs_1_.1) | copy-start | bytes 196612
  95.1 5.8 %collective-permute-start.21 = (bf16[16,2176]{1,0:T(8,128)(2,1)S(1)}, bf16[16,2176]{1,0:T(8,128)(2,1)S(1)}, u32[]{:S(2)}, u32[]{:S(2)}) collective-permute-start(bf16[16,2176]{1,0:T(8,128)(2,1)S(1)} %get-tuple-element.22), channel_id=1, source_target_pairs={{0,4},{4,0},{8,12},{12,8},{1,5},{5,1},{9,13},{13,9},{2,6},{6,2},{1... | collective-permute-start | bytes 208904 | tf_op jit(solution)/shard_map/ppermute | solution.py:183
  95.2 9.0 %collective-permute-start.22 = (bf16[16,2176]{1,0:T(8,128)(2,1)S(1)}, bf16[16,2176]{1,0:T(8,128)(2,1)S(1)}, u32[]{:S(2)}, u32[]{:S(2)}) collective-permute-start(bf16[16,2176]{1,0:T(8,128)(2,1)S(1)} %get-tuple-element.23), channel_id=1, source_target_pairs={{0,8},{4,12},{8,0},{12,4},{1,9},{5,13},{9,1},{13,5},{2,10},{6,14},... | collective-permute-start | bytes 208904 | tf_op jit(solution)/shard_map/ppermute | solution.py:183
  97.9 6.3 %collective-permute-start.23 = (bf16[16,2176]{1,0:T(8,128)(2,1)S(1)}, bf16[16,2176]{1,0:T(8,128)(2,1)S(1)}, u32[]{:S(2)}, u32[]{:S(2)}) collective-permute-start(bf16[16,2176]{1,0:T(8,128)(2,1)S(1)} %get-tuple-element.24), channel_id=1, source_target_pairs={{0,12},{4,8},{8,4},{12,0},{1,13},{5,9},{9,5},{13,1},{2,14},{6,10},... | collective-permute-start | bytes 208904 | tf_op jit(solution)/shard_map/ppermute | solution.py:183

commit v2 on v0

v2 whole, which is shorter than its diff:
```python
import jax
import jax.numpy as jnp
from jax import lax
from jax.experimental import pallas as pl
from jax.experimental.pallas import tpu as pltpu
from jax.sharding import PartitionSpec as P

EPS = 1e-05
ASCENT = 0.5
LANES = 128
STEP = 512

NN = (((1,), (0,)), ((), ()))
NT = (((1,), (1,)), ((), ()))
ANY = pl.BlockSpec(memory_space=pl.ANY)
HBM = pl.BlockSpec(memory_space=pltpu.HBM)
SMEM = pl.BlockSpec(memory_space=pltpu.SMEM)
VMEM = pl.BlockSpec(memory_space=pltpu.VMEM)
F32 = jnp.float32
BF16 = jnp.bfloat16


def dot(a, b, dims):
    return lax.dot_general(a, b, dims, preferred_element_type=F32)


def steps(length):
    count = next(c for c in range(max(1, length // STEP), length + 1) if length % (c * LANES) == 0)
    return [(i * (length // count), length // count) for i in range(count)]


def params():
    return pltpu.CompilerParams(vmem_limit_bytes=32 << 20)


def in_hbm(weights):
    return [pltpu.with_memory_space_constraint(w, pltpu.HBM) for w in weights]


def cost(m, k, n):
    return pl.CostEstimate(flops=2 * m * k * n, bytes_accessed=2 * k * n, transcendentals=0)


def split(x):
    high = x.astype(BF16)
    low = (x - high.astype(F32)).astype(BF16)
    return jnp.concatenate([jnp.broadcast_to(y, (x.shape[0], LANES // 2)) for y in (high, low)], axis=1)


def joined(x):
    return x[:, :1].astype(F32) + x[:, LANES // 2 : LANES // 2 + 1].astype(F32)


def forward(index, blocks, weights, picks, share, dims, after, name):
    size, width = blocks[0].shape
    tokens = size * len(blocks)
    parts = [(r, i, at, n) for r in range(len(picks)) for at, n in steps(share) for i in range(len(weights))]

    def kernel(index_ref, *refs):
        block_refs, refs = refs[: len(blocks)], refs[len(blocks) :]
        weight_refs, refs = refs[: len(weights)], refs[len(weights) + len(after) :]
        out_ref, rows_ref, held_ref, sems = refs
        copies = []
        for j, (r, i, at, n) in enumerate(parts):
            begin = pl.multiple_of((index_ref[0] ^ picks[r]) * share + at, LANES)
            if dims is NN:
                source, target = weight_refs[i].at[:, pl.ds(begin, n)], held_ref.at[j]
            else:
                source, target = weight_refs[i].at[pl.ds(begin, n), :], held_ref.at[j]
            copies.append(pltpu.make_async_copy(source, target, sems.at[j]))
        for copy in copies:
            copy.start()
        for p, block in enumerate(block_refs):
            rows_ref[p * size : (p + 1) * size, :] = block[...]
        for j, (r, i, at, n) in enumerate(parts):
            copies[j].wait()
            here = pl.ds((r * len(weights) + i) * share + at, n)
            out_ref[:, here] = dot(rows_ref[...], held_ref[j], dims)

    n = parts[0][3]
    total = share * len(picks) * len(weights)
    return pl.pallas_call(
        kernel,
        in_specs=[SMEM] + [VMEM] * len(blocks) + [HBM] * len(weights) + [ANY] * len(after),
        out_specs=VMEM,
        out_shape=jax.ShapeDtypeStruct((tokens, total), F32),
        scratch_shapes=[
            pltpu.VMEM((tokens, width), BF16),
            pltpu.VMEM((len(parts), width, n) if dims is NN else (len(parts), n, width), BF16),
            pltpu.SemaphoreType.DMA((len(parts),)),
        ],
        compiler_params=params(),
        cost_estimate=cost(tokens, width, total),
        name=name,
    )(index, *blocks, *in_hbm(weights), *after)


def backward(index, rows, weights, picks, share, before, pieces, name):
    tokens = rows[0].shape[0]
    width = weights[0].shape[0]
    size = tokens // pieces
    parts = [(r, i, at, n) for at, n in steps(width) for r in range(len(picks)) for i in range(len(weights))]
    extra = [] if before is None else [before]

    def kernel(index_ref, *refs):
        row_refs, refs = refs[: len(picks)], refs[len(picks) :]
        weight_refs, refs = refs[: len(weights)], refs[len(weights) :]
        before_refs, refs = refs[: len(extra)], refs[len(extra) :]
        out_refs, (held_ref, sems) = refs[:pieces], refs[pieces:]
        copies = []
        for j, (r, i, at, n) in enumerate(parts):
            begin = pl.multiple_of((index_ref[0] ^ picks[r]) * share, LANES)
            source = weight_refs[i].at[pl.ds(at, n), pl.ds(begin, share)]
            copies.append(pltpu.make_async_copy(source, held_ref.at[j], sems.at[j]))
        for copy in copies:
            copy.start()
        inner = sum(joined(r[:, pl.ds(2 * share, LANES)]) for r in row_refs)
        for b in before_refs:
            inner += b[:, pl.ds(width, 1)]
        for p, out in enumerate(out_refs):
            mine = inner[p * size : (p + 1) * size]
            out[:, pl.ds(width, LANES)] = split(mine) if p else jnp.broadcast_to(mine, (size, LANES))
        for j, (r, i, at, n) in enumerate(parts):
            copies[j].wait()
            here = pl.ds(at, n)
            product = dot(row_refs[r][:, pl.ds(i * share, share)], held_ref[j], NT)
            part = part + product if r or i else product
            if (r + 1, i + 1) == (len(picks), len(weights)):
                for b in before_refs:
                    part += b[:, here]
                for p, out in enumerate(out_refs):
                    out[:, here] = part[p * size : (p + 1) * size].astype(out.dtype)

    return pl.pallas_call(
        kernel,
        in_specs=[SMEM] + [VMEM] * len(rows) + [HBM] * len(weights) + [VMEM] * len(extra),
        out_specs=[VMEM] * pieces,
        out_shape=[jax.ShapeDtypeStruct((size, width + LANES), BF16 if p else F32) for p in range(pieces)],
        scratch_shapes=[
            pltpu.VMEM((len(parts), parts[0][3], share), BF16),
            pltpu.SemaphoreType.DMA((len(parts),)),
        ],
        compiler_params=params(),
        cost_estimate=cost(tokens, 2 * share * len(picks), width),
        name=name,
    )(index, *rows, *in_hbm(weights), *extra)


def gate_terms(gate, up, back_hidden):
    sig = jax.nn.sigmoid(gate)
    back_gate = (back_hidden * up * sig * (1.0 + gate * (1.0 - sig))).astype(BF16)
    back_up = (back_hidden * gate * sig).astype(BF16)
    return back_gate, back_up


def by_collectives(normed, target, gate_weight, up_weight, down_weight):
    stacked = jnp.stack([normed, target], axis=0)
    rows = lax.all_gather(stacked, "wide", axis=1, tiled=True)
    hidden = gate_weight.shape[1]
    sums = jnp.concatenate(
        [dot(rows[0], gate_weight, NN), dot(rows[0], up_weight, NN), dot(rows[1], down_weight, NT)], axis=1
    )
    sums = lax.psum_scatter(sums, "narrow", scatter_dimension=0, tiled=True)
    both = jnp.concatenate(
        gate_terms(sums[:, :hidden], sums[:, hidden : 2 * hidden], sums[:, 2 * hidden :]), axis=1
    )
    both = lax.all_gather(both, "narrow", axis=0, tiled=True)
    back = dot(both[:, :hidden], gate_weight, NT) + dot(both[:, hidden:], up_weight, NT)
    return lax.psum_scatter(back, "wide", scatter_dimension=0, tiled=True)


def solution(mesh):
    wide, narrow = mesh.shape["wide"], mesh.shape["narrow"]
    near, far = 1, 2

    def swap(x, axis, k):
        return lax.ppermute(x, axis, [(i, i ^ k) for i in range(mesh.shape[axis])])

    def by_swaps(normed, target, gate_weight, up_weight, down_weight):
        width, hidden = gate_weight.shape
        share = hidden // narrow
        index = lax.axis_index("narrow").astype(jnp.int32).reshape(1)
        pair = [gate_weight, up_weight]
        targets = [target] + [swap(target, "wide", k) for k in range(1, wide)]
        normeds = [normed] + [swap(normed, "wide", k) for k in range(1, wide)]

        def hidden_part(picks, after, name):
            return forward(index, targets, [down_weight], picks, share, NT, after, name)

        def pair_part(picks, after, name):
            return forward(index, normeds, pair, picks, share, NN, after, name)

        send = hidden_part([near, near | far], [], "back_hidden_send")
        send, *normeds = lax.optimization_barrier((send, *normeds))
        got = swap(send, "narrow", near)
        keep = hidden_part([0, far], normeds[1:], "back_hidden_keep")
        sum_far = (keep[:, share:] + got[:, share:]).astype(BF16)
        got_far = swap(sum_far, "narrow", far)
        back_hidden = keep[:, :share] + got[:, :share]

        part = pair_part([near | far], [sum_far], "gate_up_near_far")
        part, got_far = lax.optimization_barrier((part, got_far))
        back_hidden = back_hidden + got_far.astype(F32)
        got = swap(part, "narrow", near)
        part = pair_part([far], [part], "gate_up_far")
        sum_far = (part + got).astype(BF16)
        got_far = swap(sum_far, "narrow", far)
        part = pair_part([near, 0], [sum_far], "gate_up_near_own")
        part, got_far = lax.optimization_barrier((part, got_far))
        sums = part[:, 2 * share :] + swap(part[:, : 2 * share], "narrow", near) + got_far.astype(F32)
        gate, up = sums[:, :share], sums[:, share:]
        back_gate, back_up = gate_terms(gate, up, back_hidden)
        inner = jnp.sum(back_gate.astype(F32) * gate + back_up.astype(F32) * up, axis=1, keepdims=True)
        rows = jnp.concatenate([back_gate, back_up, split(inner)], axis=1)

        rows_far = swap(rows, "narrow", far)
        rows_near = swap(rows, "narrow", near)
        (total,) = backward(index, [rows, rows_near], pair, [0, near], share, None, 1, "back_own_near")
        total, rows_far = lax.optimization_barrier((total, rows_far))
        rows_both = swap(rows_far, "narrow", near)
        pieces = backward(
            index, [rows_far, rows_both], pair, [far, near | far], share, total, wide, "back_far_near_far"
        )
        back_normed, inner = pieces[0][:, :width], pieces[0][:, width : width + 1]
        for k in range(1, wide):
            got = swap(pieces[k], "wide", k)
            back_normed = back_normed + got[:, :width].astype(F32)
            inner = inner + joined(got[:, width:])
        return back_normed, inner

    def on_device(tokens, signs, magnitude, target, norm_gain, gate_weight, up_weight, down_weight):
        width, hidden = gate_weight.shape
        features = width * narrow
        weights = (gate_weight, up_weight, down_weight)
        square = narrow == (near | far) + 1 and hidden % (narrow * LANES) == 0 and wide & (wide - 1) == 0

        delta = (2 * signs - 1).astype(F32) * magnitude
        latent = tokens.astype(F32) + delta
        squares = jnp.sum(latent * latent, axis=1, keepdims=True)
        if square:
            squares = squares + sum(swap(squares, "narrow", k) for k in range(1, narrow))
        else:
            squares = lax.psum(squares, "narrow")
        scale = lax.rsqrt(squares / features + EPS)
        unit = latent * scale
        normed = (unit * norm_gain).astype(BF16)
        if square:
            back_normed, inner = by_swaps(normed, target, *weights)
            scaled = back_normed * norm_gain
        else:
            scaled = by_collectives(normed, target, *weights) * norm_gain
            inner = lax.psum(jnp.sum(scaled * unit, axis=1, keepdims=True), "narrow")
        back_latent = scale * (scaled - unit * (inner / features))
        return delta + ASCENT * (target.astype(F32) + back_latent)

    rows = P(("groups", "wide"), "narrow")
    in_specs = (rows, rows, rows, rows, P("narrow"), P("narrow", "wide"), P("narrow", "wide"), P("wide", "narrow"))
    return jax.shard_map(on_device, mesh=mesh, in_specs=in_specs, out_specs=rows, check_vma=False)
```

time: 213 us -> 86.5 us (0.41)
  waiting for transfers between devices: 84.2 us -> 9.86 us
  Pallas kernels: 0 us -> 47.5 us
  matrix products: 47.1 us -> 0 us
  blocking collectives: 29.6 us -> 0 us
  local copies, waits for them, and re-layouts: 28.8 us -> 1.26 us
  starting transfers between devices: 0.09 us -> 23.6 us
  between operations: 13.2 us -> 0.25 us
  other arithmetic: 9.93 us -> 3.89 us
    reduce_scatter x2 -> x0, waiting for transfers between devices: 65.9 us -> none  [the longest x1 44.1 us: on_device(): lax.psum_scatter(partial_value, 'narrow', scatter_dimension=0, tiled=True)]
    pallas_call x0 -> x7, Pallas kernels: none -> 47.5 us  [the longest x5 29.1 us: forward(): pl.pallas_call(kernel, in_specs=[SMEM] + [VMEM] * len(blocks) + [HBM] * l...]
    dot_general x3 -> x0, matrix products: 47.1 us -> none  [the longest x1 19.8 us: on_device(): lax.dot_general(piece, both_weights, (((1,), (1,)), ((), ())), preferred_...]
    ppermute x0 -> x20, starting transfers between devices: none -> 23.6 us  [swap(): return lax.ppermute(x, axis, [(i, i ^ k) for i in range(mesh.shape[axis])])]
    unnamed x17 -> x12, local copies, waits for them, and re-layouts: 20.3 us -> 0.87 us
    all_gather x1 -> x0, waiting for transfers between devices: 18.2 us -> none  [on_device(): back_both = lax.all_gather(back_share, 'narrow', axis=0, tiled=True)]
    all_gather x1 -> x0, blocking collectives: 15.6 us -> none  [on_device(): piece = lax.all_gather(stacked, 'wide', axis=1, tiled=True)]
    psum x2 -> x0, blocking collectives: 14 us -> none  [the longest x1 8.34 us: on_device(): squares = lax.psum(jnp.sum(latent * latent, axis=1), 'narrow')]
  transfers between devices with their start and end apart: 3 -> 20, of which waited for: 3 -> 7; matrix products, arithmetic and copies ran while one was open for 0% -> 1% of each run, Pallas kernels for 0% -> 44%
where the time goes in v2:
time: 86.5 us; the launch traced here: 86.3 us
  Pallas kernels  47.5 us (55%)
  starting transfers between devices  23.6 us (27%)
  waiting for transfers between devices  9.86 us (11%)
  other arithmetic  3.89 us (4%)
  local copies, waits for them, and re-layouts  1.26 us (1%)
    pallas_call x5, Pallas kernels, forward(): pl.pallas_call(kernel, in_specs=[SMEM] + [VMEM] * len(blocks) + [HBM] * l...  29.1 us
    ppermute x20, starting transfers between devices, swap(): return lax.ppermute(x, axis, [(i, i ^ k) for i in range(mesh.shape[axis])])  23.6 us
    pallas_call x2, Pallas kernels, backward(): pl.pallas_call(kernel, in_specs=[SMEM] + [VMEM] * len(rows) + [HBM] * len...  18.4 us
    ppermute x20, waiting for transfers between devices, swap(): return lax.ppermute(x, axis, [(i, i ^ k) for i in range(mesh.shape[axis])])  9.86 us
  transfers between devices with their start and end apart: 20, of which 7 were waited for; matrix products, arithmetic and copies ran while one was open for 1% of the time, Pallas kernels for 44%

profile of v2, /device:TPU:0, one launch (start us, length us, event | category | flops | bytes accessed | tf_op | source)
XLA Modules:
  0.0 86.3 jit_solution(11003385872587705539)
XLA Ops:
  0.0 1.1 %multiply_reduce_fusion = f32[16]{0:T(128)S(1)} fusion(bf16[16,2048]{1,0:T(8,128)(2,1)} %param.8, f32[16,2048]{1,0:T(8,128)} %param.10, s32[16,2048]{1,0:T(8,128)} %param.9), kind=kLoop, calls=%fused_computation.12 | loop fusion | flops 262128 | bytes 327744 | tf_op jit(solution)/shard_map/reduce_sum | solution.py:239
  1.1 0.1 copy.16
  1.2 2.4 %collective-permute-start.2 = (f32[16,1]{1,0:T(8,128)S(1)}, f32[16,1]{1,0:T(8,128)S(1)}, u32[]{:S(2)}, u32[]{:S(2)}) collective-permute-start(f32[16,1]{1,0:T(8,128)S(1)} %copy.16), channel_id=1, source_target_pairs={{0,3},{1,2},{2,1},{3,0},{4,7},{5,6},{6,5},{7,4},{8,11},{9,10},{10,... | collective-permute-start | bytes 200 | tf_op jit(solution)/shard_map/ppermute | solution.py:177
  3.6 0.6 collective-permute-start.1
  4.2 0.1 collective-permute-start
  4.3 3.9 %collective-permute-start.5 = (bf16[16,2048]{1,0:T(8,128)(2,1)}, bf16[16,2048]{1,0:T(8,128)(2,1)S(1)}, u32[]{:S(2)}, u32[]{:S(2)}) collective-permute-start(bf16[16,2048]{1,0:T(8,128)(2,1)} %refs_0_.3), channel_id=1, source_target_pairs={{0,12},{4,8},{8,4},{12,0},{1,13},{5,9},{9,5},{13,1},{2,14},{6,10},... | collective-permute-start | bytes 196616 | tf_op jit(solution)/shard_map/ppermute | solution.py:177
  8.2 0.6 collective-permute-start.3
  8.7 0.1 rsqrt_reduce_fusion
  8.8 1.1 %multiply_convert_fusion.2.refs_0_ = bf16[16,2048]{1,0:T(8,128)(2,1)S(1)} fusion(bf16[16,2048]{1,0:T(8,128)(2,1)} %param.8, f32[2048]{0:T(1024)} %param.12, f32[16]{0:T(128)S(1)} %rsqrt_reduce_fusion, f32[16,2048]{1,0:T(8,128)} %param.10, s32[16,2048]{1,0:T(8,128)} %param.9), kind=kLoop, calls=%fused_computation.11 | loop fusion | flops 294912 | bytes 401472 | tf_op jit(solution)/shard_map/convert_element_type | solution.py:246
  10.0 3.9 %collective-permute-start.8 = (bf16[16,2048]{1,0:T(8,128)(2,1)S(1)}, bf16[16,2048]{1,0:T(8,128)(2,1)S(1)}, u32[]{:S(2)}, u32[]{:S(2)}) collective-permute-start(bf16[16,2048]{1,0:T(8,128)(2,1)S(1)} %multiply_convert_fusion.2.refs_0_), channel_id=1, source_target_pairs={{0,12},{4,8},{8,4},{12,0},{1,13},{5,9},{9,5},{13,1},{2,14},{6,10},... | collective-permute-start | bytes 196616 | tf_op jit(solution)/shard_map/ppermute | solution.py:177
  13.9 0.6 collective-permute-start.6
  14.5 0.9 %collective-permute-done.4.refs_2_ = bf16[16,2048]{1,0:T(8,128)(2,1)S(1)} collective-permute-done((bf16[16,2048]{1,0:T(8,128)(2,1)}, bf16[16,2048]{1,0:T(8,128)(2,1)S(1)}, u32[]{:S(2)}, u32[]{:S(2)}) %collective-permute-start.4) | collective-permute-done | bytes 65568 | tf_op jit(solution)/shard_map/ppermute | solution.py:177
  15.4 0.8 copy-done
  16.2 5.9 %back_hidden_send.1 = f32[64,2560]{1,0:T(8,128)S(1)} custom-call(s32[1]{0:T(128)} %bitcast.1.index_ref, bf16[16,2048]{1,0:T(8,128)(2,1)S(1)} %copy-done, bf16[16,2048]{1,0:T(8,128)(2,1)S(1)} %collective-permute-done.3.refs_1_, bf16[16,2048]{1,0:T(8,128)(2,1)S(1)} %collective-permute-done.4.refs_2_, bf16[16,2048]{1,0:T(8,128)(2,1)S(1)} %collective-permute-done.5.refs_3_, ...), custom_call_target="tpu_custom_call" | custom-call | flops 671088640 | bytes 10485760 | tf_op jit(solution)/shard_map/back_hidden_send/pallas_call | solution.py:82
  22.2 0.1 collective-permute-start.9
  22.3 5.9 %back_hidden_keep.1 = f32[64,2560]{1,0:T(8,128)S(1)} custom-call(s32[1]{0:T(128)} %bitcast.1.index_ref, bf16[16,2048]{1,0:T(8,128)(2,1)S(1)} %copy-done, bf16[16,2048]{1,0:T(8,128)(2,1)S(1)} %collective-permute-done.3.refs_1_, bf16[16,2048]{1,0:T(8,128)(2,1)S(1)} %collective-permute-done.4.refs_2_, bf16[16,2048]{1,0:T(8,128)(2,1)S(1)} %collective-permute-done.5.refs_3_, ...), custom_call_target="tpu_custom_call" | custom-call | flops 671088640 | bytes 10485760 | tf_op jit(solution)/shard_map/back_hidden_keep/pallas_call | solution.py:82
  28.3 3.1 %collective-permute-start.10 = (bf16[64,1280]{1,0:T(8,128)(2,1)S(1)}, bf16[64,1280]{1,0:T(8,128)(2,1)S(1)}, u32[]{:S(2)}, u32[]{:S(2)}) collective-permute-start(bf16[64,1280]{1,0:T(8,128)(2,1)S(1)} %fusion.refs_6_), channel_id=1, source_target_pairs={{0,2},{1,3},{2,0},{3,1},{4,6},{5,7},{6,4},{7,5},{8,10},{9,11},{10,... | collective-permute-start | bytes 491528 | tf_op jit(solution)/shard_map/ppermute | solution.py:177
  31.3 4.7 %gate_up_near_far.1.refs_6_ = f32[64,2560]{1,0:T(8,128)S(1)} custom-call(s32[1]{0:T(128)} %bitcast.1.index_ref, bf16[16,2048]{1,0:T(8,128)(2,1)S(1)} %multiply_convert_fusion.2.refs_0_, bf16[16,2048]{1,0:T(8,128)(2,1)S(1)} %collective-permute-done.6.refs_5_.refs_1_, bf16[16,2048]{1,0:T(8,128)(2,1)S(1)} %collective-permute-done.7.refs_6_.refs_2_, ...), custom_call_target="tpu_custom_call" | custom-call | flops 671088640 | bytes 10485760 | tf_op jit(solution)/shard_map/gate_up_near_far/pallas_call | solution.py:82
  36.1 0.1 collective-permute-done.10
  36.2 0.2 collective-permute-start.11
  36.3 4.7 %gate_up_far.1 = f32[64,2560]{1,0:T(8,128)S(1)} custom-call(s32[1]{0:T(128)} %bitcast.1.index_ref, bf16[16,2048]{1,0:T(8,128)(2,1)S(1)} %multiply_convert_fusion.2.refs_0_, bf16[16,2048]{1,0:T(8,128)(2,1)S(1)} %collective-permute-done.6.refs_5_.refs_1_, bf16[16,2048]{1,0:T(8,128)(2,1)S(1)} %collective-permute-done.7.refs_6_.refs_2_, ...), custom_call_target="tpu_custom_call" | custom-call | flops 671088640 | bytes 10485760 | tf_op jit(solution)/shard_map/gate_up_far/pallas_call | solution.py:82
  41.1 0.1 add_convert_fusion.refs_6_
  41.2 1.6 %collective-permute-start.12 = (bf16[64,2560]{1,0:T(8,128)(2,1)S(1)}, bf16[64,2560]{1,0:T(8,128)(2,1)S(1)}, u32[]{:S(2)}, u32[]{:S(2)}) collective-permute-start(bf16[64,2560]{1,0:T(8,128)(2,1)S(1)} %add_convert_fusion.refs_6_), channel_id=1, source_target_pairs={{0,2},{1,3},{2,0},{3,1},{4,6},{5,7},{6,4},{7,5},{8,10},{9,11},{10,... | collective-permute-start | bytes 983048 | tf_op jit(solution)/shard_map/ppermute | solution.py:177
  42.8 7.9 %gate_up_near_own.1 = f32[64,5120]{1,0:T(8,128)S(1)} custom-call(s32[1]{0:T(128)} %bitcast.1.index_ref, bf16[16,2048]{1,0:T(8,128)(2,1)S(1)} %multiply_convert_fusion.2.refs_0_, bf16[16,2048]{1,0:T(8,128)(2,1)S(1)} %collective-permute-done.6.refs_5_.refs_1_, bf16[16,2048]{1,0:T(8,128)(2,1)S(1)} %collective-permute-done.7.refs_6_.refs_2_, ...), custom_call_target="tpu_custom_call" | custom-call | flops 1342177280 | bytes 20971520 | tf_op jit(solution)/shard_map/gate_up_near_own/pallas_call | solution.py:82
  50.7 0.6 collective-permute-done.12
  51.3 0.1 collective-permute-start.13
  51.4 2.1 %collective-permute-done.13 = f32[64,2560]{1,0:T(8,128)S(1)} collective-permute-done((f32[64,2560]{1,0:T(8,128)S(1)}, f32[64,2560]{1,0:T(8,128)S(1)}, u32[]{:S(2)}, u32[]{:S(2)}) %collective-permute-start.13) | collective-permute-done | bytes 655392 | tf_op jit(solution)/shard_map/ppermute | solution.py:177
  53.5 0.1 convert_add_fusion
  53.6 0.3 add_reduce_fusion
  53.9 0.1 broadcast_in_dim.8
  54.0 0.1 broadcast_in_dim.7
  54.1 0.1 concatenate.3.refs_0_
  54.2 0.2 collective-permute-start.14
  54.4 1.8 %collective-permute-start.15 = (bf16[64,2688]{1,0:T(8,128)(2,1)S(1)}, bf16[64,2688]{1,0:T(8,128)(2,1)S(1)}, u32[]{:S(2)}, u32[]{:S(2)}) collective-permute-start(bf16[64,2688]{1,0:T(8,128)(2,1)S(1)} %concatenate.3.refs_0_), channel_id=1, source_target_pairs={{0,2},{1,3},{2,0},{3,1},{4,6},{5,7},{6,4},{7,5},{8,10},{9,11},{10,... | collective-permute-start | bytes 1032200 | tf_op jit(solution)/shard_map/ppermute | solution.py:177
  56.1 9.3 %back_own_near.1.refs_4_ = f32[64,2176]{1,0:T(8,128)S(1)} custom-call(s32[1]{0:T(128)} %bitcast.1.index_ref, bf16[64,2688]{1,0:T(8,128)(2,1)S(1)} %concatenate.3.refs_0_, bf16[64,2688]{1,0:T(8,128)(2,1)S(1)} %collective-permute-done.14.refs_1_, bf16[2048,5120]{1,0:T(8,128)(2,1)} %refs_2_.3, bf16[2048,5120]{1,0:T(8,128)(2,1)} %refs_3_.3), custom_call_target="tpu_custom_call" | custom-call | flops 1342177280 | bytes 20971520 | tf_op jit(solution)/shard_map/back_own_near/pallas_call | solution.py:134
  65.4 0.0 copy-start.1
  65.4 0.0 copy-start.3
  65.4 0.0 copy-start.4
  65.5 0.1 collective-permute-start.16
  65.6 1.6 %collective-permute-done.16.refs_1_ = bf16[64,2688]{1,0:T(8,128)(2,1)S(1)} collective-permute-done((bf16[64,2688]{1,0:T(8,128)(2,1)S(1)}, bf16[64,2688]{1,0:T(8,128)(2,1)S(1)}, u32[]{:S(2)}, u32[]{:S(2)}) %collective-permute-start.16) | collective-permute-done | bytes 344096 | tf_op jit(solution)/shard_map/ppermute | solution.py:177
  67.2 9.1 %back_far_near_far.1 = (f32[16,2176]{1,0:T(8,128)S(1)}, bf16[16,2176]{1,0:T(8,128)(2,1)S(1)}, bf16[16,2176]{1,0:T(8,128)(2,1)S(1)}, bf16[16,2176]{1,0:T(8,128)(2,1)S(1)}) custom-call(s32[1]{0:T(128)} %bitcast.1.index_ref, bf16[64,2688]{1,0:T(8,128)(2,1)S(1)} %collective-permute-done.15.refs_0_, bf16[64,2688]{1,0:T(8,128)(2,1)S(1)} %collective-permute-done.16.refs_1_, ...), custom_call_target="tpu_custom_call" | custom-call | flops 1342177280 | bytes 20971520 | tf_op jit(solution)/shard_map/back_far_near_far/pallas_call | solution.py:134
  76.3 0.1 collective-permute-start.17
  76.4 1.9 %collective-permute-start.18 = (bf16[16,2176]{1,0:T(8,128)(2,1)S(1)}, bf16[16,2176]{1,0:T(8,128)(2,1)S(1)}, u32[]{:S(2)}, u32[]{:S(2)}) collective-permute-start(bf16[16,2176]{1,0:T(8,128)(2,1)S(1)} %get-tuple-element.33), channel_id=1, source_target_pairs={{0,8},{4,12},{8,0},{12,4},{1,9},{5,13},{9,1},{13,5},{2,10},{6,14},... | collective-permute-start | bytes 208904 | tf_op jit(solution)/shard_map/ppermute | solution.py:177
  78.3 2.5 %collective-permute-start.19 = (bf16[16,2176]{1,0:T(8,128)(2,1)S(1)}, bf16[16,2176]{1,0:T(8,128)(2,1)S(1)}, u32[]{:S(2)}, u32[]{:S(2)}) collective-permute-start(bf16[16,2176]{1,0:T(8,128)(2,1)S(1)} %get-tuple-element.34), channel_id=1, source_target_pairs={{0,12},{4,8},{8,4},{12,0},{1,13},{5,9},{9,5},{13,1},{2,14},{6,10},... | collective-permute-start | bytes 208904 | tf_op jit(solution)/shard_map/ppermute | solution.py:177
  80.8 0.9 %collective-permute-done.17 = bf16[16,2176]{1,0:T(8,128)(2,1)S(1)} collective-permute-done((bf16[16,2176]{1,0:T(8,128)(2,1)S(1)}, bf16[16,2176]{1,0:T(8,128)(2,1)S(1)}, u32[]{:S(2)}, u32[]{:S(2)}) %collective-permute-start.17) | collective-permute-done | bytes 69664 | tf_op jit(solution)/shard_map/ppermute | solution.py:177
  81.6 3.7 %collective-permute-done.18 = bf16[16,2176]{1,0:T(8,128)(2,1)S(1)} collective-permute-done((bf16[16,2176]{1,0:T(8,128)(2,1)S(1)}, bf16[16,2176]{1,0:T(8,128)(2,1)S(1)}, u32[]{:S(2)}, u32[]{:S(2)}) %collective-permute-start.18) | collective-permute-done | bytes 69664 | tf_op jit(solution)/shard_map/ppermute | solution.py:177
  85.3 0.2 multiply_reduce_fusion.1
  85.6 0.8 multiply_add_fusion
  (26 shorter events, 0.1 us)
Async XLA Ops:
  1.2 6.9 %collective-permute-start.2 = (f32[16,1]{1,0:T(8,128)S(1)}, f32[16,1]{1,0:T(8,128)S(1)}, u32[]{:S(2)}, u32[]{:S(2)}) collective-permute-start(f32[16,1]{1,0:T(8,128)S(1)} %copy.16), channel_id=1, source_target_pairs={{0,3},{1,2},{2,1},{3,0},{4,7},{5,6},{6,5},{7,4},{8,11},{9,10},{10,... | collective-permute-start | bytes 200 | tf_op jit(solution)/shard_map/ppermute | solution.py:177
  3.6 5.1 %collective-permute-start.1 = (f32[16,1]{1,0:T(8,128)S(1)}, f32[16,1]{1,0:T(8,128)S(1)}, u32[]{:S(2)}, u32[]{:S(2)}) collective-permute-start(f32[16,1]{1,0:T(8,128)S(1)} %copy.16), channel_id=1, source_target_pairs={{0,2},{1,3},{2,0},{3,1},{4,6},{5,7},{6,4},{7,5},{8,10},{9,11},{10,... | collective-permute-start | bytes 200 | tf_op jit(solution)/shard_map/ppermute | solution.py:177
  4.2 4.5 %collective-permute-start = (f32[16,1]{1,0:T(8,128)S(1)}, f32[16,1]{1,0:T(8,128)S(1)}, u32[]{:S(2)}, u32[]{:S(2)}) collective-permute-start(f32[16,1]{1,0:T(8,128)S(1)} %copy.16), channel_id=1, source_target_pairs={{0,1},{1,0},{2,3},{3,2},{4,5},{5,4},{6,7},{7,6},{8,9},{9,8},{10,11... | collective-permute-start | bytes 200 | tf_op jit(solution)/shard_map/ppermute | solution.py:177
  4.3 9.6 %collective-permute-start.5 = (bf16[16,2048]{1,0:T(8,128)(2,1)}, bf16[16,2048]{1,0:T(8,128)(2,1)S(1)}, u32[]{:S(2)}, u32[]{:S(2)}) collective-permute-start(bf16[16,2048]{1,0:T(8,128)(2,1)} %refs_0_.3), channel_id=1, source_target_pairs={{0,12},{4,8},{8,4},{12,0},{1,13},{5,9},{9,5},{13,1},{2,14},{6,10},... | collective-permute-start | bytes 196616 | tf_op jit(solution)/shard_map/ppermute | solution.py:177
  8.1 7.2 %collective-permute-start.4 = (bf16[16,2048]{1,0:T(8,128)(2,1)}, bf16[16,2048]{1,0:T(8,128)(2,1)S(1)}, u32[]{:S(2)}, u32[]{:S(2)}) collective-permute-start(bf16[16,2048]{1,0:T(8,128)(2,1)} %refs_0_.3), channel_id=1, source_target_pairs={{0,8},{4,12},{8,0},{12,4},{1,9},{5,13},{9,1},{13,5},{2,10},{6,14},... | collective-permute-start | bytes 196616 | tf_op jit(solution)/shard_map/ppermute | solution.py:177
  8.2 7.2 %collective-permute-start.3 = (bf16[16,2048]{1,0:T(8,128)(2,1)}, bf16[16,2048]{1,0:T(8,128)(2,1)S(1)}, u32[]{:S(2)}, u32[]{:S(2)}) collective-permute-start(bf16[16,2048]{1,0:T(8,128)(2,1)} %refs_0_.3), channel_id=1, source_target_pairs={{0,4},{4,0},{8,12},{12,8},{1,5},{5,1},{9,13},{13,9},{2,6},{6,2},{1... | collective-permute-start | bytes 196616 | tf_op jit(solution)/shard_map/ppermute | solution.py:177
  10.0 12.2 %collective-permute-start.8 = (bf16[16,2048]{1,0:T(8,128)(2,1)S(1)}, bf16[16,2048]{1,0:T(8,128)(2,1)S(1)}, u32[]{:S(2)}, u32[]{:S(2)}) collective-permute-start(bf16[16,2048]{1,0:T(8,128)(2,1)S(1)} %multiply_convert_fusion.2.refs_0_), channel_id=1, source_target_pairs={{0,12},{4,8},{8,4},{12,0},{1,13},{5,9},{9,5},{13,1},{2,14},{6,10},... | collective-permute-start | bytes 196616 | tf_op jit(solution)/shard_map/ppermute | solution.py:177
  13.8 8.3 %collective-permute-start.7 = (bf16[16,2048]{1,0:T(8,128)(2,1)S(1)}, bf16[16,2048]{1,0:T(8,128)(2,1)S(1)}, u32[]{:S(2)}, u32[]{:S(2)}) collective-permute-start(bf16[16,2048]{1,0:T(8,128)(2,1)S(1)} %multiply_convert_fusion.2.refs_0_), channel_id=1, source_target_pairs={{0,8},{4,12},{8,0},{12,4},{1,9},{5,13},{9,1},{13,5},{2,10},{6,14},... | collective-permute-start | bytes 196616 | tf_op jit(solution)/shard_map/ppermute | solution.py:177
  13.9 8.3 %collective-permute-start.6 = (bf16[16,2048]{1,0:T(8,128)(2,1)S(1)}, bf16[16,2048]{1,0:T(8,128)(2,1)S(1)}, u32[]{:S(2)}, u32[]{:S(2)}) collective-permute-start(bf16[16,2048]{1,0:T(8,128)(2,1)S(1)} %multiply_convert_fusion.2.refs_0_), channel_id=1, source_target_pairs={{0,4},{4,0},{8,12},{12,8},{1,5},{5,1},{9,13},{13,9},{2,6},{6,2},{1... | collective-permute-start | bytes 196616 | tf_op jit(solution)/shard_map/ppermute | solution.py:177
  15.4 0.8 copy-start
  22.2 6.0 %collective-permute-start.9 = (f32[64,2560]{1,0:T(8,128)S(1)}, f32[64,2560]{1,0:T(8,128)S(1)}, u32[]{:S(2)}, u32[]{:S(2)}) collective-permute-start(f32[64,2560]{1,0:T(8,128)S(1)} %back_hidden_send.1), channel_id=1, source_target_pairs={{0,1},{1,0},{2,3},{3,2},{4,5},{5,4},{6,7},{7,6},{8,9},{9,8},{10,11... | collective-permute-start | bytes 1966088 | tf_op jit(solution)/shard_map/ppermute | solution.py:177
  28.3 7.9 %collective-permute-start.10 = (bf16[64,1280]{1,0:T(8,128)(2,1)S(1)}, bf16[64,1280]{1,0:T(8,128)(2,1)S(1)}, u32[]{:S(2)}, u32[]{:S(2)}) collective-permute-start(bf16[64,1280]{1,0:T(8,128)(2,1)S(1)} %fusion.refs_6_), channel_id=1, source_target_pairs={{0,2},{1,3},{2,0},{3,1},{4,6},{5,7},{6,4},{7,5},{8,10},{9,11},{10,... | collective-permute-start | bytes 491528 | tf_op jit(solution)/shard_map/ppermute | solution.py:177
  36.2 4.9 %collective-permute-start.11 = (f32[64,2560]{1,0:T(8,128)S(1)}, f32[64,2560]{1,0:T(8,128)S(1)}, u32[]{:S(2)}, u32[]{:S(2)}) collective-permute-start(f32[64,2560]{1,0:T(8,128)S(1)} %gate_up_near_far.1.refs_6_), channel_id=1, source_target_pairs={{0,1},{1,0},{2,3},{3,2},{4,5},{5,4},{6,7},{7,6},{8,9},{9,8},{10,11... | collective-permute-start | bytes 1966088 | tf_op jit(solution)/shard_map/ppermute | solution.py:177
  41.2 10.1 %collective-permute-start.12 = (bf16[64,2560]{1,0:T(8,128)(2,1)S(1)}, bf16[64,2560]{1,0:T(8,128)(2,1)S(1)}, u32[]{:S(2)}, u32[]{:S(2)}) collective-permute-start(bf16[64,2560]{1,0:T(8,128)(2,1)S(1)} %add_convert_fusion.refs_6_), channel_id=1, source_target_pairs={{0,2},{1,3},{2,0},{3,1},{4,6},{5,7},{6,4},{7,5},{8,10},{9,11},{10,... | collective-permute-start | bytes 983048 | tf_op jit(solution)/shard_map/ppermute | solution.py:177
  51.3 2.2 %collective-permute-start.13 = (f32[64,2560]{1,0:T(8,128)S(1)}, f32[64,2560]{1,0:T(8,128)S(1)}, u32[]{:S(2)}, u32[]{:S(2)}) collective-permute-start(f32[64,2560]{1,0:T(8,128)S(1)} %slice.71), channel_id=1, source_target_pairs={{0,1},{1,0},{2,3},{3,2},{4,5},{5,4},{6,7},{7,6},{8,9},{9,8},{10,11... | collective-permute-start | bytes 1966088 | tf_op jit(solution)/shard_map/ppermute | solution.py:177
  54.2 2.0 %collective-permute-start.14 = (bf16[64,2688]{1,0:T(8,128)(2,1)S(1)}, bf16[64,2688]{1,0:T(8,128)(2,1)S(1)}, u32[]{:S(2)}, u32[]{:S(2)}) collective-permute-start(bf16[64,2688]{1,0:T(8,128)(2,1)S(1)} %concatenate.3.refs_0_), channel_id=1, source_target_pairs={{0,1},{1,0},{2,3},{3,2},{4,5},{5,4},{6,7},{7,6},{8,9},{9,8},{10,11... | collective-permute-start | bytes 1032200 | tf_op jit(solution)/shard_map/ppermute | solution.py:177
  54.4 11.1 %collective-permute-start.15 = (bf16[64,2688]{1,0:T(8,128)(2,1)S(1)}, bf16[64,2688]{1,0:T(8,128)(2,1)S(1)}, u32[]{:S(2)}, u32[]{:S(2)}) collective-permute-start(bf16[64,2688]{1,0:T(8,128)(2,1)S(1)} %concatenate.3.refs_0_), channel_id=1, source_target_pairs={{0,2},{1,3},{2,0},{3,1},{4,6},{5,7},{6,4},{7,5},{8,10},{9,11},{10,... | collective-permute-start | bytes 1032200 | tf_op jit(solution)/shard_map/ppermute | solution.py:177
  65.4 20.1 %copy-start.1 = (bf16[16,2048]{1,0:T(8,128)(2,1)S(1)}, bf16[16,2048]{1,0:T(8,128)(2,1)}, u32[]{:S(2)}) copy-start(bf16[16,2048]{1,0:T(8,128)(2,1)} %refs_0_.3) | copy-start | bytes 196612
  65.4 20.1 %copy-start.2 = (f32[16,2048]{1,0:T(8,128)S(1)}, f32[16,2048]{1,0:T(8,128)}, u32[]{:S(2)}) copy-start(f32[16,2048]{1,0:T(8,128)} %param.10) | copy-start | bytes 393220
  65.4 20.1 %copy-start.3 = (s32[16,2048]{1,0:T(8,128)S(1)}, s32[16,2048]{1,0:T(8,128)}, u32[]{:S(2)}) copy-start(s32[16,2048]{1,0:T(8,128)} %param.9) | copy-start | bytes 393220
  65.4 20.1 %copy-start.4 = (bf16[16,2048]{1,0:T(8,128)(2,1)S(1)}, bf16[16,2048]{1,0:T(8,128)(2,1)}, u32[]{:S(2)}) copy-start(bf16[16,2048]{1,0:T(8,128)(2,1)} %param.8) | copy-start | bytes 196612
  65.5 20.1 %copy-start.5 = (f32[2048]{0:T(1024)S(1)}, f32[2048]{0:T(1024)}, u32[]{:S(2)}) copy-start(f32[2048]{0:T(1024)} %param.12) | copy-start | bytes 24580
  65.5 1.7 %collective-permute-start.16 = (bf16[64,2688]{1,0:T(8,128)(2,1)S(1)}, bf16[64,2688]{1,0:T(8,128)(2,1)S(1)}, u32[]{:S(2)}, u32[]{:S(2)}) collective-permute-start(bf16[64,2688]{1,0:T(8,128)(2,1)S(1)} %collective-permute-done.15.refs_0_), channel_id=1, source_target_pairs={{0,1},{1,0},{2,3},{3,2},{4,5},{5,4},{6,7},{7,6},{8,9},{9,8},{10,11... | collective-permute-start | bytes 1032200 | tf_op jit(solution)/shard_map/ppermute | solution.py:177
  76.3 5.3 %collective-permute-start.17 = (bf16[16,2176]{1,0:T(8,128)(2,1)S(1)}, bf16[16,2176]{1,0:T(8,128)(2,1)S(1)}, u32[]{:S(2)}, u32[]{:S(2)}) collective-permute-start(bf16[16,2176]{1,0:T(8,128)(2,1)S(1)} %get-tuple-element.32), channel_id=1, source_target_pairs={{0,4},{4,0},{8,12},{12,8},{1,5},{5,1},{9,13},{13,9},{2,6},{6,2},{1... | collective-permute-start | bytes 208904 | tf_op jit(solution)/shard_map/ppermute | solution.py:177
  76.4 8.9 %collective-permute-start.18 = (bf16[16,2176]{1,0:T(8,128)(2,1)S(1)}, bf16[16,2176]{1,0:T(8,128)(2,1)S(1)}, u32[]{:S(2)}, u32[]{:S(2)}) collective-permute-start(bf16[16,2176]{1,0:T(8,128)(2,1)S(1)} %get-tuple-element.33), channel_id=1, source_target_pairs={{0,8},{4,12},{8,0},{12,4},{1,9},{5,13},{9,1},{13,5},{2,10},{6,14},... | collective-permute-start | bytes 208904 | tf_op jit(solution)/shard_map/ppermute | solution.py:177
  78.3 7.0 %collective-permute-start.19 = (bf16[16,2176]{1,0:T(8,128)(2,1)S(1)}, bf16[16,2176]{1,0:T(8,128)(2,1)S(1)}, u32[]{:S(2)}, u32[]{:S(2)}) collective-permute-start(bf16[16,2176]{1,0:T(8,128)(2,1)S(1)} %get-tuple-element.34), channel_id=1, source_target_pairs={{0,12},{4,8},{8,4},{12,0},{1,13},{5,9},{9,5},{13,1},{2,14},{6,10},... | collective-permute-start | bytes 208904 | tf_op jit(solution)/shard_map/ppermute | solution.py:177

commit v3 on v2

v3 whole, which is shorter than its diff:
```python
import jax
import jax.numpy as jnp
from jax import lax
from jax.experimental import pallas as pl
from jax.experimental.pallas import tpu as pltpu
from jax.sharding import PartitionSpec as P

EPS = 1e-05
ASCENT = 0.5
LANES = 128
STEP = 512
FIRST_FLYING = 8

NN = (((1,), (0,)), ((), ()))
NT = (((1,), (1,)), ((), ()))
ANY = pl.BlockSpec(memory_space=pl.ANY)
HBM = pl.BlockSpec(memory_space=pltpu.HBM)
SMEM = pl.BlockSpec(memory_space=pltpu.SMEM)
VMEM = pl.BlockSpec(memory_space=pltpu.VMEM)
F32 = jnp.float32
BF16 = jnp.bfloat16


def dot(a, b, dims):
    return lax.dot_general(a, b, dims, preferred_element_type=F32)


def steps(length):
    count = next(c for c in range(max(1, length // STEP), length + 1) if length % (c * LANES) == 0)
    return [(i * (length // count), length // count) for i in range(count)]


def params(mebibytes):
    return pltpu.CompilerParams(vmem_limit_bytes=mebibytes << 20)


def in_hbm(arrays):
    return [pltpu.with_memory_space_constraint(x, pltpu.HBM) for x in arrays]


def in_vmem(x):
    return pltpu.with_memory_space_constraint(x, pltpu.VMEM)


def cost(m, k, n):
    return pl.CostEstimate(flops=2 * m * k * n, bytes_accessed=2 * k * n, transcendentals=0)


def split(x):
    high = x.astype(BF16)
    low = (x - high.astype(F32)).astype(BF16)
    return jnp.concatenate([jnp.broadcast_to(y, (x.shape[0], LANES // 2)) for y in (high, low)], axis=1)


def joined(x):
    return x[:, :1].astype(F32) + x[:, LANES // 2 : LANES // 2 + 1].astype(F32)


def bring(index_ref, pick, share, sources, target_ref, place, sems, first=0):
    copies = []
    for at, n in steps(share):
        for i, source in enumerate(sources):
            begin = pl.multiple_of((index_ref[0] ^ pick) * share + at, LANES)
            copies.append(
                pltpu.make_async_copy(
                    source.at[:, pl.ds(begin, n)],
                    target_ref.at[place + i, :, pl.ds(at, n)],
                    sems.at[first + len(copies)],
                )
            )
    return copies


def hidden_gradient(index, blocks, down_weight, pair, pick, picks, share):
    size, width = blocks[0].shape
    tokens = size * len(blocks)
    parts = [(r, at, n) for r in range(len(picks)) for at, n in steps(share)]
    half = len(picks) // 2

    def kernel(index_ref, *refs):
        block_refs, refs = refs[: len(blocks)], refs[len(blocks) :]
        down_ref, refs = refs[0], refs[1:]
        pair_refs, refs = refs[: len(pair)], refs[len(pair) :]
        out_refs, refs = refs[:2], refs[2:]
        held_ref, rows_ref, down_parts, sems, pair_sems = refs
        copies = []
        for j, (r, at, n) in enumerate(parts):
            begin = pl.multiple_of((index_ref[0] ^ picks[r]) * share + at, LANES)
            copies.append(pltpu.make_async_copy(down_ref.at[pl.ds(begin, n), :], down_parts.at[j], sems.at[j]))
        copies += bring(index_ref, pick, share, pair_refs, held_ref, 0, pair_sems)
        for copy in copies[:FIRST_FLYING]:
            copy.start()
        for p, block in enumerate(block_refs):
            rows_ref[p * size : (p + 1) * size, :] = block[...]
        for j, (r, at, n) in enumerate(parts):
            copies[j].wait()
            for copy in copies[j + FIRST_FLYING : j + FIRST_FLYING + 1]:
                copy.start()
            out_refs[r // half][:, pl.ds(r % half * share + at, n)] = dot(rows_ref[...], down_parts[j], NT)
        for copy in copies[len(parts) + FIRST_FLYING :]:
            copy.start()
        for copy in copies[len(parts) :]:
            copy.wait()

    count = len(steps(share))
    total = len(picks) * share
    return pl.pallas_call(
        kernel,
        in_specs=[SMEM] + [VMEM] * len(blocks) + [HBM] * (1 + len(pair)),
        out_specs=[VMEM] * 3,
        out_shape=[jax.ShapeDtypeStruct((tokens, half * share), F32)] * 2
        + [pltpu.VMEM((len(pair), width, share), BF16)],
        scratch_shapes=[
            pltpu.VMEM((tokens, width), BF16),
            pltpu.VMEM((len(parts), parts[0][2], width), BF16),
            pltpu.SemaphoreType.DMA((len(parts),)),
            pltpu.SemaphoreType.DMA((len(pair) * count,)),
        ],
        compiler_params=params(26),
        cost_estimate=cost(tokens, width, total),
        name="back_hidden",
    )(index, *blocks, *in_hbm([down_weight, *pair]))


def gate_and_up(index, blocks, held, pair, picks, both, after, name):
    size, width = blocks[0].shape
    tokens = size * len(blocks)
    share = held.shape[2]
    outs = 2 if both else 1
    count = len(steps(share)) * len(pair)

    def kernel(index_ref, *refs):
        block_refs, refs = refs[: len(blocks)], refs[len(blocks) :]
        held_ref, refs = refs[0], refs[1:]
        pair_refs, refs = refs[: len(pair)], refs[len(pair) + len(after) :]
        out_refs, (next_ref, rows_ref, sems) = refs[:outs], refs[outs:]
        copies = []
        for k, pick in enumerate(picks):
            copies += bring(index_ref, pick, share, pair_refs, next_ref, k * len(pair), sems, k * count)
        for copy in copies:
            copy.start()
        for p, block in enumerate(block_refs):
            rows_ref[p * size : (p + 1) * size, :] = block[...]
        n = steps(share)[0][1]

        @pl.loop(0, share // n)
        def _(step):
            for i in range(len(pair)):
                part = dot(rows_ref[...], held_ref[i, :, pl.ds(pl.multiple_of(step * n, n), n)], NN)
                out_refs[0][:, pl.ds(pl.multiple_of(i * share + step * n, LANES), n)] = part

        for j, copy in enumerate(copies):
            copy.wait()
            if both and j < count:
                at, n = steps(share)[j // len(pair)]
                i = j % len(pair)
                part = dot(rows_ref[...], next_ref[i, :, pl.ds(at, n)], NN)
                out_refs[1][:, pl.ds(i * share + at, n)] = part

    return pl.pallas_call(
        kernel,
        in_specs=[SMEM] + [VMEM] * (len(blocks) + 1) + [HBM] * len(pair) + [ANY] * len(after),
        out_specs=[VMEM] * (outs + 1),
        out_shape=[jax.ShapeDtypeStruct((tokens, len(pair) * share), F32)] * outs
        + [pltpu.VMEM((len(pair) * len(picks), width, share), BF16)],
        scratch_shapes=[pltpu.VMEM((tokens, width), BF16), pltpu.SemaphoreType.DMA((count * len(picks),))],
        compiler_params=params(8),
        cost_estimate=cost(tokens, width, outs * len(pair) * share),
        name=name,
    )(index, *blocks, in_vmem(held), *in_hbm(pair), *after)


def backward(index, rows, held, pair, pick, stays, before, pieces, name):
    tokens = rows[0].shape[0]
    _, width, share = held.shape
    size = tokens // pieces
    extra = [] if before is None else [before]
    n = steps(width)[0][1]
    now = held.shape[0] // len(pair)

    def kernel(index_ref, *refs):
        row_refs, refs = refs[: len(rows)], refs[len(rows) :]
        held_ref, refs = refs[0], refs[1:]
        before_refs, refs = refs[: len(extra)], refs[len(extra) :]
        pair_refs, refs = refs[: len(pair)], refs[len(pair) :]
        out_refs, (next_ref, *sums_ref, sems) = refs[:pieces], refs[pieces:]
        copies = bring(index_ref, pick, share, pair_refs, next_ref, 0, sems)
        for copy in copies:
            copy.start()
        inner = sum(joined(r[:, pl.ds(2 * share, LANES)]) for r in row_refs)
        for b in before_refs:
            inner += b[:, pl.ds(width, 1)]
        for p, out in enumerate(out_refs):
            mine = inner[p * size : (p + 1) * size]
            out[:, pl.ds(width, LANES)] = split(mine) if p else jnp.broadcast_to(mine, (size, LANES))

        def products(weights, those, here):
            pairs = [(row, i) for row in range(len(those)) for i in range(len(pair))]
            return sum(
                dot(those[row][:, pl.ds(i * share, share)], weights[row * len(pair) + i, here, :], NT)
                for row, i in pairs
            )

        def finish(part, here):
            for b in before_refs:
                part += b[:, here]
            for p, out in enumerate(out_refs):
                out[:, here] = part[p * size : (p + 1) * size].astype(out.dtype)

        @pl.loop(0, width // n)
        def _(step):
            here = pl.ds(pl.multiple_of(step * n, n), n)
            part = products(held_ref, row_refs[:now], here)
            if stays:
                finish(part, here)
            else:
                sums_ref[0][:, here] = part

        for copy in copies:
            copy.wait()
        if not stays:

            @pl.loop(0, width // n)
            def _(step):
                here = pl.ds(pl.multiple_of(step * n, n), n)
                finish(sums_ref[0][:, here] + products(next_ref, row_refs[now:], here), here)

    brought = pltpu.VMEM((len(pair), width, share), BF16)
    return pl.pallas_call(
        kernel,
        in_specs=[SMEM] + [VMEM] * (len(rows) + 1 + len(extra)) + [HBM] * len(pair),
        out_specs=[VMEM] * (pieces + stays),
        out_shape=[jax.ShapeDtypeStruct((size, width + LANES), BF16 if p else F32) for p in range(pieces)]
        + [brought] * stays,
        scratch_shapes=([] if stays else [brought, pltpu.VMEM((tokens, width), F32)])
        + [pltpu.SemaphoreType.DMA((len(steps(share)) * len(pair),))],
        compiler_params=params(8 if stays else 16),
        cost_estimate=cost(tokens, len(pair) * len(rows) * share, width),
        name=name,
    )(index, *rows, in_vmem(held), *extra, *in_hbm(pair))


def latents(tokens, signs, magnitude, gain, target):
    given = (tokens, signs, magnitude)

    def kernel(*refs):
        sources, (delta_ref, latent_ref, squares_ref, *same_refs), scratch = refs[:5], refs[5:10], refs[10:]
        copies = [
            pltpu.make_async_copy(source, target, scratch[-1].at[i])
            for i, (source, target) in enumerate(zip(sources, (*scratch[:-1], *same_refs)))
        ]
        for copy in copies:
            copy.start()
        for copy in copies[: len(given)]:
            copy.wait()
        delta = (2 * scratch[1][...] - 1).astype(F32) * scratch[2][...]
        latent = scratch[0][...].astype(F32) + delta
        delta_ref[...] = delta
        latent_ref[...] = latent
        squares_ref[...] = jnp.sum(latent * latent, axis=1, keepdims=True)
        for copy in copies[len(given) :]:
            copy.wait()

    whole = jax.ShapeDtypeStruct(tokens.shape, F32)
    return pl.pallas_call(
        kernel,
        in_specs=[HBM] * 5,
        out_specs=[VMEM] * 5,
        out_shape=[
            whole,
            whole,
            jax.ShapeDtypeStruct((tokens.shape[0], 1), F32),
            jax.ShapeDtypeStruct(gain.shape, F32),
            jax.ShapeDtypeStruct(target.shape, target.dtype),
        ],
        scratch_shapes=[pltpu.VMEM(x.shape, x.dtype) for x in given] + [pltpu.SemaphoreType.DMA((5,))],
        compiler_params=params(8),
        cost_estimate=pl.CostEstimate(flops=8 * tokens.size, bytes_accessed=18 * tokens.size, transcendentals=0),
        name="latents",
    )(*in_hbm([*given, gain, target]))


def gate_terms(gate, up, back_hidden):
    sig = jax.nn.sigmoid(gate)
    back_gate = (back_hidden * up * sig * (1.0 + gate * (1.0 - sig))).astype(BF16)
    back_up = (back_hidden * gate * sig).astype(BF16)
    return back_gate, back_up


def gate_rows(own, got_near, got_far, hidden_own, hidden_near, hidden_far, held):
    tokens, share = hidden_far.shape

    def kernel(own_ref, near_ref, far_ref, hidden_own_ref, hidden_near_ref, hidden_far_ref, _, rows_ref, __):
        inner = jnp.zeros((tokens, 1), F32)
        for at, n in steps(share):
            here, there = pl.ds(at, n), pl.ds(share + at, n)
            gate, up = (own_ref[:, x] + near_ref[:, x] + far_ref[:, x].astype(F32) for x in (here, there))
            back_hidden = hidden_own_ref[:, here] + hidden_near_ref[:, here] + hidden_far_ref[:, here].astype(F32)
            back_gate, back_up = gate_terms(gate, up, back_hidden)
            rows_ref[:, here] = back_gate
            rows_ref[:, there] = back_up
            products = back_gate.astype(F32) * gate + back_up.astype(F32) * up
            inner += jnp.sum(products, axis=1, keepdims=True)
        rows_ref[:, pl.ds(2 * share, LANES)] = split(inner)

    return pl.pallas_call(
        kernel,
        in_specs=[VMEM] * 7,
        out_specs=[VMEM] * 2,
        out_shape=[
            jax.ShapeDtypeStruct((tokens, 2 * share + LANES), BF16),
            pltpu.VMEM(held.shape, held.dtype),
        ],
        input_output_aliases={6: 1},
        compiler_params=params(8),
        cost_estimate=pl.CostEstimate(
            flops=20 * tokens * share, bytes_accessed=30 * tokens * share, transcendentals=tokens * share
        ),
        name="gate",
    )(own, got_near, got_far, hidden_own, hidden_near, hidden_far, in_vmem(held))


def by_collectives(normed, target, gate_weight, up_weight, down_weight):
    stacked = jnp.stack([normed, target], axis=0)
    rows = lax.all_gather(stacked, "wide", axis=1, tiled=True)
    hidden = gate_weight.shape[1]
    sums = jnp.concatenate(
        [dot(rows[0], gate_weight, NN), dot(rows[0], up_weight, NN), dot(rows[1], down_weight, NT)], axis=1
    )
    sums = lax.psum_scatter(sums, "narrow", scatter_dimension=0, tiled=True)
    both = jnp.concatenate(
        gate_terms(sums[:, :hidden], sums[:, hidden : 2 * hidden], sums[:, 2 * hidden :]), axis=1
    )
    both = lax.all_gather(both, "narrow", axis=0, tiled=True)
    back = dot(both[:, :hidden], gate_weight, NT) + dot(both[:, hidden:], up_weight, NT)
    return lax.psum_scatter(back, "wide", scatter_dimension=0, tiled=True)


def solution(mesh):
    wide, narrow = mesh.shape["wide"], mesh.shape["narrow"]
    near, far = 1, 2

    def swap(x, axis, k):
        return lax.ppermute(x, axis, [(i, i ^ k) for i in range(mesh.shape[axis])])

    def by_swaps(normed, target, own_target, gate_weight, up_weight, down_weight):
        width, hidden = gate_weight.shape
        share = hidden // narrow
        index = lax.axis_index("narrow").astype(jnp.int32).reshape(1)
        pair = [gate_weight, up_weight]
        diagonal = near | far
        targets = [own_target] + [swap(target, "wide", k) for k in range(1, wide)]
        normeds = [normed] + [swap(normed, "wide", k) for k in range(1, wide)]

        send, keep, held_diagonal = hidden_gradient(
            index, targets, down_weight, pair, diagonal, [near, diagonal, 0, far], share
        )
        send, *normeds = lax.optimization_barrier((send, *normeds))
        got = swap(send, "narrow", near)
        part, held_far = gate_and_up(
            index, normeds, held_diagonal, pair, [far], False, [send], "gate_up_diagonal"
        )
        part, got = lax.optimization_barrier((part, got))
        hidden_far = swap((keep[:, share:] + got[:, share:]).astype(BF16), "narrow", far)
        hidden_near = got
        got = swap(part, "narrow", near)
        part, held_near = gate_and_up(index, normeds, held_far, pair, [near], False, [part], "gate_up_far")
        part, got, hidden_far = lax.optimization_barrier((part, got, hidden_far))
        sum_far = (part + got).astype(BF16)
        got_far = swap(sum_far, "narrow", far)
        part, own, held = gate_and_up(
            index, normeds, held_near, pair, [0, near], True, [sum_far], "gate_up_near_own"
        )
        part, got_far = lax.optimization_barrier((part, got_far))
        got = swap(part, "narrow", near)
        rows, held = gate_rows(own, got, got_far, keep, hidden_near, hidden_far, held)

        rows_far = swap(rows, "narrow", far)
        rows_near = swap(rows, "narrow", near)
        total, held = backward(
            index, [rows, rows_near], held, pair, far, True, None, 1, "back_own_near"
        )
        total, rows_far = lax.optimization_barrier((total, rows_far))
        rows_diagonal = swap(rows_far, "narrow", near)
        pieces = backward(
            index, [rows_far, rows_diagonal], held, pair, diagonal, False, total, wide, "back_far_diagonal"
        )
        back_normed, inner = pieces[0][:, :width], pieces[0][:, width : width + 1]
        for k in range(1, wide):
            got = swap(pieces[k], "wide", k)
            back_normed = back_normed + got[:, :width].astype(F32)
            inner = inner + joined(got[:, width:])
        return back_normed, inner

    def on_device(tokens, signs, magnitude, target, norm_gain, gate_weight, up_weight, down_weight):
        width, hidden = gate_weight.shape
        features = width * narrow
        weights = (gate_weight, up_weight, down_weight)
        square = narrow == (near | far) + 1 and hidden % (narrow * LANES) == 0 and wide & (wide - 1) == 0

        delta, latent, squares, gain, own_target = latents(
            tokens, signs, magnitude, norm_gain.reshape(1, -1), target
        )
        if square:
            squares = squares + sum(swap(squares, "narrow", k) for k in range(1, narrow))
        else:
            squares = lax.psum(squares, "narrow")
        scale = lax.rsqrt(squares / features + EPS)
        unit = latent * scale
        normed = (unit * gain).astype(BF16)
        if square:
            back_normed, inner = by_swaps(normed, target, own_target, *weights)
            scaled = back_normed * gain
        else:
            scaled = by_collectives(normed, target, *weights) * gain
            inner = lax.psum(jnp.sum(scaled * unit, axis=1, keepdims=True), "narrow")
        back_latent = scale * (scaled - unit * (inner / features))
        return delta + ASCENT * (own_target.astype(F32) + back_latent)

    rows = P(("groups", "wide"), "narrow")
    in_specs = (rows, rows, rows, rows, P("narrow"), P("narrow", "wide"), P("narrow", "wide"), P("wide", "narrow"))
    return jax.shard_map(on_device, mesh=mesh, in_specs=in_specs, out_specs=rows, check_vma=False)
```

time: 86.5 us -> 79.8 us (0.923)
  Pallas kernels: 47.5 us -> 42.4 us
  waiting for transfers between devices: 9.86 us -> 14.1 us
  other arithmetic: 3.89 us -> 1.27 us
  starting transfers between devices: 23.6 us -> 21.7 us
  local copies, waits for them, and re-layouts: 1.26 us -> 0 us
    pallas_call x7 -> x8, Pallas kernels: 47.5 us -> 42.4 us  [the longest x3 15.6 us: gate_and_up(): pl.pallas_call(kernel, in_specs=[SMEM] + [VMEM] * (len(blocks) + 1) + [HB...]
    ppermute x20, waiting for transfers between devices: 9.86 us -> 14.1 us  [swap(): return lax.ppermute(x, axis, [(i, i ^ k) for i in range(mesh.shape[axis])])]
    ppermute x20, starting transfers between devices: 23.6 us -> 21.7 us  [swap(): return lax.ppermute(x, axis, [(i, i ^ k) for i in range(mesh.shape[axis])])]
    reduce_sum x2 -> x0, other arithmetic: 1.48 us -> none  [the longest x1 1.15 us: on_device(): squares = jnp.sum(latent * latent, axis=1, keepdims=True)]
    convert_element_type x3 -> x2, other arithmetic: 1.16 us -> 0.13 us  [the longest x1 0.09 us: on_device(): normed = (unit * gain).astype(BF16)]
    unnamed x12 -> x0, local copies, waits for them, and re-layouts: 0.87 us -> none
  transfers between devices with their start and end apart: 20 -> 20, of which waited for: 7 -> 11; matrix products, arithmetic and copies ran while one was open for 1% -> 0% of each run, Pallas kernels for 44% -> 43%
where the time goes in v3:
time: 79.8 us; the launch traced here: 79.6 us
  Pallas kernels  42.4 us (53%)
  starting transfers between devices  21.7 us (27%)
  waiting for transfers between devices  14.1 us (18%)
  other arithmetic  1.27 us (2%)
    ppermute x20, starting transfers between devices, swap(): return lax.ppermute(x, axis, [(i, i ^ k) for i in range(mesh.shape[axis])])  21.7 us
    pallas_call x3, Pallas kernels, gate_and_up(): pl.pallas_call(kernel, in_specs=[SMEM] + [VMEM] * (len(blocks) + 1) + [HB...  15.6 us
    pallas_call x2, Pallas kernels, backward(): pl.pallas_call(kernel, in_specs=[SMEM] + [VMEM] * (len(rows) + 1 + len(ex...  14.8 us
    ppermute x20, waiting for transfers between devices, swap(): return lax.ppermute(x, axis, [(i, i ^ k) for i in range(mesh.shape[axis])])  14.1 us
    pallas_call x1, Pallas kernels, hidden_gradient(): pl.pallas_call(kernel, in_specs=[SMEM] + [VMEM] * len(blocks) + [HBM] * (...  10.4 us
  transfers between devices with their start and end apart: 20, of which 11 were waited for; matrix products, arithmetic and copies ran while one was open for 0% of the time, Pallas kernels for 43%

profile of v3, /device:TPU:0, one launch (start us, length us, event | category | flops | bytes accessed | tf_op | source)
XLA Modules:
  0.0 79.6 jit_solution(7517244683661633982)
XLA Ops:
  0.0 3.0 %collective-permute-start.3 = (bf16[16,2048]{1,0:T(8,128)(2,1)}, bf16[16,2048]{1,0:T(8,128)(2,1)S(1)}, u32[]{:S(2)}, u32[]{:S(2)}) collective-permute-start(bf16[16,2048]{1,0:T(8,128)(2,1)} %refs_4_.4), channel_id=1, source_target_pairs={{0,4},{4,0},{8,12},{12,8},{1,5},{5,1},{9,13},{13,9},{2,6},{6,2},{1... | collective-permute-start | bytes 196616 | tf_op jit(solution)/shard_map/ppermute | solution.py:344
  3.0 2.5 %collective-permute-start.5 = (bf16[16,2048]{1,0:T(8,128)(2,1)}, bf16[16,2048]{1,0:T(8,128)(2,1)S(1)}, u32[]{:S(2)}, u32[]{:S(2)}) collective-permute-start(bf16[16,2048]{1,0:T(8,128)(2,1)} %refs_4_.4), channel_id=1, source_target_pairs={{0,12},{4,8},{8,4},{12,0},{1,13},{5,9},{9,5},{13,1},{2,14},{6,10},... | collective-permute-start | bytes 196616 | tf_op jit(solution)/shard_map/ppermute | solution.py:344
  5.5 0.1 collective-permute-start.4
  5.6 1.2 %latents.1 = (f32[16,2048]{1,0:T(8,128)S(1)}, f32[16,2048]{1,0:T(8,128)S(1)}, f32[16,1]{1,0:T(8,128)S(1)}, f32[1,2048]{1,0:T(1,128)S(1)}, bf16[16,2048]{1,0:T(8,128)(2,1)S(1)}) custom-call(bf16[16,2048]{1,0:T(8,128)(2,1)} %refs_0_.1, s32[16,2048]{1,0:T(8,128)} %refs_1_.1, f32[16,2048]{1,0:T(8,128)} %refs_2_.1, f32[1,2048]{1,0:T(1,128)} %bitcast.5, ...), custom_call_target="tpu_custom_call" | custom-call | flops 262144 | bytes 589824 | tf_op jit(solution)/shard_map/latents/pallas_call | solution.py:265
  6.8 0.4 collective-permute-start.2
  7.2 1.2 %collective-permute-start.1 = (f32[16,1]{1,0:T(8,128)S(1)}, f32[16,1]{1,0:T(8,128)S(1)}, u32[]{:S(2)}, u32[]{:S(2)}) collective-permute-start(f32[16,1]{1,0:T(8,128)S(1)} %get-tuple-element.44), channel_id=1, source_target_pairs={{0,2},{1,3},{2,0},{3,1},{4,6},{5,7},{6,4},{7,5},{8,10},{9,11},{10,... | collective-permute-start | bytes 200 | tf_op jit(solution)/shard_map/ppermute | solution.py:344
  8.4 1.5 %collective-permute-done.2 = f32[16,1]{1,0:T(8,128)S(1)} collective-permute-done((f32[16,1]{1,0:T(8,128)S(1)}, f32[16,1]{1,0:T(8,128)S(1)}, u32[]{:S(2)}, u32[]{:S(2)}) %collective-permute-start.2) | collective-permute-done | bytes 96 | tf_op jit(solution)/shard_map/ppermute | solution.py:344
  10.0 0.2 collective-permute-start
  10.1 0.7 collective-permute-done.1
  10.9 0.3 collective-permute-done
  11.2 0.1 rsqrt_reduce_fusion
  11.3 0.1 multiply_convert_fusion.refs_0_
  11.4 3.0 %collective-permute-start.8 = (bf16[16,2048]{1,0:T(8,128)(2,1)S(1)}, bf16[16,2048]{1,0:T(8,128)(2,1)S(1)}, u32[]{:S(2)}, u32[]{:S(2)}) collective-permute-start(bf16[16,2048]{1,0:T(8,128)(2,1)S(1)} %multiply_convert_fusion.refs_0_), channel_id=1, source_target_pairs={{0,12},{4,8},{8,4},{12,0},{1,13},{5,9},{9,5},{13,1},{2,14},{6,10},... | collective-permute-start | bytes 196616 | tf_op jit(solution)/shard_map/ppermute | solution.py:344
  14.4 0.3 collective-permute-start.7
  14.7 0.0 collective-permute-done.3.refs_1_
  14.7 1.1 %collective-permute-start.6 = (bf16[16,2048]{1,0:T(8,128)(2,1)S(1)}, bf16[16,2048]{1,0:T(8,128)(2,1)S(1)}, u32[]{:S(2)}, u32[]{:S(2)}) collective-permute-start(bf16[16,2048]{1,0:T(8,128)(2,1)S(1)} %multiply_convert_fusion.refs_0_), channel_id=1, source_target_pairs={{0,4},{4,0},{8,12},{12,8},{1,5},{5,1},{9,13},{13,9},{2,6},{6,2},{1... | collective-permute-start | bytes 196616 | tf_op jit(solution)/shard_map/ppermute | solution.py:344
  15.8 0.0 collective-permute-done.5.refs_3_
  15.8 10.4 %back_hidden.1 = (f32[64,2560]{1,0:T(8,128)S(1)}, f32[64,2560]{1,0:T(8,128)S(1)}, bf16[2,2048,1280]{2,1,0:T(8,128)(2,1)S(1)}) custom-call(s32[1]{0:T(128)} %bitcast.1.index_ref, bf16[16,2048]{1,0:T(8,128)(2,1)S(1)} %get-tuple-element.43.refs_0_, bf16[16,2048]{1,0:T(8,128)(2,1)S(1)} %collective-permute-done.3.refs_1_, ...), custom_call_target="tpu_custom_call" | custom-call | flops 1342177280 | bytes 20971520 | tf_op jit(solution)/shard_map/back_hidden/pallas_call | solution.py:107
  26.3 0.0 collective-permute-done.7.refs_2_
  26.3 0.1 collective-permute-start.9
  26.4 4.2 %gate_up_diagonal.1 = (f32[64,2560]{1,0:T(8,128)S(1)}, bf16[2,2048,1280]{2,1,0:T(8,128)(2,1)S(1)}) custom-call(s32[1]{0:T(128)} %bitcast.1.index_ref, bf16[16,2048]{1,0:T(8,128)(2,1)S(1)} %multiply_convert_fusion.refs_0_, bf16[16,2048]{1,0:T(8,128)(2,1)S(1)} %collective-permute-done.6.refs_1_, bf16[16,2048]{1,0:T(8,128)(2,1)S(1)} %collective-permute-done.7.refs_2_, ...), custom_call_target="tpu_custom_call" | custom-call | flops 671088640 | bytes 10485760 | tf_op jit(solution)/shard_map/gate_up_diagonal/pallas_call | solution.py:160
  30.5 0.0 collective-permute-done.9.hidden_near_ref
  30.5 0.6 collective-permute-start.10
  31.1 1.6 %collective-permute-start.11 = (bf16[64,1280]{1,0:T(8,128)(2,1)S(1)}, bf16[64,1280]{1,0:T(8,128)(2,1)S(1)}, u32[]{:S(2)}, u32[]{:S(2)}) collective-permute-start(bf16[64,1280]{1,0:T(8,128)(2,1)S(1)} %add_convert_fusion.1), channel_id=1, source_target_pairs={{0,2},{1,3},{2,0},{3,1},{4,6},{5,7},{6,4},{7,5},{8,10},{9,11},{10,... | collective-permute-start | bytes 491528 | tf_op jit(solution)/shard_map/ppermute | solution.py:344
  32.7 4.2 %gate_up_far.1 = (f32[64,2560]{1,0:T(8,128)S(1)}, bf16[2,2048,1280]{2,1,0:T(8,128)(2,1)S(1)}) custom-call(s32[1]{0:T(128)} %bitcast.1.index_ref, bf16[16,2048]{1,0:T(8,128)(2,1)S(1)} %multiply_convert_fusion.refs_0_, bf16[16,2048]{1,0:T(8,128)(2,1)S(1)} %collective-permute-done.6.refs_1_, bf16[16,2048]{1,0:T(8,128)(2,1)S(1)} %collective-permute-done.7.refs_2_, ...), custom_call_target="tpu_custom_call" | custom-call | flops 671088640 | bytes 10485760 | tf_op jit(solution)/shard_map/gate_up_far/pallas_call | solution.py:160
  37.0 0.4 collective-permute-done.11.hidden_far_ref
  37.3 0.0 collective-permute-done.10
  37.3 0.1 add_convert_fusion.refs_7_
  37.4 1.6 %collective-permute-start.12 = (bf16[64,2560]{1,0:T(8,128)(2,1)S(1)}, bf16[64,2560]{1,0:T(8,128)(2,1)S(1)}, u32[]{:S(2)}, u32[]{:S(2)}) collective-permute-start(bf16[64,2560]{1,0:T(8,128)(2,1)S(1)} %add_convert_fusion.refs_7_), channel_id=1, source_target_pairs={{0,2},{1,3},{2,0},{3,1},{4,6},{5,7},{6,4},{7,5},{8,10},{9,11},{10,... | collective-permute-start | bytes 983048 | tf_op jit(solution)/shard_map/ppermute | solution.py:344
  39.0 7.3 %gate_up_near_own.1 = (f32[64,2560]{1,0:T(8,128)S(1)}, f32[64,2560]{1,0:T(8,128)S(1)}, bf16[4,2048,1280]{2,1,0:T(8,128)(2,1)S(1)}) custom-call(s32[1]{0:T(128)} %bitcast.1.index_ref, bf16[16,2048]{1,0:T(8,128)(2,1)S(1)} %multiply_convert_fusion.refs_0_, bf16[16,2048]{1,0:T(8,128)(2,1)S(1)} %collective-permute-done.6.refs_1_, ...), custom_call_target="tpu_custom_call" | custom-call | flops 1342177280 | bytes 20971520 | tf_op jit(solution)/shard_map/gate_up_near_own/pallas_call | solution.py:160
  46.3 0.1 collective-permute-done.12.far_ref
  46.4 0.0 collective-permute-start.13
  46.4 2.1 %collective-permute-done.13.near_ref = f32[64,2560]{1,0:T(8,128)S(1)} collective-permute-done((f32[64,2560]{1,0:T(8,128)S(1)}, f32[64,2560]{1,0:T(8,128)S(1)}, u32[]{:S(2)}, u32[]{:S(2)}) %collective-permute-start.13) | collective-permute-done | bytes 655392 | tf_op jit(solution)/shard_map/ppermute | solution.py:344
  48.5 0.4 gate.1
  48.9 0.2 collective-permute-start.14
  49.1 1.4 %collective-permute-start.15 = (bf16[64,2688]{1,0:T(8,128)(2,1)S(1)}, bf16[64,2688]{1,0:T(8,128)(2,1)S(1)}, u32[]{:S(2)}, u32[]{:S(2)}) collective-permute-start(bf16[64,2688]{1,0:T(8,128)(2,1)S(1)} %get-tuple-element.69.refs_0_), channel_id=1, source_target_pairs={{0,2},{1,3},{2,0},{3,1},{4,6},{5,7},{6,4},{7,5},{8,10},{9,11},{10,... | collective-permute-start | bytes 1032200 | tf_op jit(solution)/shard_map/ppermute | solution.py:344
  50.5 0.1 collective-permute-done.14.refs_1_
  50.6 7.0 %back_own_near.1 = (f32[64,2176]{1,0:T(8,128)S(1)}, bf16[2,2048,1280]{2,1,0:T(8,128)(2,1)S(1)}) custom-call(s32[1]{0:T(128)} %bitcast.1.index_ref, bf16[64,2688]{1,0:T(8,128)(2,1)S(1)} %get-tuple-element.69.refs_0_, bf16[64,2688]{1,0:T(8,128)(2,1)S(1)} %collective-permute-done.14.refs_1_, bf16[4,2048,1280]{2,1,0:T(8,128)(2,1)S(1)} %get-tuple-element.70.refs_2_, ...), custom_call_target="tpu_custom_call" | custom-call | flops 1342177280 | bytes 20971520 | tf_op jit(solution)/shard_map/back_own_near/pallas_call | solution.py:229
  57.6 1.9 %collective-permute-done.15.refs_0_ = bf16[64,2688]{1,0:T(8,128)(2,1)S(1)} collective-permute-done((bf16[64,2688]{1,0:T(8,128)(2,1)S(1)}, bf16[64,2688]{1,0:T(8,128)(2,1)S(1)}, u32[]{:S(2)}, u32[]{:S(2)}) %collective-permute-start.15) | collective-permute-done | bytes 344096 | tf_op jit(solution)/shard_map/ppermute | solution.py:344
  59.4 1.6 %collective-permute-done.16.refs_1_ = bf16[64,2688]{1,0:T(8,128)(2,1)S(1)} collective-permute-done((bf16[64,2688]{1,0:T(8,128)(2,1)S(1)}, bf16[64,2688]{1,0:T(8,128)(2,1)S(1)}, u32[]{:S(2)}, u32[]{:S(2)}) %collective-permute-start.16) | collective-permute-done | bytes 344096 | tf_op jit(solution)/shard_map/ppermute | solution.py:344
  61.1 7.8 %back_far_diagonal.1 = (f32[16,2176]{1,0:T(8,128)S(1)}, bf16[16,2176]{1,0:T(8,128)(2,1)S(1)}, bf16[16,2176]{1,0:T(8,128)(2,1)S(1)}, bf16[16,2176]{1,0:T(8,128)(2,1)S(1)}) custom-call(s32[1]{0:T(128)} %bitcast.1.index_ref, bf16[64,2688]{1,0:T(8,128)(2,1)S(1)} %collective-permute-done.15.refs_0_, bf16[64,2688]{1,0:T(8,128)(2,1)S(1)} %collective-permute-done.16.refs_1_, ...), custom_call_target="tpu_custom_call" | custom-call | flops 1342177280 | bytes 20971520 | tf_op jit(solution)/shard_map/back_far_diagonal/pallas_call | solution.py:229
  68.9 1.0 %collective-permute-start.17 = (bf16[16,2176]{1,0:T(8,128)(2,1)S(1)}, bf16[16,2176]{1,0:T(8,128)(2,1)S(1)}, u32[]{:S(2)}, u32[]{:S(2)}) collective-permute-start(bf16[16,2176]{1,0:T(8,128)(2,1)S(1)} %get-tuple-element.76), channel_id=1, source_target_pairs={{0,4},{4,0},{8,12},{12,8},{1,5},{5,1},{9,13},{13,9},{2,6},{6,2},{1... | collective-permute-start | bytes 208904 | tf_op jit(solution)/shard_map/ppermute | solution.py:344
  69.8 2.6 %collective-permute-start.18 = (bf16[16,2176]{1,0:T(8,128)(2,1)S(1)}, bf16[16,2176]{1,0:T(8,128)(2,1)S(1)}, u32[]{:S(2)}, u32[]{:S(2)}) collective-permute-start(bf16[16,2176]{1,0:T(8,128)(2,1)S(1)} %get-tuple-element.77), channel_id=1, source_target_pairs={{0,8},{4,12},{8,0},{12,4},{1,9},{5,13},{9,1},{13,5},{2,10},{6,14},... | collective-permute-start | bytes 208904 | tf_op jit(solution)/shard_map/ppermute | solution.py:344
  72.4 0.9 %collective-permute-start.19 = (bf16[16,2176]{1,0:T(8,128)(2,1)S(1)}, bf16[16,2176]{1,0:T(8,128)(2,1)S(1)}, u32[]{:S(2)}, u32[]{:S(2)}) collective-permute-start(bf16[16,2176]{1,0:T(8,128)(2,1)S(1)} %get-tuple-element.78), channel_id=1, source_target_pairs={{0,12},{4,8},{8,4},{12,0},{1,13},{5,9},{9,5},{13,1},{2,14},{6,10},... | collective-permute-start | bytes 208904 | tf_op jit(solution)/shard_map/ppermute | solution.py:344
  73.3 4.3 %collective-permute-done.18 = bf16[16,2176]{1,0:T(8,128)(2,1)S(1)} collective-permute-done((bf16[16,2176]{1,0:T(8,128)(2,1)S(1)}, bf16[16,2176]{1,0:T(8,128)(2,1)S(1)}, u32[]{:S(2)}, u32[]{:S(2)}) %collective-permute-start.18) | collective-permute-done | bytes 69664 | tf_op jit(solution)/shard_map/ppermute | solution.py:344
  77.6 1.0 %collective-permute-done.19 = bf16[16,2176]{1,0:T(8,128)(2,1)S(1)} collective-permute-done((bf16[16,2176]{1,0:T(8,128)(2,1)S(1)}, bf16[16,2176]{1,0:T(8,128)(2,1)S(1)}, u32[]{:S(2)}, u32[]{:S(2)}) %collective-permute-start.19) | collective-permute-done | bytes 69664 | tf_op jit(solution)/shard_map/ppermute | solution.py:344
  78.7 0.2 multiply_reduce_fusion
  78.8 0.8 multiply_add_fusion
  (6 shorter events, 0.1 us)
Async XLA Ops:
  0.0 14.7 %collective-permute-start.3 = (bf16[16,2048]{1,0:T(8,128)(2,1)}, bf16[16,2048]{1,0:T(8,128)(2,1)S(1)}, u32[]{:S(2)}, u32[]{:S(2)}) collective-permute-start(bf16[16,2048]{1,0:T(8,128)(2,1)} %refs_4_.4), channel_id=1, source_target_pairs={{0,4},{4,0},{8,12},{12,8},{1,5},{5,1},{9,13},{13,9},{2,6},{6,2},{1... | collective-permute-start | bytes 196616 | tf_op jit(solution)/shard_map/ppermute | solution.py:344
  3.0 12.8 %collective-permute-start.5 = (bf16[16,2048]{1,0:T(8,128)(2,1)}, bf16[16,2048]{1,0:T(8,128)(2,1)S(1)}, u32[]{:S(2)}, u32[]{:S(2)}) collective-permute-start(bf16[16,2048]{1,0:T(8,128)(2,1)} %refs_4_.4), channel_id=1, source_target_pairs={{0,12},{4,8},{8,4},{12,0},{1,13},{5,9},{9,5},{13,1},{2,14},{6,10},... | collective-permute-start | bytes 196616 | tf_op jit(solution)/shard_map/ppermute | solution.py:344
  5.5 10.3 %collective-permute-start.4 = (bf16[16,2048]{1,0:T(8,128)(2,1)}, bf16[16,2048]{1,0:T(8,128)(2,1)S(1)}, u32[]{:S(2)}, u32[]{:S(2)}) collective-permute-start(bf16[16,2048]{1,0:T(8,128)(2,1)} %refs_4_.4), channel_id=1, source_target_pairs={{0,8},{4,12},{8,0},{12,4},{1,9},{5,13},{9,1},{13,5},{2,10},{6,14},... | collective-permute-start | bytes 196616 | tf_op jit(solution)/shard_map/ppermute | solution.py:344
  6.8 3.2 %collective-permute-start.2 = (f32[16,1]{1,0:T(8,128)S(1)}, f32[16,1]{1,0:T(8,128)S(1)}, u32[]{:S(2)}, u32[]{:S(2)}) collective-permute-start(f32[16,1]{1,0:T(8,128)S(1)} %get-tuple-element.44), channel_id=1, source_target_pairs={{0,3},{1,2},{2,1},{3,0},{4,7},{5,6},{6,5},{7,4},{8,11},{9,10},{10,... | collective-permute-start | bytes 200 | tf_op jit(solution)/shard_map/ppermute | solution.py:344
  7.2 3.7 %collective-permute-start.1 = (f32[16,1]{1,0:T(8,128)S(1)}, f32[16,1]{1,0:T(8,128)S(1)}, u32[]{:S(2)}, u32[]{:S(2)}) collective-permute-start(f32[16,1]{1,0:T(8,128)S(1)} %get-tuple-element.44), channel_id=1, source_target_pairs={{0,2},{1,3},{2,0},{3,1},{4,6},{5,7},{6,4},{7,5},{8,10},{9,11},{10,... | collective-permute-start | bytes 200 | tf_op jit(solution)/shard_map/ppermute | solution.py:344
  10.0 1.2 %collective-permute-start = (f32[16,1]{1,0:T(8,128)S(1)}, f32[16,1]{1,0:T(8,128)S(1)}, u32[]{:S(2)}, u32[]{:S(2)}) collective-permute-start(f32[16,1]{1,0:T(8,128)S(1)} %get-tuple-element.44), channel_id=1, source_target_pairs={{0,1},{1,0},{2,3},{3,2},{4,5},{5,4},{6,7},{7,6},{8,9},{9,8},{10,11... | collective-permute-start | bytes 200 | tf_op jit(solution)/shard_map/ppermute | solution.py:344
  11.4 14.9 %collective-permute-start.8 = (bf16[16,2048]{1,0:T(8,128)(2,1)S(1)}, bf16[16,2048]{1,0:T(8,128)(2,1)S(1)}, u32[]{:S(2)}, u32[]{:S(2)}) collective-permute-start(bf16[16,2048]{1,0:T(8,128)(2,1)S(1)} %multiply_convert_fusion.refs_0_), channel_id=1, source_target_pairs={{0,12},{4,8},{8,4},{12,0},{1,13},{5,9},{9,5},{13,1},{2,14},{6,10},... | collective-permute-start | bytes 196616 | tf_op jit(solution)/shard_map/ppermute | solution.py:344
  14.4 11.9 %collective-permute-start.7 = (bf16[16,2048]{1,0:T(8,128)(2,1)S(1)}, bf16[16,2048]{1,0:T(8,128)(2,1)S(1)}, u32[]{:S(2)}, u32[]{:S(2)}) collective-permute-start(bf16[16,2048]{1,0:T(8,128)(2,1)S(1)} %multiply_convert_fusion.refs_0_), channel_id=1, source_target_pairs={{0,8},{4,12},{8,0},{12,4},{1,9},{5,13},{9,1},{13,5},{2,10},{6,14},... | collective-permute-start | bytes 196616 | tf_op jit(solution)/shard_map/ppermute | solution.py:344
  14.7 11.6 %collective-permute-start.6 = (bf16[16,2048]{1,0:T(8,128)(2,1)S(1)}, bf16[16,2048]{1,0:T(8,128)(2,1)S(1)}, u32[]{:S(2)}, u32[]{:S(2)}) collective-permute-start(bf16[16,2048]{1,0:T(8,128)(2,1)S(1)} %multiply_convert_fusion.refs_0_), channel_id=1, source_target_pairs={{0,4},{4,0},{8,12},{12,8},{1,5},{5,1},{9,13},{13,9},{2,6},{6,2},{1... | collective-permute-start | bytes 196616 | tf_op jit(solution)/shard_map/ppermute | solution.py:344
  26.3 4.2 %collective-permute-start.9 = (f32[64,2560]{1,0:T(8,128)S(1)}, f32[64,2560]{1,0:T(8,128)S(1)}, u32[]{:S(2)}, u32[]{:S(2)}) collective-permute-start(f32[64,2560]{1,0:T(8,128)S(1)} %get-tuple-element.53.refs_7_), channel_id=1, source_target_pairs={{0,1},{1,0},{2,3},{3,2},{4,5},{5,4},{6,7},{7,6},{8,9},{9,8},{10,11... | collective-permute-start | bytes 1966088 | tf_op jit(solution)/shard_map/ppermute | solution.py:344
  30.5 6.8 %collective-permute-start.10 = (f32[64,2560]{1,0:T(8,128)S(1)}, f32[64,2560]{1,0:T(8,128)S(1)}, u32[]{:S(2)}, u32[]{:S(2)}) collective-permute-start(f32[64,2560]{1,0:T(8,128)S(1)} %get-tuple-element.56.refs_7_), channel_id=1, source_target_pairs={{0,1},{1,0},{2,3},{3,2},{4,5},{5,4},{6,7},{7,6},{8,9},{9,8},{10,11... | collective-permute-start | bytes 1966088 | tf_op jit(solution)/shard_map/ppermute | solution.py:344
  31.1 6.2 %collective-permute-start.11 = (bf16[64,1280]{1,0:T(8,128)(2,1)S(1)}, bf16[64,1280]{1,0:T(8,128)(2,1)S(1)}, u32[]{:S(2)}, u32[]{:S(2)}) collective-permute-start(bf16[64,1280]{1,0:T(8,128)(2,1)S(1)} %add_convert_fusion.1), channel_id=1, source_target_pairs={{0,2},{1,3},{2,0},{3,1},{4,6},{5,7},{6,4},{7,5},{8,10},{9,11},{10,... | collective-permute-start | bytes 491528 | tf_op jit(solution)/shard_map/ppermute | solution.py:344
  37.4 9.0 %collective-permute-start.12 = (bf16[64,2560]{1,0:T(8,128)(2,1)S(1)}, bf16[64,2560]{1,0:T(8,128)(2,1)S(1)}, u32[]{:S(2)}, u32[]{:S(2)}) collective-permute-start(bf16[64,2560]{1,0:T(8,128)(2,1)S(1)} %add_convert_fusion.refs_7_), channel_id=1, source_target_pairs={{0,2},{1,3},{2,0},{3,1},{4,6},{5,7},{6,4},{7,5},{8,10},{9,11},{10,... | collective-permute-start | bytes 983048 | tf_op jit(solution)/shard_map/ppermute | solution.py:344
  46.4 2.1 %collective-permute-start.13 = (f32[64,2560]{1,0:T(8,128)S(1)}, f32[64,2560]{1,0:T(8,128)S(1)}, u32[]{:S(2)}, u32[]{:S(2)}) collective-permute-start(f32[64,2560]{1,0:T(8,128)S(1)} %get-tuple-element.65), channel_id=1, source_target_pairs={{0,1},{1,0},{2,3},{3,2},{4,5},{5,4},{6,7},{7,6},{8,9},{9,8},{10,11... | collective-permute-start | bytes 1966088 | tf_op jit(solution)/shard_map/ppermute | solution.py:344
  48.9 1.7 %collective-permute-start.14 = (bf16[64,2688]{1,0:T(8,128)(2,1)S(1)}, bf16[64,2688]{1,0:T(8,128)(2,1)S(1)}, u32[]{:S(2)}, u32[]{:S(2)}) collective-permute-start(bf16[64,2688]{1,0:T(8,128)(2,1)S(1)} %get-tuple-element.69.refs_0_), channel_id=1, source_target_pairs={{0,1},{1,0},{2,3},{3,2},{4,5},{5,4},{6,7},{7,6},{8,9},{9,8},{10,11... | collective-permute-start | bytes 1032200 | tf_op jit(solution)/shard_map/ppermute | solution.py:344
  49.1 10.3 %collective-permute-start.15 = (bf16[64,2688]{1,0:T(8,128)(2,1)S(1)}, bf16[64,2688]{1,0:T(8,128)(2,1)S(1)}, u32[]{:S(2)}, u32[]{:S(2)}) collective-permute-start(bf16[64,2688]{1,0:T(8,128)(2,1)S(1)} %get-tuple-element.69.refs_0_), channel_id=1, source_target_pairs={{0,2},{1,3},{2,0},{3,1},{4,6},{5,7},{6,4},{7,5},{8,10},{9,11},{10,... | collective-permute-start | bytes 1032200 | tf_op jit(solution)/shard_map/ppermute | solution.py:344
  59.4 1.7 %collective-permute-start.16 = (bf16[64,2688]{1,0:T(8,128)(2,1)S(1)}, bf16[64,2688]{1,0:T(8,128)(2,1)S(1)}, u32[]{:S(2)}, u32[]{:S(2)}) collective-permute-start(bf16[64,2688]{1,0:T(8,128)(2,1)S(1)} %collective-permute-done.15.refs_0_), channel_id=1, source_target_pairs={{0,1},{1,0},{2,3},{3,2},{4,5},{5,4},{6,7},{7,6},{8,9},{9,8},{10,11... | collective-permute-start | bytes 1032200 | tf_op jit(solution)/shard_map/ppermute | solution.py:344
  68.9 4.5 %collective-permute-start.17 = (bf16[16,2176]{1,0:T(8,128)(2,1)S(1)}, bf16[16,2176]{1,0:T(8,128)(2,1)S(1)}, u32[]{:S(2)}, u32[]{:S(2)}) collective-permute-start(bf16[16,2176]{1,0:T(8,128)(2,1)S(1)} %get-tuple-element.76), channel_id=1, source_target_pairs={{0,4},{4,0},{8,12},{12,8},{1,5},{5,1},{9,13},{13,9},{2,6},{6,2},{1... | collective-permute-start | bytes 208904 | tf_op jit(solution)/shard_map/ppermute | solution.py:344
  69.8 7.8 %collective-permute-start.18 = (bf16[16,2176]{1,0:T(8,128)(2,1)S(1)}, bf16[16,2176]{1,0:T(8,128)(2,1)S(1)}, u32[]{:S(2)}, u32[]{:S(2)}) collective-permute-start(bf16[16,2176]{1,0:T(8,128)(2,1)S(1)} %get-tuple-element.77), channel_id=1, source_target_pairs={{0,8},{4,12},{8,0},{12,4},{1,9},{5,13},{9,1},{13,5},{2,10},{6,14},... | collective-permute-start | bytes 208904 | tf_op jit(solution)/shard_map/ppermute | solution.py:344
  72.4 6.2 %collective-permute-start.19 = (bf16[16,2176]{1,0:T(8,128)(2,1)S(1)}, bf16[16,2176]{1,0:T(8,128)(2,1)S(1)}, u32[]{:S(2)}, u32[]{:S(2)}) collective-permute-start(bf16[16,2176]{1,0:T(8,128)(2,1)S(1)} %get-tuple-element.78), channel_id=1, source_target_pairs={{0,12},{4,8},{8,4},{12,0},{1,13},{5,9},{9,5},{13,1},{2,14},{6,10},... | collective-permute-start | bytes 208904 | tf_op jit(solution)/shard_map/ppermute | solution.py:344

commit v4 on v3

--- a/solution.py
+++ b/solution.py
@@ -9,7 +9,6 @@
 ASCENT = 0.5
 LANES = 128
 STEP = 512
-FIRST_FLYING = 8
 
 NN = (((1,), (0,)), ((), ()))
 NT = (((1,), (1,)), ((), ()))
@@ -71,120 +70,163 @@
     return copies
 
 
-def hidden_gradient(index, blocks, down_weight, pair, pick, picks, share):
+def rows_ahead(index, down_weight, picks, share):
+    width = down_weight.shape[1]
+
+    def kernel(index_ref, down_ref, out_ref, sems):
+        copies = []
+        for r, pick in enumerate(picks):
+            begin = pl.multiple_of((index_ref[0] ^ pick) * share, LANES)
+            source, target = down_ref.at[pl.ds(begin, share), :], out_ref.at[pl.ds(r * share, share), :]
+            copies.append(pltpu.make_async_copy(source, target, sems.at[r]))
+        for copy in copies:
+            copy.start()
+        for copy in copies:
+            copy.wait()
+
+    return pl.pallas_call(
+        kernel,
+        in_specs=[SMEM, HBM],
+        out_specs=VMEM,
+        out_shape=pltpu.VMEM((len(picks) * share, width), down_weight.dtype),
+        scratch_shapes=[pltpu.SemaphoreType.DMA((len(picks),))],
+        compiler_params=params(8),
+        cost_estimate=cost(8, width, len(picks) * share),
+        name="rows_ahead",
+    )(index, *in_hbm([down_weight]))
+
+
+def hidden_gradient(index, blocks, held, down_weight, pair, pick, picks, share):
     size, width = blocks[0].shape
     tokens = size * len(blocks)
-    parts = [(r, at, n) for r in range(len(picks)) for at, n in steps(share)]
-    half = len(picks) // 2
+    first = held.shape[0] // share
+    parts = [(r, at, n) for r in range(first, len(picks)) for at, n in steps(share)]
+    n = parts[0][2]
+    half = len(picks) // 2 * share
 
     def kernel(index_ref, *refs):
         block_refs, refs = refs[: len(blocks)], refs[len(blocks) :]
-        down_ref, refs = refs[0], refs[1:]
+        held_ref, down_ref, refs = refs[0], refs[1], refs[2:]
         pair_refs, refs = refs[: len(pair)], refs[len(pair) :]
-        out_refs, refs = refs[:2], refs[2:]
-        held_ref, rows_ref, down_parts, sems, pair_sems = refs
+        send_ref, keep_ref, next_ref, rows_ref, down_parts, sems, pair_sems = refs
         copies = []
-        for j, (r, at, n) in enumerate(parts):
+        for j, (r, at, _) in enumerate(parts):
             begin = pl.multiple_of((index_ref[0] ^ picks[r]) * share + at, LANES)
             copies.append(pltpu.make_async_copy(down_ref.at[pl.ds(begin, n), :], down_parts.at[j], sems.at[j]))
-        copies += bring(index_ref, pick, share, pair_refs, held_ref, 0, pair_sems)
-        for copy in copies[:FIRST_FLYING]:
+        later = bring(index_ref, pick, share, pair_refs, next_ref, 0, pair_sems)
+        for copy in copies + later:
             copy.start()
         for p, block in enumerate(block_refs):
             rows_ref[p * size : (p + 1) * size, :] = block[...]
-        for j, (r, at, n) in enumerate(parts):
+
+        @pl.loop(0, held.shape[0] // n)
+        def _(step):
+            here = pl.ds(pl.multiple_of(step * n, n), n)
+            send_ref[:, here] = dot(rows_ref[...], held_ref[here, :], NT).astype(BF16)
+
+        for j, (r, at, _) in enumerate(parts):
             copies[j].wait()
-            for copy in copies[j + FIRST_FLYING : j + FIRST_FLYING + 1]:
-                copy.start()
-            out_refs[r // half][:, pl.ds(r % half * share + at, n)] = dot(rows_ref[...], down_parts[j], NT)
-        for copy in copies[len(parts) + FIRST_FLYING :]:
-            copy.start()
-        for copy in copies[len(parts) :]:
+            here, part = r * share + at, dot(rows_ref[...], down_parts[j], NT)
+            if here < half:
+                send_ref[:, pl.ds(here, n)] = part.astype(BF16)
+            else:
+                keep_ref[:, pl.ds(here - half, n)] = part
+        for copy in later:
             copy.wait()
 
     count = len(steps(share))
-    total = len(picks) * share
-    return pl.pallas_call(
-        kernel,
-        in_specs=[SMEM] + [VMEM] * len(blocks) + [HBM] * (1 + len(pair)),
+    return pl.pallas_call(
+        kernel,
+        in_specs=[SMEM] + [VMEM] * (len(blocks) + 1) + [HBM] * (1 + len(pair)),
         out_specs=[VMEM] * 3,
-        out_shape=[jax.ShapeDtypeStruct((tokens, half * share), F32)] * 2
-        + [pltpu.VMEM((len(pair), width, share), BF16)],
+        out_shape=[
+            jax.ShapeDtypeStruct((tokens, half), BF16),
+            jax.ShapeDtypeStruct((tokens, half), F32),
+            pltpu.VMEM((len(pair), width, share), BF16),
+        ],
         scratch_shapes=[
             pltpu.VMEM((tokens, width), BF16),
-            pltpu.VMEM((len(parts), parts[0][2], width), BF16),
+            pltpu.VMEM((len(parts), n, width), BF16),
             pltpu.SemaphoreType.DMA((len(parts),)),
             pltpu.SemaphoreType.DMA((len(pair) * count,)),
         ],
-        compiler_params=params(26),
-        cost_estimate=cost(tokens, width, total),
+        compiler_params=params(22),
+        cost_estimate=cost(tokens, width, len(picks) * share),
         name="back_hidden",
-    )(index, *blocks, *in_hbm([down_weight, *pair]))
-
-
-def gate_and_up(index, blocks, held, pair, picks, both, after, name):
+    )(index, *blocks, in_vmem(held), *in_hbm([down_weight, *pair]))
+
+
+def gate_and_up(index, blocks, held, pair, picks, share, after, name, stays=True):
     size, width = blocks[0].shape
     tokens = size * len(blocks)
-    share = held.shape[2]
-    outs = 2 if both else 1
+    given = [] if held is None else [held]
+    use = held is None
+    outs = len(picks) if use else 1
     count = len(steps(share)) * len(pair)
 
     def kernel(index_ref, *refs):
         block_refs, refs = refs[: len(blocks)], refs[len(blocks) :]
-        held_ref, refs = refs[0], refs[1:]
+        held_refs, refs = refs[: len(given)], refs[len(given) :]
         pair_refs, refs = refs[: len(pair)], refs[len(pair) + len(after) :]
-        out_refs, (next_ref, rows_ref, sems) = refs[:outs], refs[outs:]
+        out_refs, (*next_ref, rows_ref, sems) = refs[:outs], refs[outs:]
         copies = []
         for k, pick in enumerate(picks):
-            copies += bring(index_ref, pick, share, pair_refs, next_ref, k * len(pair), sems, k * count)
+            copies += bring(index_ref, pick, share, pair_refs, next_ref[0], k * len(pair), sems, k * count)
         for copy in copies:
             copy.start()
         for p, block in enumerate(block_refs):
             rows_ref[p * size : (p + 1) * size, :] = block[...]
         n = steps(share)[0][1]
-
-        @pl.loop(0, share // n)
-        def _(step):
-            for i in range(len(pair)):
-                part = dot(rows_ref[...], held_ref[i, :, pl.ds(pl.multiple_of(step * n, n), n)], NN)
-                out_refs[0][:, pl.ds(pl.multiple_of(i * share + step * n, LANES), n)] = part
+        for held_ref, out in zip(held_refs, out_refs):
+
+            @pl.loop(0, share // n)
+            def _(step):
+                for i in range(len(pair)):
+                    part = dot(rows_ref[...], held_ref[i, :, pl.ds(pl.multiple_of(step * n, n), n)], NN)
+                    out[:, pl.ds(pl.multiple_of(i * share + step * n, LANES), n)] = part
 
         for j, copy in enumerate(copies):
             copy.wait()
-            if both and j < count:
-                at, n = steps(share)[j // len(pair)]
-                i = j % len(pair)
-                part = dot(rows_ref[...], next_ref[i, :, pl.ds(at, n)], NN)
-                out_refs[1][:, pl.ds(i * share + at, n)] = part
-
-    return pl.pallas_call(
-        kernel,
-        in_specs=[SMEM] + [VMEM] * (len(blocks) + 1) + [HBM] * len(pair) + [ANY] * len(after),
-        out_specs=[VMEM] * (outs + 1),
-        out_shape=[jax.ShapeDtypeStruct((tokens, len(pair) * share), F32)] * outs
-        + [pltpu.VMEM((len(pair) * len(picks), width, share), BF16)],
-        scratch_shapes=[pltpu.VMEM((tokens, width), BF16), pltpu.SemaphoreType.DMA((count * len(picks),))],
-        compiler_params=params(8),
+            if use:
+                k, (at, n), i = j // count, steps(share)[j % count // len(pair)], j % len(pair)
+                part = dot(rows_ref[...], next_ref[0][k * len(pair) + i, :, pl.ds(at, n)], NN)
+                out_refs[k][:, pl.ds(i * share + at, n)] = part.astype(out_refs[k].dtype)
+
+    brought = [pltpu.VMEM((len(pair) * len(picks), width, share), BF16)] if picks else []
+    more, scratch = (brought, []) if stays else ([], brought)
+    return pl.pallas_call(
+        kernel,
+        in_specs=[SMEM] + [VMEM] * (len(blocks) + len(given)) + [HBM] * len(pair) + [ANY] * len(after),
+        out_specs=[VMEM] * (outs + len(more)),
+        out_shape=[jax.ShapeDtypeStruct((tokens, len(pair) * share), BF16 if i else F32) for i in range(outs)] + more,
+        scratch_shapes=scratch
+        + [
+            pltpu.VMEM((tokens, width), BF16),
+            pltpu.SemaphoreType.DMA((max(1, count * len(picks)),)),
+        ],
+        compiler_params=params(8 if stays else 20),
         cost_estimate=cost(tokens, width, outs * len(pair) * share),
         name=name,
-    )(index, *blocks, in_vmem(held), *in_hbm(pair), *after)
-
-
-def backward(index, rows, held, pair, pick, stays, before, pieces, name):
+    )(index, *blocks, *[in_vmem(h) for h in given], *in_hbm(pair), *after)
+
+
+def backward(index, rows, held, pair, picks, before, pieces, name):
     tokens = rows[0].shape[0]
     _, width, share = held.shape
     size = tokens // pieces
     extra = [] if before is None else [before]
+    count = len(steps(share)) * len(pair)
     n = steps(width)[0][1]
-    now = held.shape[0] // len(pair)
 
     def kernel(index_ref, *refs):
         row_refs, refs = refs[: len(rows)], refs[len(rows) :]
         held_ref, refs = refs[0], refs[1:]
         before_refs, refs = refs[: len(extra)], refs[len(extra) :]
         pair_refs, refs = refs[: len(pair)], refs[len(pair) :]
-        out_refs, (next_ref, *sums_ref, sems) = refs[:pieces], refs[pieces:]
-        copies = bring(index_ref, pick, share, pair_refs, next_ref, 0, sems)
+        out_refs, refs = refs[:pieces], refs[pieces:]
+        copies = []
+        for k, pick in enumerate(picks):
+            copies += bring(index_ref, pick, share, pair_refs, refs[0], k * len(pair), refs[1], k * count)
         for copy in copies:
             copy.start()
         inner = sum(joined(r[:, pl.ds(2 * share, LANES)]) for r in row_refs)
@@ -194,48 +236,30 @@
             mine = inner[p * size : (p + 1) * size]
             out[:, pl.ds(width, LANES)] = split(mine) if p else jnp.broadcast_to(mine, (size, LANES))
 
-        def products(weights, those, here):
-            pairs = [(row, i) for row in range(len(those)) for i in range(len(pair))]
-            return sum(
-                dot(those[row][:, pl.ds(i * share, share)], weights[row * len(pair) + i, here, :], NT)
-                for row, i in pairs
+        @pl.loop(0, width // n)
+        def _(step):
+            here = pl.ds(pl.multiple_of(step * n, n), n)
+            part = sum(
+                dot(row_refs[j // 2][:, pl.ds(j % 2 * share, share)], held_ref[j, here, :], NT)
+                for j in range(2 * len(rows))
             )
-
-        def finish(part, here):
             for b in before_refs:
                 part += b[:, here]
             for p, out in enumerate(out_refs):
                 out[:, here] = part[p * size : (p + 1) * size].astype(out.dtype)
 
-        @pl.loop(0, width // n)
-        def _(step):
-            here = pl.ds(pl.multiple_of(step * n, n), n)
-            part = products(held_ref, row_refs[:now], here)
-            if stays:
-                finish(part, here)
-            else:
-                sums_ref[0][:, here] = part
-
-        for copy in copies:
-            copy.wait()
-        if not stays:
-
-            @pl.loop(0, width // n)
-            def _(step):
-                here = pl.ds(pl.multiple_of(step * n, n), n)
-                finish(sums_ref[0][:, here] + products(next_ref, row_refs[now:], here), here)
-
-    brought = pltpu.VMEM((len(pair), width, share), BF16)
+        for copy in copies:
+            copy.wait()
+
+    more = [pltpu.VMEM((len(pair) * len(picks), width, share), BF16)] if picks else []
     return pl.pallas_call(
         kernel,
         in_specs=[SMEM] + [VMEM] * (len(rows) + 1 + len(extra)) + [HBM] * len(pair),
-        out_specs=[VMEM] * (pieces + stays),
-        out_shape=[jax.ShapeDtypeStruct((size, width + LANES), BF16 if p else F32) for p in range(pieces)]
-        + [brought] * stays,
-        scratch_shapes=([] if stays else [brought, pltpu.VMEM((tokens, width), F32)])
-        + [pltpu.SemaphoreType.DMA((len(steps(share)) * len(pair),))],
-        compiler_params=params(8 if stays else 16),
-        cost_estimate=cost(tokens, len(pair) * len(rows) * share, width),
+        out_specs=[VMEM] * (pieces + len(more)),
+        out_shape=[jax.ShapeDtypeStruct((size, width + LANES), BF16 if p else F32) for p in range(pieces)] + more,
+        scratch_shapes=[pltpu.SemaphoreType.DMA((max(1, count * len(picks)),))],
+        compiler_params=params(8),
+        cost_estimate=cost(tokens, held.shape[0] * share, width),
         name=name,
     )(index, *rows, in_vmem(held), *extra, *in_hbm(pair))
 
@@ -294,8 +318,11 @@
         inner = jnp.zeros((tokens, 1), F32)
         for at, n in steps(share):
             here, there = pl.ds(at, n), pl.ds(share + at, n)
-            gate, up = (own_ref[:, x] + near_ref[:, x] + far_ref[:, x].astype(F32) for x in (here, there))
-            back_hidden = hidden_own_ref[:, here] + hidden_near_ref[:, here] + hidden_far_ref[:, here].astype(F32)
+            gate, up = (
+                own_ref[:, x] + near_ref[:, x].astype(F32) + far_ref[:, x].astype(F32) for x in (here, there)
+            )
+            back_hidden = hidden_own_ref[:, here] + hidden_near_ref[:, here].astype(F32)
+            back_hidden += hidden_far_ref[:, here].astype(F32)
             back_gate, back_up = gate_terms(gate, up, back_hidden)
             rows_ref[:, here] = back_gate
             rows_ref[:, there] = back_up
@@ -349,27 +376,27 @@
         index = lax.axis_index("narrow").astype(jnp.int32).reshape(1)
         pair = [gate_weight, up_weight]
         diagonal = near | far
-        targets = [own_target] + [swap(target, "wide", k) for k in range(1, wide)]
+        targets = [own_target] + [swap(own_target, "wide", k) for k in range(1, wide)]
         normeds = [normed] + [swap(normed, "wide", k) for k in range(1, wide)]
 
+        ahead = rows_ahead(index, down_weight, [near], share)
+        ahead, *targets[1:] = lax.optimization_barrier((ahead, *targets[1:]))
         send, keep, held_diagonal = hidden_gradient(
-            index, targets, down_weight, pair, diagonal, [near, diagonal, 0, far], share
+            index, targets, ahead, down_weight, pair, diagonal, [near, diagonal, 0, far], share
         )
         send, *normeds = lax.optimization_barrier((send, *normeds))
-        got = swap(send, "narrow", near)
-        part, held_far = gate_and_up(
-            index, normeds, held_diagonal, pair, [far], False, [send], "gate_up_diagonal"
-        )
-        part, got = lax.optimization_barrier((part, got))
-        hidden_far = swap((keep[:, share:] + got[:, share:]).astype(BF16), "narrow", far)
-        hidden_near = got
+        hidden_near = swap(send, "narrow", near)
+        (part,) = gate_and_up(index, normeds, held_diagonal, pair, [], share, [send], "gate_up_diagonal")
+        part, hidden_near = lax.optimization_barrier((part, hidden_near))
+        sum_far = (keep[:, share:] + hidden_near[:, share:].astype(F32)).astype(BF16)
+        hidden_far = swap(sum_far, "narrow", far)
         got = swap(part, "narrow", near)
-        part, held_near = gate_and_up(index, normeds, held_far, pair, [near], False, [part], "gate_up_far")
+        (part,) = gate_and_up(index, normeds, None, pair, [far], share, [sum_far], "gate_up_far", False)
         part, got, hidden_far = lax.optimization_barrier((part, got, hidden_far))
         sum_far = (part + got).astype(BF16)
         got_far = swap(sum_far, "narrow", far)
-        part, own, held = gate_and_up(
-            index, normeds, held_near, pair, [0, near], True, [sum_far], "gate_up_near_own"
+        own, part, held = gate_and_up(
+            index, normeds, None, pair, [0, near], share, [sum_far], "gate_up_near_own"
         )
         part, got_far = lax.optimization_barrier((part, got_far))
         got = swap(part, "narrow", near)
@@ -377,14 +404,11 @@
 
         rows_far = swap(rows, "narrow", far)
         rows_near = swap(rows, "narrow", near)
-        total, held = backward(
-            index, [rows, rows_near], held, pair, far, True, None, 1, "back_own_near"
-        )
+        total, held = backward(index, [rows, rows_near], held, pair, [far], None, 1, "back_own_near")
         total, rows_far = lax.optimization_barrier((total, rows_far))
         rows_diagonal = swap(rows_far, "narrow", near)
-        pieces = backward(
-            index, [rows_far, rows_diagonal], held, pair, diagonal, False, total, wide, "back_far_diagonal"
-        )
+        total, held = backward(index, [rows_far], held, pair, [diagonal], total, 1, "back_far")
+        pieces = backward(index, [rows_diagonal], held, pair, [], total, wide, "back_diagonal")
         back_normed, inner = pieces[0][:, :width], pieces[0][:, width : width + 1]
         for k in range(1, wide):
             got = swap(pieces[k], "wide", k)

time: 79.8 us -> 75.9 us (0.951)
  waiting for transfers between devices: 14.1 us -> 10.3 us
    ppermute x20, waiting for transfers between devices: 14.1 us -> 10.3 us  [swap(): return lax.ppermute(x, axis, [(i, i ^ k) for i in range(mesh.shape[axis])])]
    pallas_call x4 -> x5, Pallas kernels: 26.1 us -> 26.3 us  [the longest x3 14.7 us: gate_and_up(): pl.pallas_call(kernel, in_specs=[SMEM] + [VMEM] * (len(blocks) + len(give...]
    pallas_call x2 -> x3, Pallas kernels: 14.8 us -> 14.9 us  [backward(): pl.pallas_call(kernel, in_specs=[SMEM] + [VMEM] * (len(rows) + 1 + len(ex...]
  transfers between devices with their start and end apart: 20 -> 20, of which waited for: 11 -> 7; matrix products, arithmetic and copies ran while one was open for 0% -> 0% of each run, Pallas kernels for 43% -> 49%
where the time goes in v4:
time: 75.9 us; the launch traced here: 75.7 us
  Pallas kernels  42.8 us (56%)
  starting transfers between devices  21.2 us (28%)
  waiting for transfers between devices  10.3 us (14%)
  other arithmetic  1.26 us (2%)
    ppermute x20, starting transfers between devices, swap(): return lax.ppermute(x, axis, [(i, i ^ k) for i in range(mesh.shape[axis])])  21.2 us
    pallas_call x3, Pallas kernels, backward(): pl.pallas_call(kernel, in_specs=[SMEM] + [VMEM] * (len(rows) + 1 + len(ex...  14.9 us
    pallas_call x3, Pallas kernels, gate_and_up(): pl.pallas_call(kernel, in_specs=[SMEM] + [VMEM] * (len(blocks) + len(give...  14.7 us
    ppermute x20, waiting for transfers between devices, swap(): return lax.ppermute(x, axis, [(i, i ^ k) for i in range(mesh.shape[axis])])  10.3 us
    pallas_call x1, Pallas kernels, hidden_gradient(): pl.pallas_call(kernel, in_specs=[SMEM] + [VMEM] * (len(blocks) + 1) + [HB...  9.16 us
    pallas_call x1, Pallas kernels, rows_ahead(): pl.pallas_call(kernel, in_specs=[SMEM, HBM], out_specs=VMEM, out_shape=pl...  2.49 us
  transfers between devices with their start and end apart: 20, of which 7 were waited for; matrix products, arithmetic and copies ran while one was open for 0% of the time, Pallas kernels for 49%

profile of v4, /device:TPU:0, one launch (start us, length us, event | category | flops | bytes accessed | tf_op | source)
XLA Modules:
  0.0 75.7 jit_solution(3899399227494061271)
XLA Ops:
  0.0 1.2 %latents.1 = (f32[16,2048]{1,0:T(8,128)S(1)}, f32[16,2048]{1,0:T(8,128)S(1)}, f32[16,1]{1,0:T(8,128)S(1)}, f32[1,2048]{1,0:T(1,128)S(1)}, bf16[16,2048]{1,0:T(8,128)(2,1)S(1)}) custom-call(bf16[16,2048]{1,0:T(8,128)(2,1)} %refs_0_.1, s32[16,2048]{1,0:T(8,128)} %refs_1_.1, f32[16,2048]{1,0:T(8,128)} %refs_2_.1, f32[1,2048]{1,0:T(1,128)} %bitcast.5, ...), custom_call_target="tpu_custom_call" | custom-call | flops 262144 | bytes 589824 | tf_op jit(solution)/shard_map/latents/pallas_call | solution.py:289
  1.2 2.4 %collective-permute-start.2 = (f32[16,1]{1,0:T(8,128)S(1)}, f32[16,1]{1,0:T(8,128)S(1)}, u32[]{:S(2)}, u32[]{:S(2)}) collective-permute-start(f32[16,1]{1,0:T(8,128)S(1)} %get-tuple-element.46), channel_id=1, source_target_pairs={{0,3},{1,2},{2,1},{3,0},{4,7},{5,6},{6,5},{7,4},{8,11},{9,10},{10,... | collective-permute-start | bytes 200 | tf_op jit(solution)/shard_map/ppermute | solution.py:371
  3.6 0.6 collective-permute-start.1
  4.3 0.0 collective-permute-start
  4.3 3.9 %collective-permute-start.5 = (bf16[16,2048]{1,0:T(8,128)(2,1)S(1)}, bf16[16,2048]{1,0:T(8,128)(2,1)S(1)}, u32[]{:S(2)}, u32[]{:S(2)}) collective-permute-start(bf16[16,2048]{1,0:T(8,128)(2,1)S(1)} %get-tuple-element.45.refs_0_), channel_id=1, source_target_pairs={{0,12},{4,8},{8,4},{12,0},{1,13},{5,9},{9,5},{13,1},{2,14},{6,10},... | collective-permute-start | bytes 196616 | tf_op jit(solution)/shard_map/ppermute | solution.py:371
  8.2 0.0 collective-permute-start.4
  8.2 2.5 %rows_ahead.1.refs_4_ = bf16[1280,2048]{1,0:T(8,128)(2,1)S(1)} custom-call(s32[1]{0:T(128)} %bitcast.1.index_ref, bf16[5120,2048]{1,0:T(8,128)(2,1)} %refs_5_.4), custom_call_target="tpu_custom_call" | custom-call | flops 41943040 | bytes 5242880 | tf_op jit(solution)/shard_map/rows_ahead/pallas_call | solution.py:87
  10.7 0.0 collective-permute-done.2
  10.7 0.6 collective-permute-start.3
  11.3 0.0 collective-permute-done.1
  11.3 0.0 collective-permute-done
  11.3 0.1 rsqrt_reduce_fusion
  11.4 0.1 multiply_convert_fusion.refs_0_
  11.5 3.9 %collective-permute-start.8 = (bf16[16,2048]{1,0:T(8,128)(2,1)S(1)}, bf16[16,2048]{1,0:T(8,128)(2,1)S(1)}, u32[]{:S(2)}, u32[]{:S(2)}) collective-permute-start(bf16[16,2048]{1,0:T(8,128)(2,1)S(1)} %multiply_convert_fusion.refs_0_), channel_id=1, source_target_pairs={{0,12},{4,8},{8,4},{12,0},{1,13},{5,9},{9,5},{13,1},{2,14},{6,10},... | collective-permute-start | bytes 196616 | tf_op jit(solution)/shard_map/ppermute | solution.py:371
  15.4 0.0 collective-permute-start.7
  15.4 0.0 collective-permute-done.5.refs_3_
  15.4 0.6 collective-permute-start.6
  16.1 0.0 collective-permute-done.3.refs_1_
  16.1 9.2 %back_hidden.1 = (bf16[64,2560]{1,0:T(8,128)(2,1)S(1)}, f32[64,2560]{1,0:T(8,128)S(1)}, bf16[2,2048,1280]{2,1,0:T(8,128)(2,1)S(1)}) custom-call(s32[1]{0:T(128)} %bitcast.1.index_ref, bf16[16,2048]{1,0:T(8,128)(2,1)S(1)} %get-tuple-element.45.refs_0_, bf16[16,2048]{1,0:T(8,128)(2,1)S(1)} %collective-permute-done.3.refs_1_, ...), custom_call_target="tpu_custom_call" | custom-call | flops 1342177280 | bytes 20971520 | tf_op jit(solution)/shard_map/back_hidden/pallas_call | solution.py:138
  25.2 0.0 collective-permute-done.7.refs_2_
  25.3 0.0 collective-permute-done.6.refs_1_
  25.3 0.1 collective-permute-start.9
  25.3 2.1 %gate_up_diagonal.1 = f32[64,2560]{1,0:T(8,128)S(1)} custom-call(s32[1]{0:T(128)} %bitcast.1.index_ref, bf16[16,2048]{1,0:T(8,128)(2,1)S(1)} %multiply_convert_fusion.refs_0_, bf16[16,2048]{1,0:T(8,128)(2,1)S(1)} %collective-permute-done.6.refs_1_, bf16[16,2048]{1,0:T(8,128)(2,1)S(1)} %collective-permute-done.7.refs_2_, ...), custom_call_target="tpu_custom_call" | custom-call | flops 671088640 | bytes 10485760 | tf_op jit(solution)/shard_map/gate_up_diagonal/pallas_call | solution.py:197
  27.5 0.6 collective-permute-start.10
  28.1 1.5 %collective-permute-start.11 = (bf16[64,1280]{1,0:T(8,128)(2,1)S(1)}, bf16[64,1280]{1,0:T(8,128)(2,1)S(1)}, u32[]{:S(2)}, u32[]{:S(2)}) collective-permute-start(bf16[64,1280]{1,0:T(8,128)(2,1)S(1)} %add_convert_fusion.1.refs_6_), channel_id=1, source_target_pairs={{0,2},{1,3},{2,0},{3,1},{4,6},{5,7},{6,4},{7,5},{8,10},{9,11},{10,... | collective-permute-start | bytes 491528 | tf_op jit(solution)/shard_map/ppermute | solution.py:371
  29.6 4.7 %gate_up_far.1 = f32[64,2560]{1,0:T(8,128)S(1)} custom-call(s32[1]{0:T(128)} %bitcast.1.index_ref, bf16[16,2048]{1,0:T(8,128)(2,1)S(1)} %multiply_convert_fusion.refs_0_, bf16[16,2048]{1,0:T(8,128)(2,1)S(1)} %collective-permute-done.6.refs_1_, bf16[16,2048]{1,0:T(8,128)(2,1)S(1)} %collective-permute-done.7.refs_2_, ...), custom_call_target="tpu_custom_call" | custom-call | flops 671088640 | bytes 10485760 | tf_op jit(solution)/shard_map/gate_up_far/pallas_call | solution.py:197
  34.3 0.0 collective-permute-done.11.hidden_far_ref
  34.3 0.1 add_convert_fusion.refs_6_
  34.4 1.4 %collective-permute-start.12 = (bf16[64,2560]{1,0:T(8,128)(2,1)S(1)}, bf16[64,2560]{1,0:T(8,128)(2,1)S(1)}, u32[]{:S(2)}, u32[]{:S(2)}) collective-permute-start(bf16[64,2560]{1,0:T(8,128)(2,1)S(1)} %add_convert_fusion.refs_6_), channel_id=1, source_target_pairs={{0,2},{1,3},{2,0},{3,1},{4,6},{5,7},{6,4},{7,5},{8,10},{9,11},{10,... | collective-permute-start | bytes 983048 | tf_op jit(solution)/shard_map/ppermute | solution.py:371
  35.8 7.9 %gate_up_near_own.1 = (f32[64,2560]{1,0:T(8,128)S(1)}, bf16[64,2560]{1,0:T(8,128)(2,1)S(1)}, bf16[4,2048,1280]{2,1,0:T(8,128)(2,1)S(1)}) custom-call(s32[1]{0:T(128)} %bitcast.1.index_ref, bf16[16,2048]{1,0:T(8,128)(2,1)S(1)} %multiply_convert_fusion.refs_0_, bf16[16,2048]{1,0:T(8,128)(2,1)S(1)} %collective-permute-done.6.refs_1_, ...), custom_call_target="tpu_custom_call" | custom-call | flops 1342177280 | bytes 20971520 | tf_op jit(solution)/shard_map/gate_up_near_own/pallas_call | solution.py:197
  43.7 0.1 collective-permute-done.12.far_ref
  43.8 1.6 %collective-permute-done.13.near_ref = bf16[64,2560]{1,0:T(8,128)(2,1)S(1)} collective-permute-done((bf16[64,2560]{1,0:T(8,128)(2,1)S(1)}, bf16[64,2560]{1,0:T(8,128)(2,1)S(1)}, u32[]{:S(2)}, u32[]{:S(2)}) %collective-permute-start.13) | collective-permute-done | bytes 327712 | tf_op jit(solution)/shard_map/ppermute | solution.py:371
  45.4 0.4 gate.1
  45.8 0.2 collective-permute-start.14
  46.0 0.8 %collective-permute-start.15 = (bf16[64,2688]{1,0:T(8,128)(2,1)S(1)}, bf16[64,2688]{1,0:T(8,128)(2,1)S(1)}, u32[]{:S(2)}, u32[]{:S(2)}) collective-permute-start(bf16[64,2688]{1,0:T(8,128)(2,1)S(1)} %get-tuple-element.71.refs_0_), channel_id=1, source_target_pairs={{0,2},{1,3},{2,0},{3,1},{4,6},{5,7},{6,4},{7,5},{8,10},{9,11},{10,... | collective-permute-start | bytes 1032200 | tf_op jit(solution)/shard_map/ppermute | solution.py:371
  46.8 0.7 collective-permute-done.14.refs_1_
  47.5 6.9 %back_own_near.1 = (f32[64,2176]{1,0:T(8,128)S(1)}, bf16[2,2048,1280]{2,1,0:T(8,128)(2,1)S(1)}) custom-call(s32[1]{0:T(128)} %bitcast.1.index_ref, bf16[64,2688]{1,0:T(8,128)(2,1)S(1)} %get-tuple-element.71.refs_0_, bf16[64,2688]{1,0:T(8,128)(2,1)S(1)} %collective-permute-done.14.refs_1_, bf16[4,2048,1280]{2,1,0:T(8,128)(2,1)S(1)} %get-tuple-element.72.refs_2_, ...), custom_call_target="tpu_custom_call" | custom-call | flops 1342177280 | bytes 20971520 | tf_op jit(solution)/shard_map/back_own_near/pallas_call | solution.py:255
  54.5 1.9 %collective-permute-done.15.refs_0_ = bf16[64,2688]{1,0:T(8,128)(2,1)S(1)} collective-permute-done((bf16[64,2688]{1,0:T(8,128)(2,1)S(1)}, bf16[64,2688]{1,0:T(8,128)(2,1)S(1)}, u32[]{:S(2)}, u32[]{:S(2)}) %collective-permute-start.15) | collective-permute-done | bytes 344096 | tf_op jit(solution)/shard_map/ppermute | solution.py:371
  56.4 4.1 %back_far.1 = (f32[64,2176]{1,0:T(8,128)S(1)}, bf16[2,2048,1280]{2,1,0:T(8,128)(2,1)S(1)}) custom-call(s32[1]{0:T(128)} %bitcast.1.index_ref, bf16[64,2688]{1,0:T(8,128)(2,1)S(1)} %collective-permute-done.15.refs_0_, bf16[2,2048,1280]{2,1,0:T(8,128)(2,1)S(1)} %get-tuple-element.75.refs_1_, f32[64,2176]{1,0:T(8,128)S(1)} %get-tuple-element.76.refs_2_, ...), custom_call_target="tpu_custom_call" | custom-call | flops 671088640 | bytes 10485760 | tf_op jit(solution)/shard_map/back_far/pallas_call | solution.py:255
  60.5 3.8 %back_diagonal.1 = (f32[16,2176]{1,0:T(8,128)S(1)}, bf16[16,2176]{1,0:T(8,128)(2,1)S(1)}, bf16[16,2176]{1,0:T(8,128)(2,1)S(1)}, bf16[16,2176]{1,0:T(8,128)(2,1)S(1)}) custom-call(s32[1]{0:T(128)} %bitcast.1.index_ref, bf16[64,2688]{1,0:T(8,128)(2,1)S(1)} %collective-permute-done.16.refs_0_, bf16[2,2048,1280]{2,1,0:T(8,128)(2,1)S(1)} %get-tuple-element.77.refs_1_, ...), custom_call_target="tpu_custom_call" | custom-call | flops 671088640 | bytes 10485760 | tf_op jit(solution)/shard_map/back_diagonal/pallas_call | solution.py:255
  64.3 1.3 %collective-permute-start.17 = (bf16[16,2176]{1,0:T(8,128)(2,1)S(1)}, bf16[16,2176]{1,0:T(8,128)(2,1)S(1)}, u32[]{:S(2)}, u32[]{:S(2)}) collective-permute-start(bf16[16,2176]{1,0:T(8,128)(2,1)S(1)} %get-tuple-element.80), channel_id=1, source_target_pairs={{0,4},{4,0},{8,12},{12,8},{1,5},{5,1},{9,13},{13,9},{2,6},{6,2},{1... | collective-permute-start | bytes 208904 | tf_op jit(solution)/shard_map/ppermute | solution.py:371
  65.7 2.9 %collective-permute-start.18 = (bf16[16,2176]{1,0:T(8,128)(2,1)S(1)}, bf16[16,2176]{1,0:T(8,128)(2,1)S(1)}, u32[]{:S(2)}, u32[]{:S(2)}) collective-permute-start(bf16[16,2176]{1,0:T(8,128)(2,1)S(1)} %get-tuple-element.81), channel_id=1, source_target_pairs={{0,8},{4,12},{8,0},{12,4},{1,9},{5,13},{9,1},{13,5},{2,10},{6,14},... | collective-permute-start | bytes 208904 | tf_op jit(solution)/shard_map/ppermute | solution.py:371
  68.6 0.2 collective-permute-start.19
  68.8 0.2 collective-permute-done.17
  69.0 4.8 %collective-permute-done.18 = bf16[16,2176]{1,0:T(8,128)(2,1)S(1)} collective-permute-done((bf16[16,2176]{1,0:T(8,128)(2,1)S(1)}, bf16[16,2176]{1,0:T(8,128)(2,1)S(1)}, u32[]{:S(2)}, u32[]{:S(2)}) %collective-permute-start.18) | collective-permute-done | bytes 69664 | tf_op jit(solution)/shard_map/ppermute | solution.py:371
  73.8 1.0 %collective-permute-done.19 = bf16[16,2176]{1,0:T(8,128)(2,1)S(1)} collective-permute-done((bf16[16,2176]{1,0:T(8,128)(2,1)S(1)}, bf16[16,2176]{1,0:T(8,128)(2,1)S(1)}, u32[]{:S(2)}, u32[]{:S(2)}) %collective-permute-start.19) | collective-permute-done | bytes 69664 | tf_op jit(solution)/shard_map/ppermute | solution.py:371
  74.7 0.2 multiply_reduce_fusion
  74.9 0.8 %multiply_add_fusion = f32[16,2048]{1,0:T(8,128)} fusion(f32[16,2048]{1,0:T(8,128)S(1)} %get-tuple-element.44, f32[16,2176]{1,0:T(8,128)S(1)} %get-tuple-element.79, bf16[16,2048]{1,0:T(8,128)(2,1)S(1)} %get-tuple-element.45.refs_0_, f32[16,2048]{1,0:T(8,128)S(1)} %get-tuple-element.52, bf16[16,2176]{1,0:T(8,128)(2,1)S(1)} %collective-permute-done.19, ...), kind=kLoop, calls=%fused_computation.2 | loop fusion | flops 491520 | bytes 794752 | tf_op jit(solution)/shard_map/add | solution.py:442
  (8 shorter events, 0.0 us)
Async XLA Ops:
  1.2 9.5 %collective-permute-start.2 = (f32[16,1]{1,0:T(8,128)S(1)}, f32[16,1]{1,0:T(8,128)S(1)}, u32[]{:S(2)}, u32[]{:S(2)}) collective-permute-start(f32[16,1]{1,0:T(8,128)S(1)} %get-tuple-element.46), channel_id=1, source_target_pairs={{0,3},{1,2},{2,1},{3,0},{4,7},{5,6},{6,5},{7,4},{8,11},{9,10},{10,... | collective-permute-start | bytes 200 | tf_op jit(solution)/shard_map/ppermute | solution.py:371
  3.6 7.7 %collective-permute-start.1 = (f32[16,1]{1,0:T(8,128)S(1)}, f32[16,1]{1,0:T(8,128)S(1)}, u32[]{:S(2)}, u32[]{:S(2)}) collective-permute-start(f32[16,1]{1,0:T(8,128)S(1)} %get-tuple-element.46), channel_id=1, source_target_pairs={{0,2},{1,3},{2,0},{3,1},{4,6},{5,7},{6,4},{7,5},{8,10},{9,11},{10,... | collective-permute-start | bytes 200 | tf_op jit(solution)/shard_map/ppermute | solution.py:371
  4.3 7.0 %collective-permute-start = (f32[16,1]{1,0:T(8,128)S(1)}, f32[16,1]{1,0:T(8,128)S(1)}, u32[]{:S(2)}, u32[]{:S(2)}) collective-permute-start(f32[16,1]{1,0:T(8,128)S(1)} %get-tuple-element.46), channel_id=1, source_target_pairs={{0,1},{1,0},{2,3},{3,2},{4,5},{5,4},{6,7},{7,6},{8,9},{9,8},{10,11... | collective-permute-start | bytes 200 | tf_op jit(solution)/shard_map/ppermute | solution.py:371
  4.3 11.1 %collective-permute-start.5 = (bf16[16,2048]{1,0:T(8,128)(2,1)S(1)}, bf16[16,2048]{1,0:T(8,128)(2,1)S(1)}, u32[]{:S(2)}, u32[]{:S(2)}) collective-permute-start(bf16[16,2048]{1,0:T(8,128)(2,1)S(1)} %get-tuple-element.45.refs_0_), channel_id=1, source_target_pairs={{0,12},{4,8},{8,4},{12,0},{1,13},{5,9},{9,5},{13,1},{2,14},{6,10},... | collective-permute-start | bytes 196616 | tf_op jit(solution)/shard_map/ppermute | solution.py:371
  8.2 7.9 %collective-permute-start.4 = (bf16[16,2048]{1,0:T(8,128)(2,1)S(1)}, bf16[16,2048]{1,0:T(8,128)(2,1)S(1)}, u32[]{:S(2)}, u32[]{:S(2)}) collective-permute-start(bf16[16,2048]{1,0:T(8,128)(2,1)S(1)} %get-tuple-element.45.refs_0_), channel_id=1, source_target_pairs={{0,8},{4,12},{8,0},{12,4},{1,9},{5,13},{9,1},{13,5},{2,10},{6,14},... | collective-permute-start | bytes 196616 | tf_op jit(solution)/shard_map/ppermute | solution.py:371
  10.7 5.4 %collective-permute-start.3 = (bf16[16,2048]{1,0:T(8,128)(2,1)S(1)}, bf16[16,2048]{1,0:T(8,128)(2,1)S(1)}, u32[]{:S(2)}, u32[]{:S(2)}) collective-permute-start(bf16[16,2048]{1,0:T(8,128)(2,1)S(1)} %get-tuple-element.45.refs_0_), channel_id=1, source_target_pairs={{0,4},{4,0},{8,12},{12,8},{1,5},{5,1},{9,13},{13,9},{2,6},{6,2},{1... | collective-permute-start | bytes 196616 | tf_op jit(solution)/shard_map/ppermute | solution.py:371
  11.5 13.7 %collective-permute-start.8 = (bf16[16,2048]{1,0:T(8,128)(2,1)S(1)}, bf16[16,2048]{1,0:T(8,128)(2,1)S(1)}, u32[]{:S(2)}, u32[]{:S(2)}) collective-permute-start(bf16[16,2048]{1,0:T(8,128)(2,1)S(1)} %multiply_convert_fusion.refs_0_), channel_id=1, source_target_pairs={{0,12},{4,8},{8,4},{12,0},{1,13},{5,9},{9,5},{13,1},{2,14},{6,10},... | collective-permute-start | bytes 196616 | tf_op jit(solution)/shard_map/ppermute | solution.py:371
  15.4 9.8 %collective-permute-start.7 = (bf16[16,2048]{1,0:T(8,128)(2,1)S(1)}, bf16[16,2048]{1,0:T(8,128)(2,1)S(1)}, u32[]{:S(2)}, u32[]{:S(2)}) collective-permute-start(bf16[16,2048]{1,0:T(8,128)(2,1)S(1)} %multiply_convert_fusion.refs_0_), channel_id=1, source_target_pairs={{0,8},{4,12},{8,0},{12,4},{1,9},{5,13},{9,1},{13,5},{2,10},{6,14},... | collective-permute-start | bytes 196616 | tf_op jit(solution)/shard_map/ppermute | solution.py:371
  15.4 9.8 %collective-permute-start.6 = (bf16[16,2048]{1,0:T(8,128)(2,1)S(1)}, bf16[16,2048]{1,0:T(8,128)(2,1)S(1)}, u32[]{:S(2)}, u32[]{:S(2)}) collective-permute-start(bf16[16,2048]{1,0:T(8,128)(2,1)S(1)} %multiply_convert_fusion.refs_0_), channel_id=1, source_target_pairs={{0,4},{4,0},{8,12},{12,8},{1,5},{5,1},{9,13},{13,9},{2,6},{6,2},{1... | collective-permute-start | bytes 196616 | tf_op jit(solution)/shard_map/ppermute | solution.py:371
  25.3 2.2 %collective-permute-start.9 = (bf16[64,2560]{1,0:T(8,128)(2,1)S(1)}, bf16[64,2560]{1,0:T(8,128)(2,1)S(1)}, u32[]{:S(2)}, u32[]{:S(2)}) collective-permute-start(bf16[64,2560]{1,0:T(8,128)(2,1)S(1)} %get-tuple-element.60.refs_7_), channel_id=1, source_target_pairs={{0,1},{1,0},{2,3},{3,2},{4,5},{5,4},{6,7},{7,6},{8,9},{9,8},{10,11... | collective-permute-start | bytes 983048 | tf_op jit(solution)/shard_map/ppermute | solution.py:371
  27.5 6.8 %collective-permute-start.10 = (f32[64,2560]{1,0:T(8,128)S(1)}, f32[64,2560]{1,0:T(8,128)S(1)}, u32[]{:S(2)}, u32[]{:S(2)}) collective-permute-start(f32[64,2560]{1,0:T(8,128)S(1)} %gate_up_diagonal.1), channel_id=1, source_target_pairs={{0,1},{1,0},{2,3},{3,2},{4,5},{5,4},{6,7},{7,6},{8,9},{9,8},{10,11... | collective-permute-start | bytes 1966088 | tf_op jit(solution)/shard_map/ppermute | solution.py:371
  28.1 6.2 %collective-permute-start.11 = (bf16[64,1280]{1,0:T(8,128)(2,1)S(1)}, bf16[64,1280]{1,0:T(8,128)(2,1)S(1)}, u32[]{:S(2)}, u32[]{:S(2)}) collective-permute-start(bf16[64,1280]{1,0:T(8,128)(2,1)S(1)} %add_convert_fusion.1.refs_6_), channel_id=1, source_target_pairs={{0,2},{1,3},{2,0},{3,1},{4,6},{5,7},{6,4},{7,5},{8,10},{9,11},{10,... | collective-permute-start | bytes 491528 | tf_op jit(solution)/shard_map/ppermute | solution.py:371
  34.4 9.4 %collective-permute-start.12 = (bf16[64,2560]{1,0:T(8,128)(2,1)S(1)}, bf16[64,2560]{1,0:T(8,128)(2,1)S(1)}, u32[]{:S(2)}, u32[]{:S(2)}) collective-permute-start(bf16[64,2560]{1,0:T(8,128)(2,1)S(1)} %add_convert_fusion.refs_6_), channel_id=1, source_target_pairs={{0,2},{1,3},{2,0},{3,1},{4,6},{5,7},{6,4},{7,5},{8,10},{9,11},{10,... | collective-permute-start | bytes 983048 | tf_op jit(solution)/shard_map/ppermute | solution.py:371
  43.8 1.6 %collective-permute-start.13 = (bf16[64,2560]{1,0:T(8,128)(2,1)S(1)}, bf16[64,2560]{1,0:T(8,128)(2,1)S(1)}, u32[]{:S(2)}, u32[]{:S(2)}) collective-permute-start(bf16[64,2560]{1,0:T(8,128)(2,1)S(1)} %get-tuple-element.67), channel_id=1, source_target_pairs={{0,1},{1,0},{2,3},{3,2},{4,5},{5,4},{6,7},{7,6},{8,9},{9,8},{10,11... | collective-permute-start | bytes 983048 | tf_op jit(solution)/shard_map/ppermute | solution.py:371
  45.8 1.7 %collective-permute-start.14 = (bf16[64,2688]{1,0:T(8,128)(2,1)S(1)}, bf16[64,2688]{1,0:T(8,128)(2,1)S(1)}, u32[]{:S(2)}, u32[]{:S(2)}) collective-permute-start(bf16[64,2688]{1,0:T(8,128)(2,1)S(1)} %get-tuple-element.71.refs_0_), channel_id=1, source_target_pairs={{0,1},{1,0},{2,3},{3,2},{4,5},{5,4},{6,7},{7,6},{8,9},{9,8},{10,11... | collective-permute-start | bytes 1032200 | tf_op jit(solution)/shard_map/ppermute | solution.py:371
  46.0 10.3 %collective-permute-start.15 = (bf16[64,2688]{1,0:T(8,128)(2,1)S(1)}, bf16[64,2688]{1,0:T(8,128)(2,1)S(1)}, u32[]{:S(2)}, u32[]{:S(2)}) collective-permute-start(bf16[64,2688]{1,0:T(8,128)(2,1)S(1)} %get-tuple-element.71.refs_0_), channel_id=1, source_target_pairs={{0,2},{1,3},{2,0},{3,1},{4,6},{5,7},{6,4},{7,5},{8,10},{9,11},{10,... | collective-permute-start | bytes 1032200 | tf_op jit(solution)/shard_map/ppermute | solution.py:371
  56.4 4.2 %collective-permute-start.16 = (bf16[64,2688]{1,0:T(8,128)(2,1)S(1)}, bf16[64,2688]{1,0:T(8,128)(2,1)S(1)}, u32[]{:S(2)}, u32[]{:S(2)}) collective-permute-start(bf16[64,2688]{1,0:T(8,128)(2,1)S(1)} %collective-permute-done.15.refs_0_), channel_id=1, source_target_pairs={{0,1},{1,0},{2,3},{3,2},{4,5},{5,4},{6,7},{7,6},{8,9},{9,8},{10,11... | collective-permute-start | bytes 1032200 | tf_op jit(solution)/shard_map/ppermute | solution.py:371
  64.3 4.7 %collective-permute-start.17 = (bf16[16,2176]{1,0:T(8,128)(2,1)S(1)}, bf16[16,2176]{1,0:T(8,128)(2,1)S(1)}, u32[]{:S(2)}, u32[]{:S(2)}) collective-permute-start(bf16[16,2176]{1,0:T(8,128)(2,1)S(1)} %get-tuple-element.80), channel_id=1, source_target_pairs={{0,4},{4,0},{8,12},{12,8},{1,5},{5,1},{9,13},{13,9},{2,6},{6,2},{1... | collective-permute-start | bytes 208904 | tf_op jit(solution)/shard_map/ppermute | solution.py:371
  65.7 8.1 %collective-permute-start.18 = (bf16[16,2176]{1,0:T(8,128)(2,1)S(1)}, bf16[16,2176]{1,0:T(8,128)(2,1)S(1)}, u32[]{:S(2)}, u32[]{:S(2)}) collective-permute-start(bf16[16,2176]{1,0:T(8,128)(2,1)S(1)} %get-tuple-element.81), channel_id=1, source_target_pairs={{0,8},{4,12},{8,0},{12,4},{1,9},{5,13},{9,1},{13,5},{2,10},{6,14},... | collective-permute-start | bytes 208904 | tf_op jit(solution)/shard_map/ppermute | solution.py:371
  68.6 6.2 %collective-permute-start.19 = (bf16[16,2176]{1,0:T(8,128)(2,1)S(1)}, bf16[16,2176]{1,0:T(8,128)(2,1)S(1)}, u32[]{:S(2)}, u32[]{:S(2)}) collective-permute-start(bf16[16,2176]{1,0:T(8,128)(2,1)S(1)} %get-tuple-element.82), channel_id=1, source_target_pairs={{0,12},{4,8},{8,4},{12,0},{1,13},{5,9},{9,5},{13,1},{2,14},{6,10},... | collective-permute-start | bytes 208904 | tf_op jit(solution)/shard_map/ppermute | solution.py:371

commit v5 on v4

--- a/solution.py
+++ b/solution.py
@@ -122,13 +122,13 @@
         @pl.loop(0, held.shape[0] // n)
         def _(step):
             here = pl.ds(pl.multiple_of(step * n, n), n)
-            send_ref[:, here] = dot(rows_ref[...], held_ref[here, :], NT).astype(BF16)
+            send_ref[:, here] = dot(rows_ref[...], held_ref[here, :], NT)
 
         for j, (r, at, _) in enumerate(parts):
             copies[j].wait()
             here, part = r * share + at, dot(rows_ref[...], down_parts[j], NT)
             if here < half:
-                send_ref[:, pl.ds(here, n)] = part.astype(BF16)
+                send_ref[:, pl.ds(here, n)] = part
             else:
                 keep_ref[:, pl.ds(here - half, n)] = part
         for copy in later:
@@ -140,7 +140,7 @@
         in_specs=[SMEM] + [VMEM] * (len(blocks) + 1) + [HBM] * (1 + len(pair)),
         out_specs=[VMEM] * 3,
         out_shape=[
-            jax.ShapeDtypeStruct((tokens, half), BF16),
+            jax.ShapeDtypeStruct((tokens, half), F32),
             jax.ShapeDtypeStruct((tokens, half), F32),
             pltpu.VMEM((len(pair), width, share), BF16),
         ],
@@ -369,6 +369,9 @@
 
     def swap(x, axis, k):
         return lax.ppermute(x, axis, [(i, i ^ k) for i in range(mesh.shape[axis])])
+
+    def turn(x, k):
+        return lax.ppermute(x, "wide", [(i, (i + k) % wide) for i in range(wide)])
 
     def by_swaps(normed, target, own_target, gate_weight, up_weight, down_weight):
         width, hidden = gate_weight.shape
@@ -410,7 +413,7 @@
         total, held = backward(index, [rows_far], held, pair, [diagonal], total, 1, "back_far")
         pieces = backward(index, [rows_diagonal], held, pair, [], total, wide, "back_diagonal")
         back_normed, inner = pieces[0][:, :width], pieces[0][:, width : width + 1]
-        for k in range(1, wide):
+        for k in reversed(range(1, wide)):
             got = swap(pieces[k], "wide", k)
             back_normed = back_normed + got[:, :width].astype(F32)
             inner = inner + joined(got[:, width:])

time: 75.9 us -> 75.3 us (level)
  transfers between devices with their start and end apart: 20 -> 20, of which waited for: 7 -> 6; matrix products, arithmetic and copies ran while one was open for 0% -> 0% of each run, Pallas kernels for 49% -> 50%
where the time goes in v5:
time: 75.3 us; the launch traced here: 75.1 us
  Pallas kernels  42.8 us (57%)
  starting transfers between devices  21.2 us (28%)
  waiting for transfers between devices  9.71 us (13%)
  other arithmetic  1.27 us (2%)
    ppermute x20, starting transfers between devices, swap(): return lax.ppermute(x, axis, [(i, i ^ k) for i in range(mesh.shape[axis])])  21.2 us
    pallas_call x3, Pallas kernels, backward(): pl.pallas_call(kernel, in_specs=[SMEM] + [VMEM] * (len(rows) + 1 + len(ex...  14.9 us
    pallas_call x3, Pallas kernels, gate_and_up(): pl.pallas_call(kernel, in_specs=[SMEM] + [VMEM] * (len(blocks) + len(give...  14.7 us
    ppermute x20, waiting for transfers between devices, swap(): return lax.ppermute(x, axis, [(i, i ^ k) for i in range(mesh.shape[axis])])  9.71 us
    pallas_call x1, Pallas kernels, hidden_gradient(): pl.pallas_call(kernel, in_specs=[SMEM] + [VMEM] * (len(blocks) + 1) + [HB...  9.16 us
    pallas_call x1, Pallas kernels, rows_ahead(): pl.pallas_call(kernel, in_specs=[SMEM, HBM], out_specs=VMEM, out_shape=pl...  2.49 us
  transfers between devices with their start and end apart: 20, of which 6 were waited for; matrix products, arithmetic and copies ran while one was open for 0% of the time, Pallas kernels for 50%

profile of v5, /device:TPU:0, one launch (start us, length us, event | category | flops | bytes accessed | tf_op | source)
XLA Modules:
  0.0 75.1 jit_solution(7661391909979452402)
XLA Ops:
  0.0 1.2 %latents.1 = (f32[16,2048]{1,0:T(8,128)S(1)}, f32[16,2048]{1,0:T(8,128)S(1)}, f32[16,1]{1,0:T(8,128)S(1)}, f32[1,2048]{1,0:T(1,128)S(1)}, bf16[16,2048]{1,0:T(8,128)(2,1)S(1)}) custom-call(bf16[16,2048]{1,0:T(8,128)(2,1)} %refs_0_.1, s32[16,2048]{1,0:T(8,128)} %refs_1_.1, f32[16,2048]{1,0:T(8,128)} %refs_2_.1, f32[1,2048]{1,0:T(1,128)} %bitcast.5, ...), custom_call_target="tpu_custom_call" | custom-call | flops 262144 | bytes 589824 | tf_op jit(solution)/shard_map/latents/pallas_call | solution.py:289
  1.2 2.4 %collective-permute-start.2 = (f32[16,1]{1,0:T(8,128)S(1)}, f32[16,1]{1,0:T(8,128)S(1)}, u32[]{:S(2)}, u32[]{:S(2)}) collective-permute-start(f32[16,1]{1,0:T(8,128)S(1)} %get-tuple-element.46), channel_id=1, source_target_pairs={{0,3},{1,2},{2,1},{3,0},{4,7},{5,6},{6,5},{7,4},{8,11},{9,10},{10,... | collective-permute-start | bytes 200 | tf_op jit(solution)/shard_map/ppermute | solution.py:371
  3.6 0.6 collective-permute-start.1
  4.3 0.0 collective-permute-start
  4.3 3.9 %collective-permute-start.5 = (bf16[16,2048]{1,0:T(8,128)(2,1)S(1)}, bf16[16,2048]{1,0:T(8,128)(2,1)S(1)}, u32[]{:S(2)}, u32[]{:S(2)}) collective-permute-start(bf16[16,2048]{1,0:T(8,128)(2,1)S(1)} %get-tuple-element.45.refs_0_), channel_id=1, source_target_pairs={{0,12},{4,8},{8,4},{12,0},{1,13},{5,9},{9,5},{13,1},{2,14},{6,10},... | collective-permute-start | bytes 196616 | tf_op jit(solution)/shard_map/ppermute | solution.py:371
  8.2 0.0 collective-permute-start.4
  8.2 2.5 %rows_ahead.1.refs_4_ = bf16[1280,2048]{1,0:T(8,128)(2,1)S(1)} custom-call(s32[1]{0:T(128)} %bitcast.1.index_ref, bf16[5120,2048]{1,0:T(8,128)(2,1)} %refs_5_.4), custom_call_target="tpu_custom_call" | custom-call | flops 41943040 | bytes 5242880 | tf_op jit(solution)/shard_map/rows_ahead/pallas_call | solution.py:87
  10.7 0.0 collective-permute-done.2
  10.7 0.6 collective-permute-start.3
  11.3 0.0 collective-permute-done.1
  11.3 0.0 collective-permute-done
  11.3 0.1 rsqrt_reduce_fusion
  11.4 0.1 multiply_convert_fusion.refs_0_
  11.5 3.9 %collective-permute-start.8 = (bf16[16,2048]{1,0:T(8,128)(2,1)S(1)}, bf16[16,2048]{1,0:T(8,128)(2,1)S(1)}, u32[]{:S(2)}, u32[]{:S(2)}) collective-permute-start(bf16[16,2048]{1,0:T(8,128)(2,1)S(1)} %multiply_convert_fusion.refs_0_), channel_id=1, source_target_pairs={{0,12},{4,8},{8,4},{12,0},{1,13},{5,9},{9,5},{13,1},{2,14},{6,10},... | collective-permute-start | bytes 196616 | tf_op jit(solution)/shard_map/ppermute | solution.py:371
  15.4 0.0 collective-permute-start.7
  15.4 0.0 collective-permute-done.5.refs_3_
  15.4 0.6 collective-permute-start.6
  16.1 0.0 collective-permute-done.3.refs_1_
  16.1 9.2 %back_hidden.1 = (f32[64,2560]{1,0:T(8,128)S(1)}, f32[64,2560]{1,0:T(8,128)S(1)}, bf16[2,2048,1280]{2,1,0:T(8,128)(2,1)S(1)}) custom-call(s32[1]{0:T(128)} %bitcast.1.index_ref, bf16[16,2048]{1,0:T(8,128)(2,1)S(1)} %get-tuple-element.45.refs_0_, bf16[16,2048]{1,0:T(8,128)(2,1)S(1)} %collective-permute-done.3.refs_1_, ...), custom_call_target="tpu_custom_call" | custom-call | flops 1342177280 | bytes 20971520 | tf_op jit(solution)/shard_map/back_hidden/pallas_call | solution.py:138
  25.2 0.0 collective-permute-done.7.refs_2_
  25.3 0.0 collective-permute-done.6.refs_1_
  25.3 0.1 collective-permute-start.9
  25.3 2.1 %gate_up_diagonal.1 = f32[64,2560]{1,0:T(8,128)S(1)} custom-call(s32[1]{0:T(128)} %bitcast.1.index_ref, bf16[16,2048]{1,0:T(8,128)(2,1)S(1)} %multiply_convert_fusion.refs_0_, bf16[16,2048]{1,0:T(8,128)(2,1)S(1)} %collective-permute-done.6.refs_1_, bf16[16,2048]{1,0:T(8,128)(2,1)S(1)} %collective-permute-done.7.refs_2_, ...), custom_call_target="tpu_custom_call" | custom-call | flops 671088640 | bytes 10485760 | tf_op jit(solution)/shard_map/gate_up_diagonal/pallas_call | solution.py:197
  27.5 0.6 collective-permute-start.10
  28.1 1.5 %collective-permute-start.11 = (bf16[64,1280]{1,0:T(8,128)(2,1)S(1)}, bf16[64,1280]{1,0:T(8,128)(2,1)S(1)}, u32[]{:S(2)}, u32[]{:S(2)}) collective-permute-start(bf16[64,1280]{1,0:T(8,128)(2,1)S(1)} %add_convert_fusion.1.refs_6_), channel_id=1, source_target_pairs={{0,2},{1,3},{2,0},{3,1},{4,6},{5,7},{6,4},{7,5},{8,10},{9,11},{10,... | collective-permute-start | bytes 491528 | tf_op jit(solution)/shard_map/ppermute | solution.py:371
  29.6 4.7 %gate_up_far.1 = f32[64,2560]{1,0:T(8,128)S(1)} custom-call(s32[1]{0:T(128)} %bitcast.1.index_ref, bf16[16,2048]{1,0:T(8,128)(2,1)S(1)} %multiply_convert_fusion.refs_0_, bf16[16,2048]{1,0:T(8,128)(2,1)S(1)} %collective-permute-done.6.refs_1_, bf16[16,2048]{1,0:T(8,128)(2,1)S(1)} %collective-permute-done.7.refs_2_, ...), custom_call_target="tpu_custom_call" | custom-call | flops 671088640 | bytes 10485760 | tf_op jit(solution)/shard_map/gate_up_far/pallas_call | solution.py:197
  34.3 0.0 collective-permute-done.10
  34.3 0.1 add_convert_fusion.refs_6_
  34.4 1.4 %collective-permute-start.12 = (bf16[64,2560]{1,0:T(8,128)(2,1)S(1)}, bf16[64,2560]{1,0:T(8,128)(2,1)S(1)}, u32[]{:S(2)}, u32[]{:S(2)}) collective-permute-start(bf16[64,2560]{1,0:T(8,128)(2,1)S(1)} %add_convert_fusion.refs_6_), channel_id=1, source_target_pairs={{0,2},{1,3},{2,0},{3,1},{4,6},{5,7},{6,4},{7,5},{8,10},{9,11},{10,... | collective-permute-start | bytes 983048 | tf_op jit(solution)/shard_map/ppermute | solution.py:371
  35.8 7.8 %gate_up_near_own.1 = (f32[64,2560]{1,0:T(8,128)S(1)}, bf16[64,2560]{1,0:T(8,128)(2,1)S(1)}, bf16[4,2048,1280]{2,1,0:T(8,128)(2,1)S(1)}) custom-call(s32[1]{0:T(128)} %bitcast.1.index_ref, bf16[16,2048]{1,0:T(8,128)(2,1)S(1)} %multiply_convert_fusion.refs_0_, bf16[16,2048]{1,0:T(8,128)(2,1)S(1)} %collective-permute-done.6.refs_1_, ...), custom_call_target="tpu_custom_call" | custom-call | flops 1342177280 | bytes 20971520 | tf_op jit(solution)/shard_map/gate_up_near_own/pallas_call | solution.py:197
  43.7 0.1 collective-permute-done.12.far_ref
  43.8 0.0 collective-permute-start.13
  43.8 1.6 %collective-permute-done.13.near_ref = bf16[64,2560]{1,0:T(8,128)(2,1)S(1)} collective-permute-done((bf16[64,2560]{1,0:T(8,128)(2,1)S(1)}, bf16[64,2560]{1,0:T(8,128)(2,1)S(1)}, u32[]{:S(2)}, u32[]{:S(2)}) %collective-permute-start.13) | collective-permute-done | bytes 327712 | tf_op jit(solution)/shard_map/ppermute | solution.py:371
  45.4 0.4 gate.1
  45.9 0.2 collective-permute-start.14
  46.0 0.8 %collective-permute-start.15 = (bf16[64,2688]{1,0:T(8,128)(2,1)S(1)}, bf16[64,2688]{1,0:T(8,128)(2,1)S(1)}, u32[]{:S(2)}, u32[]{:S(2)}) collective-permute-start(bf16[64,2688]{1,0:T(8,128)(2,1)S(1)} %get-tuple-element.71.refs_0_), channel_id=1, source_target_pairs={{0,2},{1,3},{2,0},{3,1},{4,6},{5,7},{6,4},{7,5},{8,10},{9,11},{10,... | collective-permute-start | bytes 1032200 | tf_op jit(solution)/shard_map/ppermute | solution.py:371
  46.8 0.7 collective-permute-done.14.refs_1_
  47.5 6.9 %back_own_near.1 = (f32[64,2176]{1,0:T(8,128)S(1)}, bf16[2,2048,1280]{2,1,0:T(8,128)(2,1)S(1)}) custom-call(s32[1]{0:T(128)} %bitcast.1.index_ref, bf16[64,2688]{1,0:T(8,128)(2,1)S(1)} %get-tuple-element.71.refs_0_, bf16[64,2688]{1,0:T(8,128)(2,1)S(1)} %collective-permute-done.14.refs_1_, bf16[4,2048,1280]{2,1,0:T(8,128)(2,1)S(1)} %get-tuple-element.72.refs_2_, ...), custom_call_target="tpu_custom_call" | custom-call | flops 1342177280 | bytes 20971520 | tf_op jit(solution)/shard_map/back_own_near/pallas_call | solution.py:255
  54.5 1.9 %collective-permute-done.15.refs_0_ = bf16[64,2688]{1,0:T(8,128)(2,1)S(1)} collective-permute-done((bf16[64,2688]{1,0:T(8,128)(2,1)S(1)}, bf16[64,2688]{1,0:T(8,128)(2,1)S(1)}, u32[]{:S(2)}, u32[]{:S(2)}) %collective-permute-start.15) | collective-permute-done | bytes 344096 | tf_op jit(solution)/shard_map/ppermute | solution.py:371
  56.4 4.1 %back_far.1 = (f32[64,2176]{1,0:T(8,128)S(1)}, bf16[2,2048,1280]{2,1,0:T(8,128)(2,1)S(1)}) custom-call(s32[1]{0:T(128)} %bitcast.1.index_ref, bf16[64,2688]{1,0:T(8,128)(2,1)S(1)} %collective-permute-done.15.refs_0_, bf16[2,2048,1280]{2,1,0:T(8,128)(2,1)S(1)} %get-tuple-element.75.refs_1_, f32[64,2176]{1,0:T(8,128)S(1)} %get-tuple-element.76.refs_2_, ...), custom_call_target="tpu_custom_call" | custom-call | flops 671088640 | bytes 10485760 | tf_op jit(solution)/shard_map/back_far/pallas_call | solution.py:255
  60.5 3.8 %back_diagonal.1 = (f32[16,2176]{1,0:T(8,128)S(1)}, bf16[16,2176]{1,0:T(8,128)(2,1)S(1)}, bf16[16,2176]{1,0:T(8,128)(2,1)S(1)}, bf16[16,2176]{1,0:T(8,128)(2,1)S(1)}) custom-call(s32[1]{0:T(128)} %bitcast.1.index_ref, bf16[64,2688]{1,0:T(8,128)(2,1)S(1)} %collective-permute-done.16.refs_0_, bf16[2,2048,1280]{2,1,0:T(8,128)(2,1)S(1)} %get-tuple-element.77.refs_1_, ...), custom_call_target="tpu_custom_call" | custom-call | flops 671088640 | bytes 10485760 | tf_op jit(solution)/shard_map/back_diagonal/pallas_call | solution.py:255
  64.3 3.7 %collective-permute-start.17 = (bf16[16,2176]{1,0:T(8,128)(2,1)S(1)}, bf16[16,2176]{1,0:T(8,128)(2,1)S(1)}, u32[]{:S(2)}, u32[]{:S(2)}) collective-permute-start(bf16[16,2176]{1,0:T(8,128)(2,1)S(1)} %get-tuple-element.80), channel_id=1, source_target_pairs={{0,12},{4,8},{8,4},{12,0},{1,13},{5,9},{9,5},{13,1},{2,14},{6,10},... | collective-permute-start | bytes 208904 | tf_op jit(solution)/shard_map/ppermute | solution.py:371
  68.0 0.8 %collective-permute-start.19 = (bf16[16,2176]{1,0:T(8,128)(2,1)S(1)}, bf16[16,2176]{1,0:T(8,128)(2,1)S(1)}, u32[]{:S(2)}, u32[]{:S(2)}) collective-permute-start(bf16[16,2176]{1,0:T(8,128)(2,1)S(1)} %get-tuple-element.82), channel_id=1, source_target_pairs={{0,4},{4,0},{8,12},{12,8},{1,5},{5,1},{9,13},{13,9},{2,6},{6,2},{1... | collective-permute-start | bytes 208904 | tf_op jit(solution)/shard_map/ppermute | solution.py:371
  68.8 2.5 %collective-permute-done.17 = bf16[16,2176]{1,0:T(8,128)(2,1)S(1)} collective-permute-done((bf16[16,2176]{1,0:T(8,128)(2,1)S(1)}, bf16[16,2176]{1,0:T(8,128)(2,1)S(1)}, u32[]{:S(2)}, u32[]{:S(2)}) %collective-permute-start.17) | collective-permute-done | bytes 69664 | tf_op jit(solution)/shard_map/ppermute | solution.py:371
  71.3 2.9 %collective-permute-done.18 = bf16[16,2176]{1,0:T(8,128)(2,1)S(1)} collective-permute-done((bf16[16,2176]{1,0:T(8,128)(2,1)S(1)}, bf16[16,2176]{1,0:T(8,128)(2,1)S(1)}, u32[]{:S(2)}, u32[]{:S(2)}) %collective-permute-start.18) | collective-permute-done | bytes 69664 | tf_op jit(solution)/shard_map/ppermute | solution.py:371
  74.2 0.0 collective-permute-done.19
  74.2 0.2 multiply_reduce_fusion
  74.4 0.8 %multiply_add_fusion = f32[16,2048]{1,0:T(8,128)} fusion(f32[16,2048]{1,0:T(8,128)S(1)} %get-tuple-element.44, f32[16,2176]{1,0:T(8,128)S(1)} %get-tuple-element.79, bf16[16,2048]{1,0:T(8,128)(2,1)S(1)} %get-tuple-element.45.refs_0_, f32[16,2048]{1,0:T(8,128)S(1)} %get-tuple-element.52, bf16[16,2176]{1,0:T(8,128)(2,1)S(1)} %collective-permute-done.19, ...), kind=kLoop, calls=%fused_computation.2 | loop fusion | flops 491520 | bytes 794752 | tf_op jit(solution)/shard_map/add | solution.py:445
  (8 shorter events, 0.1 us)
Async XLA Ops:
  1.2 9.5 %collective-permute-start.2 = (f32[16,1]{1,0:T(8,128)S(1)}, f32[16,1]{1,0:T(8,128)S(1)}, u32[]{:S(2)}, u32[]{:S(2)}) collective-permute-start(f32[16,1]{1,0:T(8,128)S(1)} %get-tuple-element.46), channel_id=1, source_target_pairs={{0,3},{1,2},{2,1},{3,0},{4,7},{5,6},{6,5},{7,4},{8,11},{9,10},{10,... | collective-permute-start | bytes 200 | tf_op jit(solution)/shard_map/ppermute | solution.py:371
  3.6 7.7 %collective-permute-start.1 = (f32[16,1]{1,0:T(8,128)S(1)}, f32[16,1]{1,0:T(8,128)S(1)}, u32[]{:S(2)}, u32[]{:S(2)}) collective-permute-start(f32[16,1]{1,0:T(8,128)S(1)} %get-tuple-element.46), channel_id=1, source_target_pairs={{0,2},{1,3},{2,0},{3,1},{4,6},{5,7},{6,4},{7,5},{8,10},{9,11},{10,... | collective-permute-start | bytes 200 | tf_op jit(solution)/shard_map/ppermute | solution.py:371
  4.3 7.0 %collective-permute-start = (f32[16,1]{1,0:T(8,128)S(1)}, f32[16,1]{1,0:T(8,128)S(1)}, u32[]{:S(2)}, u32[]{:S(2)}) collective-permute-start(f32[16,1]{1,0:T(8,128)S(1)} %get-tuple-element.46), channel_id=1, source_target_pairs={{0,1},{1,0},{2,3},{3,2},{4,5},{5,4},{6,7},{7,6},{8,9},{9,8},{10,11... | collective-permute-start | bytes 200 | tf_op jit(solution)/shard_map/ppermute | solution.py:371
  4.3 11.1 %collective-permute-start.5 = (bf16[16,2048]{1,0:T(8,128)(2,1)S(1)}, bf16[16,2048]{1,0:T(8,128)(2,1)S(1)}, u32[]{:S(2)}, u32[]{:S(2)}) collective-permute-start(bf16[16,2048]{1,0:T(8,128)(2,1)S(1)} %get-tuple-element.45.refs_0_), channel_id=1, source_target_pairs={{0,12},{4,8},{8,4},{12,0},{1,13},{5,9},{9,5},{13,1},{2,14},{6,10},... | collective-permute-start | bytes 196616 | tf_op jit(solution)/shard_map/ppermute | solution.py:371
  8.2 7.9 %collective-permute-start.4 = (bf16[16,2048]{1,0:T(8,128)(2,1)S(1)}, bf16[16,2048]{1,0:T(8,128)(2,1)S(1)}, u32[]{:S(2)}, u32[]{:S(2)}) collective-permute-start(bf16[16,2048]{1,0:T(8,128)(2,1)S(1)} %get-tuple-element.45.refs_0_), channel_id=1, source_target_pairs={{0,8},{4,12},{8,0},{12,4},{1,9},{5,13},{9,1},{13,5},{2,10},{6,14},... | collective-permute-start | bytes 196616 | tf_op jit(solution)/shard_map/ppermute | solution.py:371
  10.7 5.4 %collective-permute-start.3 = (bf16[16,2048]{1,0:T(8,128)(2,1)S(1)}, bf16[16,2048]{1,0:T(8,128)(2,1)S(1)}, u32[]{:S(2)}, u32[]{:S(2)}) collective-permute-start(bf16[16,2048]{1,0:T(8,128)(2,1)S(1)} %get-tuple-element.45.refs_0_), channel_id=1, source_target_pairs={{0,4},{4,0},{8,12},{12,8},{1,5},{5,1},{9,13},{13,9},{2,6},{6,2},{1... | collective-permute-start | bytes 196616 | tf_op jit(solution)/shard_map/ppermute | solution.py:371
  11.5 13.7 %collective-permute-start.8 = (bf16[16,2048]{1,0:T(8,128)(2,1)S(1)}, bf16[16,2048]{1,0:T(8,128)(2,1)S(1)}, u32[]{:S(2)}, u32[]{:S(2)}) collective-permute-start(bf16[16,2048]{1,0:T(8,128)(2,1)S(1)} %multiply_convert_fusion.refs_0_), channel_id=1, source_target_pairs={{0,12},{4,8},{8,4},{12,0},{1,13},{5,9},{9,5},{13,1},{2,14},{6,10},... | collective-permute-start | bytes 196616 | tf_op jit(solution)/shard_map/ppermute | solution.py:371
  15.4 9.8 %collective-permute-start.7 = (bf16[16,2048]{1,0:T(8,128)(2,1)S(1)}, bf16[16,2048]{1,0:T(8,128)(2,1)S(1)}, u32[]{:S(2)}, u32[]{:S(2)}) collective-permute-start(bf16[16,2048]{1,0:T(8,128)(2,1)S(1)} %multiply_convert_fusion.refs_0_), channel_id=1, source_target_pairs={{0,8},{4,12},{8,0},{12,4},{1,9},{5,13},{9,1},{13,5},{2,10},{6,14},... | collective-permute-start | bytes 196616 | tf_op jit(solution)/shard_map/ppermute | solution.py:371
  15.4 9.8 %collective-permute-start.6 = (bf16[16,2048]{1,0:T(8,128)(2,1)S(1)}, bf16[16,2048]{1,0:T(8,128)(2,1)S(1)}, u32[]{:S(2)}, u32[]{:S(2)}) collective-permute-start(bf16[16,2048]{1,0:T(8,128)(2,1)S(1)} %multiply_convert_fusion.refs_0_), channel_id=1, source_target_pairs={{0,4},{4,0},{8,12},{12,8},{1,5},{5,1},{9,13},{13,9},{2,6},{6,2},{1... | collective-permute-start | bytes 196616 | tf_op jit(solution)/shard_map/ppermute | solution.py:371
  25.3 2.2 %collective-permute-start.9 = (f32[64,2560]{1,0:T(8,128)S(1)}, f32[64,2560]{1,0:T(8,128)S(1)}, u32[]{:S(2)}, u32[]{:S(2)}) collective-permute-start(f32[64,2560]{1,0:T(8,128)S(1)} %get-tuple-element.60.refs_7_), channel_id=1, source_target_pairs={{0,1},{1,0},{2,3},{3,2},{4,5},{5,4},{6,7},{7,6},{8,9},{9,8},{10,11... | collective-permute-start | bytes 1966088 | tf_op jit(solution)/shard_map/ppermute | solution.py:371
  27.5 6.9 %collective-permute-start.10 = (f32[64,2560]{1,0:T(8,128)S(1)}, f32[64,2560]{1,0:T(8,128)S(1)}, u32[]{:S(2)}, u32[]{:S(2)}) collective-permute-start(f32[64,2560]{1,0:T(8,128)S(1)} %gate_up_diagonal.1), channel_id=1, source_target_pairs={{0,1},{1,0},{2,3},{3,2},{4,5},{5,4},{6,7},{7,6},{8,9},{9,8},{10,11... | collective-permute-start | bytes 1966088 | tf_op jit(solution)/shard_map/ppermute | solution.py:371
  28.1 6.2 %collective-permute-start.11 = (bf16[64,1280]{1,0:T(8,128)(2,1)S(1)}, bf16[64,1280]{1,0:T(8,128)(2,1)S(1)}, u32[]{:S(2)}, u32[]{:S(2)}) collective-permute-start(bf16[64,1280]{1,0:T(8,128)(2,1)S(1)} %add_convert_fusion.1.refs_6_), channel_id=1, source_target_pairs={{0,2},{1,3},{2,0},{3,1},{4,6},{5,7},{6,4},{7,5},{8,10},{9,11},{10,... | collective-permute-start | bytes 491528 | tf_op jit(solution)/shard_map/ppermute | solution.py:371
  34.4 9.4 %collective-permute-start.12 = (bf16[64,2560]{1,0:T(8,128)(2,1)S(1)}, bf16[64,2560]{1,0:T(8,128)(2,1)S(1)}, u32[]{:S(2)}, u32[]{:S(2)}) collective-permute-start(bf16[64,2560]{1,0:T(8,128)(2,1)S(1)} %add_convert_fusion.refs_6_), channel_id=1, source_target_pairs={{0,2},{1,3},{2,0},{3,1},{4,6},{5,7},{6,4},{7,5},{8,10},{9,11},{10,... | collective-permute-start | bytes 983048 | tf_op jit(solution)/shard_map/ppermute | solution.py:371
  43.8 1.6 %collective-permute-start.13 = (bf16[64,2560]{1,0:T(8,128)(2,1)S(1)}, bf16[64,2560]{1,0:T(8,128)(2,1)S(1)}, u32[]{:S(2)}, u32[]{:S(2)}) collective-permute-start(bf16[64,2560]{1,0:T(8,128)(2,1)S(1)} %get-tuple-element.67), channel_id=1, source_target_pairs={{0,1},{1,0},{2,3},{3,2},{4,5},{5,4},{6,7},{7,6},{8,9},{9,8},{10,11... | collective-permute-start | bytes 983048 | tf_op jit(solution)/shard_map/ppermute | solution.py:371
  45.9 1.7 %collective-permute-start.14 = (bf16[64,2688]{1,0:T(8,128)(2,1)S(1)}, bf16[64,2688]{1,0:T(8,128)(2,1)S(1)}, u32[]{:S(2)}, u32[]{:S(2)}) collective-permute-start(bf16[64,2688]{1,0:T(8,128)(2,1)S(1)} %get-tuple-element.71.refs_0_), channel_id=1, source_target_pairs={{0,1},{1,0},{2,3},{3,2},{4,5},{5,4},{6,7},{7,6},{8,9},{9,8},{10,11... | collective-permute-start | bytes 1032200 | tf_op jit(solution)/shard_map/ppermute | solution.py:371
  46.0 10.3 %collective-permute-start.15 = (bf16[64,2688]{1,0:T(8,128)(2,1)S(1)}, bf16[64,2688]{1,0:T(8,128)(2,1)S(1)}, u32[]{:S(2)}, u32[]{:S(2)}) collective-permute-start(bf16[64,2688]{1,0:T(8,128)(2,1)S(1)} %get-tuple-element.71.refs_0_), channel_id=1, source_target_pairs={{0,2},{1,3},{2,0},{3,1},{4,6},{5,7},{6,4},{7,5},{8,10},{9,11},{10,... | collective-permute-start | bytes 1032200 | tf_op jit(solution)/shard_map/ppermute | solution.py:371
  56.4 4.2 %collective-permute-start.16 = (bf16[64,2688]{1,0:T(8,128)(2,1)S(1)}, bf16[64,2688]{1,0:T(8,128)(2,1)S(1)}, u32[]{:S(2)}, u32[]{:S(2)}) collective-permute-start(bf16[64,2688]{1,0:T(8,128)(2,1)S(1)} %collective-permute-done.15.refs_0_), channel_id=1, source_target_pairs={{0,1},{1,0},{2,3},{3,2},{4,5},{5,4},{6,7},{7,6},{8,9},{9,8},{10,11... | collective-permute-start | bytes 1032200 | tf_op jit(solution)/shard_map/ppermute | solution.py:371
  64.3 6.9 %collective-permute-start.17 = (bf16[16,2176]{1,0:T(8,128)(2,1)S(1)}, bf16[16,2176]{1,0:T(8,128)(2,1)S(1)}, u32[]{:S(2)}, u32[]{:S(2)}) collective-permute-start(bf16[16,2176]{1,0:T(8,128)(2,1)S(1)} %get-tuple-element.80), channel_id=1, source_target_pairs={{0,12},{4,8},{8,4},{12,0},{1,13},{5,9},{9,5},{13,1},{2,14},{6,10},... | collective-permute-start | bytes 208904 | tf_op jit(solution)/shard_map/ppermute | solution.py:371
  68.0 6.1 %collective-permute-start.18 = (bf16[16,2176]{1,0:T(8,128)(2,1)S(1)}, bf16[16,2176]{1,0:T(8,128)(2,1)S(1)}, u32[]{:S(2)}, u32[]{:S(2)}) collective-permute-start(bf16[16,2176]{1,0:T(8,128)(2,1)S(1)} %get-tuple-element.81), channel_id=1, source_target_pairs={{0,8},{4,12},{8,0},{12,4},{1,9},{5,13},{9,1},{13,5},{2,10},{6,14},... | collective-permute-start | bytes 208904 | tf_op jit(solution)/shard_map/ppermute | solution.py:371
  68.0 6.1 %collective-permute-start.19 = (bf16[16,2176]{1,0:T(8,128)(2,1)S(1)}, bf16[16,2176]{1,0:T(8,128)(2,1)S(1)}, u32[]{:S(2)}, u32[]{:S(2)}) collective-permute-start(bf16[16,2176]{1,0:T(8,128)(2,1)S(1)} %get-tuple-element.82), channel_id=1, source_target_pairs={{0,4},{4,0},{8,12},{12,8},{1,5},{5,1},{9,13},{13,9},{2,6},{6,2},{1... | collective-permute-start | bytes 208904 | tf_op jit(solution)/shard_map/ppermute | solution.py:371

commit v6 on v5

--- a/solution.py
+++ b/solution.py
@@ -216,7 +216,7 @@
     size = tokens // pieces
     extra = [] if before is None else [before]
     count = len(steps(share)) * len(pair)
-    n = steps(width)[0][1]
+    n = width // 2 if picks and width % (2 * LANES) == 0 else width
 
     def kernel(index_ref, *refs):
         row_refs, refs = refs[: len(rows)], refs[len(rows) :]

time: 75.3 us -> 74.8 us (level)
  Pallas kernels: 42.8 us -> 42 us
    pallas_call x3, Pallas kernels: 14.9 us -> 14.1 us  [backward(): pl.pallas_call(kernel, in_specs=[SMEM] + [VMEM] * (len(rows) + 1 + len(ex...]
where the time goes in v6:
time: 74.8 us; the launch traced here: 74.6 us
  Pallas kernels  42 us (56%)
  starting transfers between devices  21.2 us (28%)
  waiting for transfers between devices  9.94 us (13%)
  other arithmetic  1.27 us (2%)
    ppermute x20, starting transfers between devices, swap(): return lax.ppermute(x, axis, [(i, i ^ k) for i in range(mesh.shape[axis])])  21.2 us
    pallas_call x3, Pallas kernels, gate_and_up(): pl.pallas_call(kernel, in_specs=[SMEM] + [VMEM] * (len(blocks) + len(give...  14.7 us
    pallas_call x3, Pallas kernels, backward(): pl.pallas_call(kernel, in_specs=[SMEM] + [VMEM] * (len(rows) + 1 + len(ex...  14.1 us
    ppermute x20, waiting for transfers between devices, swap(): return lax.ppermute(x, axis, [(i, i ^ k) for i in range(mesh.shape[axis])])  9.94 us
    pallas_call x1, Pallas kernels, hidden_gradient(): pl.pallas_call(kernel, in_specs=[SMEM] + [VMEM] * (len(blocks) + 1) + [HB...  9.17 us
    pallas_call x1, Pallas kernels, rows_ahead(): pl.pallas_call(kernel, in_specs=[SMEM, HBM], out_specs=VMEM, out_shape=pl...  2.49 us
  transfers between devices with their start and end apart: 20, of which 6 were waited for; matrix products, arithmetic and copies ran while one was open for 0% of the time, Pallas kernels for 50%

profile of v6, /device:TPU:0, one launch (start us, length us, event | category | flops | bytes accessed | tf_op | source)
XLA Modules:
  0.0 74.6 jit_solution(5024994306129809754)
XLA Ops:
  0.0 1.2 %latents.1 = (f32[16,2048]{1,0:T(8,128)S(1)}, f32[16,2048]{1,0:T(8,128)S(1)}, f32[16,1]{1,0:T(8,128)S(1)}, f32[1,2048]{1,0:T(1,128)S(1)}, bf16[16,2048]{1,0:T(8,128)(2,1)S(1)}) custom-call(bf16[16,2048]{1,0:T(8,128)(2,1)} %refs_0_.1, s32[16,2048]{1,0:T(8,128)} %refs_1_.1, f32[16,2048]{1,0:T(8,128)} %refs_2_.1, f32[1,2048]{1,0:T(1,128)} %bitcast.5, ...), custom_call_target="tpu_custom_call" | custom-call | flops 262144 | bytes 589824 | tf_op jit(solution)/shard_map/latents/pallas_call | solution.py:289
  1.2 2.4 %collective-permute-start.2 = (f32[16,1]{1,0:T(8,128)S(1)}, f32[16,1]{1,0:T(8,128)S(1)}, u32[]{:S(2)}, u32[]{:S(2)}) collective-permute-start(f32[16,1]{1,0:T(8,128)S(1)} %get-tuple-element.46), channel_id=1, source_target_pairs={{0,3},{1,2},{2,1},{3,0},{4,7},{5,6},{6,5},{7,4},{8,11},{9,10},{10,... | collective-permute-start | bytes 200 | tf_op jit(solution)/shard_map/ppermute | solution.py:371
  3.6 0.6 collective-permute-start.1
  4.3 0.0 collective-permute-start
  4.3 3.9 %collective-permute-start.5 = (bf16[16,2048]{1,0:T(8,128)(2,1)S(1)}, bf16[16,2048]{1,0:T(8,128)(2,1)S(1)}, u32[]{:S(2)}, u32[]{:S(2)}) collective-permute-start(bf16[16,2048]{1,0:T(8,128)(2,1)S(1)} %get-tuple-element.45.refs_0_), channel_id=1, source_target_pairs={{0,12},{4,8},{8,4},{12,0},{1,13},{5,9},{9,5},{13,1},{2,14},{6,10},... | collective-permute-start | bytes 196616 | tf_op jit(solution)/shard_map/ppermute | solution.py:371
  8.2 0.0 collective-permute-start.4
  8.2 2.5 %rows_ahead.1.refs_4_ = bf16[1280,2048]{1,0:T(8,128)(2,1)S(1)} custom-call(s32[1]{0:T(128)} %bitcast.1.index_ref, bf16[5120,2048]{1,0:T(8,128)(2,1)} %refs_5_.4), custom_call_target="tpu_custom_call" | custom-call | flops 41943040 | bytes 5242880 | tf_op jit(solution)/shard_map/rows_ahead/pallas_call | solution.py:87
  10.7 0.0 collective-permute-done.2
  10.7 0.6 collective-permute-start.3
  11.3 0.0 collective-permute-done.1
  11.3 0.0 collective-permute-done
  11.3 0.1 rsqrt_reduce_fusion
  11.4 0.1 multiply_convert_fusion.refs_0_
  11.5 3.9 %collective-permute-start.8 = (bf16[16,2048]{1,0:T(8,128)(2,1)S(1)}, bf16[16,2048]{1,0:T(8,128)(2,1)S(1)}, u32[]{:S(2)}, u32[]{:S(2)}) collective-permute-start(bf16[16,2048]{1,0:T(8,128)(2,1)S(1)} %multiply_convert_fusion.refs_0_), channel_id=1, source_target_pairs={{0,12},{4,8},{8,4},{12,0},{1,13},{5,9},{9,5},{13,1},{2,14},{6,10},... | collective-permute-start | bytes 196616 | tf_op jit(solution)/shard_map/ppermute | solution.py:371
  15.4 0.0 collective-permute-start.7
  15.4 0.0 collective-permute-done.5.refs_3_
  15.4 0.6 collective-permute-start.6
  16.1 0.0 collective-permute-done.3.refs_1_
  16.1 9.2 %back_hidden.1 = (f32[64,2560]{1,0:T(8,128)S(1)}, f32[64,2560]{1,0:T(8,128)S(1)}, bf16[2,2048,1280]{2,1,0:T(8,128)(2,1)S(1)}) custom-call(s32[1]{0:T(128)} %bitcast.1.index_ref, bf16[16,2048]{1,0:T(8,128)(2,1)S(1)} %get-tuple-element.45.refs_0_, bf16[16,2048]{1,0:T(8,128)(2,1)S(1)} %collective-permute-done.3.refs_1_, ...), custom_call_target="tpu_custom_call" | custom-call | flops 1342177280 | bytes 20971520 | tf_op jit(solution)/shard_map/back_hidden/pallas_call | solution.py:138
  25.2 0.0 collective-permute-done.8.refs_3_
  25.3 0.0 collective-permute-done.7.refs_2_
  25.3 0.1 collective-permute-start.9
  25.4 2.1 %gate_up_diagonal.1 = f32[64,2560]{1,0:T(8,128)S(1)} custom-call(s32[1]{0:T(128)} %bitcast.1.index_ref, bf16[16,2048]{1,0:T(8,128)(2,1)S(1)} %multiply_convert_fusion.refs_0_, bf16[16,2048]{1,0:T(8,128)(2,1)S(1)} %collective-permute-done.6.refs_1_, bf16[16,2048]{1,0:T(8,128)(2,1)S(1)} %collective-permute-done.7.refs_2_, ...), custom_call_target="tpu_custom_call" | custom-call | flops 671088640 | bytes 10485760 | tf_op jit(solution)/shard_map/gate_up_diagonal/pallas_call | solution.py:197
  27.5 0.0 collective-permute-done.9.hidden_near_ref
  27.5 0.6 collective-permute-start.10
  28.1 1.5 %collective-permute-start.11 = (bf16[64,1280]{1,0:T(8,128)(2,1)S(1)}, bf16[64,1280]{1,0:T(8,128)(2,1)S(1)}, u32[]{:S(2)}, u32[]{:S(2)}) collective-permute-start(bf16[64,1280]{1,0:T(8,128)(2,1)S(1)} %add_convert_fusion.1.refs_6_), channel_id=1, source_target_pairs={{0,2},{1,3},{2,0},{3,1},{4,6},{5,7},{6,4},{7,5},{8,10},{9,11},{10,... | collective-permute-start | bytes 491528 | tf_op jit(solution)/shard_map/ppermute | solution.py:371
  29.6 4.7 %gate_up_far.1 = f32[64,2560]{1,0:T(8,128)S(1)} custom-call(s32[1]{0:T(128)} %bitcast.1.index_ref, bf16[16,2048]{1,0:T(8,128)(2,1)S(1)} %multiply_convert_fusion.refs_0_, bf16[16,2048]{1,0:T(8,128)(2,1)S(1)} %collective-permute-done.6.refs_1_, bf16[16,2048]{1,0:T(8,128)(2,1)S(1)} %collective-permute-done.7.refs_2_, ...), custom_call_target="tpu_custom_call" | custom-call | flops 671088640 | bytes 10485760 | tf_op jit(solution)/shard_map/gate_up_far/pallas_call | solution.py:197
  34.3 0.0 collective-permute-done.11.hidden_far_ref
  34.3 0.0 collective-permute-done.10
  34.3 0.1 add_convert_fusion.refs_6_
  34.4 1.4 %collective-permute-start.12 = (bf16[64,2560]{1,0:T(8,128)(2,1)S(1)}, bf16[64,2560]{1,0:T(8,128)(2,1)S(1)}, u32[]{:S(2)}, u32[]{:S(2)}) collective-permute-start(bf16[64,2560]{1,0:T(8,128)(2,1)S(1)} %add_convert_fusion.refs_6_), channel_id=1, source_target_pairs={{0,2},{1,3},{2,0},{3,1},{4,6},{5,7},{6,4},{7,5},{8,10},{9,11},{10,... | collective-permute-start | bytes 983048 | tf_op jit(solution)/shard_map/ppermute | solution.py:371
  35.8 7.8 %gate_up_near_own.1 = (f32[64,2560]{1,0:T(8,128)S(1)}, bf16[64,2560]{1,0:T(8,128)(2,1)S(1)}, bf16[4,2048,1280]{2,1,0:T(8,128)(2,1)S(1)}) custom-call(s32[1]{0:T(128)} %bitcast.1.index_ref, bf16[16,2048]{1,0:T(8,128)(2,1)S(1)} %multiply_convert_fusion.refs_0_, bf16[16,2048]{1,0:T(8,128)(2,1)S(1)} %collective-permute-done.6.refs_1_, ...), custom_call_target="tpu_custom_call" | custom-call | flops 1342177280 | bytes 20971520 | tf_op jit(solution)/shard_map/gate_up_near_own/pallas_call | solution.py:197
  43.7 0.1 collective-permute-done.12.far_ref
  43.8 1.6 %collective-permute-done.13.near_ref = bf16[64,2560]{1,0:T(8,128)(2,1)S(1)} collective-permute-done((bf16[64,2560]{1,0:T(8,128)(2,1)S(1)}, bf16[64,2560]{1,0:T(8,128)(2,1)S(1)}, u32[]{:S(2)}, u32[]{:S(2)}) %collective-permute-start.13) | collective-permute-done | bytes 327712 | tf_op jit(solution)/shard_map/ppermute | solution.py:371
  45.5 0.4 gate.1
  45.9 0.2 collective-permute-start.14
  46.0 0.8 %collective-permute-start.15 = (bf16[64,2688]{1,0:T(8,128)(2,1)S(1)}, bf16[64,2688]{1,0:T(8,128)(2,1)S(1)}, u32[]{:S(2)}, u32[]{:S(2)}) collective-permute-start(bf16[64,2688]{1,0:T(8,128)(2,1)S(1)} %get-tuple-element.71.refs_0_), channel_id=1, source_target_pairs={{0,2},{1,3},{2,0},{3,1},{4,6},{5,7},{6,4},{7,5},{8,10},{9,11},{10,... | collective-permute-start | bytes 1032200 | tf_op jit(solution)/shard_map/ppermute | solution.py:371
  46.8 0.7 collective-permute-done.14.refs_1_
  47.5 6.7 %back_own_near.1 = (f32[64,2176]{1,0:T(8,128)S(1)}, bf16[2,2048,1280]{2,1,0:T(8,128)(2,1)S(1)}) custom-call(s32[1]{0:T(128)} %bitcast.1.index_ref, bf16[64,2688]{1,0:T(8,128)(2,1)S(1)} %get-tuple-element.71.refs_0_, bf16[64,2688]{1,0:T(8,128)(2,1)S(1)} %collective-permute-done.14.refs_1_, bf16[4,2048,1280]{2,1,0:T(8,128)(2,1)S(1)} %get-tuple-element.72.refs_2_, ...), custom_call_target="tpu_custom_call" | custom-call | flops 1342177280 | bytes 20971520 | tf_op jit(solution)/shard_map/back_own_near/pallas_call | solution.py:255
  54.3 2.1 %collective-permute-done.15.refs_0_ = bf16[64,2688]{1,0:T(8,128)(2,1)S(1)} collective-permute-done((bf16[64,2688]{1,0:T(8,128)(2,1)S(1)}, bf16[64,2688]{1,0:T(8,128)(2,1)S(1)}, u32[]{:S(2)}, u32[]{:S(2)}) %collective-permute-start.15) | collective-permute-done | bytes 344096 | tf_op jit(solution)/shard_map/ppermute | solution.py:371
  56.4 4.1 %back_far.1 = (f32[64,2176]{1,0:T(8,128)S(1)}, bf16[2,2048,1280]{2,1,0:T(8,128)(2,1)S(1)}) custom-call(s32[1]{0:T(128)} %bitcast.1.index_ref, bf16[64,2688]{1,0:T(8,128)(2,1)S(1)} %collective-permute-done.15.refs_0_, bf16[2,2048,1280]{2,1,0:T(8,128)(2,1)S(1)} %get-tuple-element.75.refs_1_, f32[64,2176]{1,0:T(8,128)S(1)} %get-tuple-element.76.refs_2_, ...), custom_call_target="tpu_custom_call" | custom-call | flops 671088640 | bytes 10485760 | tf_op jit(solution)/shard_map/back_far/pallas_call | solution.py:255
  60.5 3.3 %back_diagonal.1 = (f32[16,2176]{1,0:T(8,128)S(1)}, bf16[16,2176]{1,0:T(8,128)(2,1)S(1)}, bf16[16,2176]{1,0:T(8,128)(2,1)S(1)}, bf16[16,2176]{1,0:T(8,128)(2,1)S(1)}) custom-call(s32[1]{0:T(128)} %bitcast.1.index_ref, bf16[64,2688]{1,0:T(8,128)(2,1)S(1)} %collective-permute-done.16.refs_0_, bf16[2,2048,1280]{2,1,0:T(8,128)(2,1)S(1)} %get-tuple-element.77.refs_1_, ...), custom_call_target="tpu_custom_call" | custom-call | flops 671088640 | bytes 10485760 | tf_op jit(solution)/shard_map/back_diagonal/pallas_call | solution.py:255
  63.8 3.7 %collective-permute-start.17 = (bf16[16,2176]{1,0:T(8,128)(2,1)S(1)}, bf16[16,2176]{1,0:T(8,128)(2,1)S(1)}, u32[]{:S(2)}, u32[]{:S(2)}) collective-permute-start(bf16[16,2176]{1,0:T(8,128)(2,1)S(1)} %get-tuple-element.80), channel_id=1, source_target_pairs={{0,12},{4,8},{8,4},{12,0},{1,13},{5,9},{9,5},{13,1},{2,14},{6,10},... | collective-permute-start | bytes 208904 | tf_op jit(solution)/shard_map/ppermute | solution.py:371
  67.5 0.8 %collective-permute-start.19 = (bf16[16,2176]{1,0:T(8,128)(2,1)S(1)}, bf16[16,2176]{1,0:T(8,128)(2,1)S(1)}, u32[]{:S(2)}, u32[]{:S(2)}) collective-permute-start(bf16[16,2176]{1,0:T(8,128)(2,1)S(1)} %get-tuple-element.82), channel_id=1, source_target_pairs={{0,4},{4,0},{8,12},{12,8},{1,5},{5,1},{9,13},{13,9},{2,6},{6,2},{1... | collective-permute-start | bytes 208904 | tf_op jit(solution)/shard_map/ppermute | solution.py:371
  68.3 2.5 %collective-permute-done.17 = bf16[16,2176]{1,0:T(8,128)(2,1)S(1)} collective-permute-done((bf16[16,2176]{1,0:T(8,128)(2,1)S(1)}, bf16[16,2176]{1,0:T(8,128)(2,1)S(1)}, u32[]{:S(2)}, u32[]{:S(2)}) %collective-permute-start.17) | collective-permute-done | bytes 69664 | tf_op jit(solution)/shard_map/ppermute | solution.py:371
  70.8 2.9 %collective-permute-done.18 = bf16[16,2176]{1,0:T(8,128)(2,1)S(1)} collective-permute-done((bf16[16,2176]{1,0:T(8,128)(2,1)S(1)}, bf16[16,2176]{1,0:T(8,128)(2,1)S(1)}, u32[]{:S(2)}, u32[]{:S(2)}) %collective-permute-start.18) | collective-permute-done | bytes 69664 | tf_op jit(solution)/shard_map/ppermute | solution.py:371
  73.6 0.2 multiply_reduce_fusion
  73.8 0.8 %multiply_add_fusion = f32[16,2048]{1,0:T(8,128)} fusion(f32[16,2048]{1,0:T(8,128)S(1)} %get-tuple-element.44, f32[16,2176]{1,0:T(8,128)S(1)} %get-tuple-element.79, bf16[16,2048]{1,0:T(8,128)(2,1)S(1)} %get-tuple-element.45.refs_0_, f32[16,2048]{1,0:T(8,128)S(1)} %get-tuple-element.52, bf16[16,2176]{1,0:T(8,128)(2,1)S(1)} %collective-permute-done.19, ...), kind=kLoop, calls=%fused_computation.2 | loop fusion | flops 491520 | bytes 794752 | tf_op jit(solution)/shard_map/add | solution.py:445
  (8 shorter events, 0.1 us)
Async XLA Ops:
  1.2 9.5 %collective-permute-start.2 = (f32[16,1]{1,0:T(8,128)S(1)}, f32[16,1]{1,0:T(8,128)S(1)}, u32[]{:S(2)}, u32[]{:S(2)}) collective-permute-start(f32[16,1]{1,0:T(8,128)S(1)} %get-tuple-element.46), channel_id=1, source_target_pairs={{0,3},{1,2},{2,1},{3,0},{4,7},{5,6},{6,5},{7,4},{8,11},{9,10},{10,... | collective-permute-start | bytes 200 | tf_op jit(solution)/shard_map/ppermute | solution.py:371
  3.6 7.7 %collective-permute-start.1 = (f32[16,1]{1,0:T(8,128)S(1)}, f32[16,1]{1,0:T(8,128)S(1)}, u32[]{:S(2)}, u32[]{:S(2)}) collective-permute-start(f32[16,1]{1,0:T(8,128)S(1)} %get-tuple-element.46), channel_id=1, source_target_pairs={{0,2},{1,3},{2,0},{3,1},{4,6},{5,7},{6,4},{7,5},{8,10},{9,11},{10,... | collective-permute-start | bytes 200 | tf_op jit(solution)/shard_map/ppermute | solution.py:371
  4.3 7.0 %collective-permute-start = (f32[16,1]{1,0:T(8,128)S(1)}, f32[16,1]{1,0:T(8,128)S(1)}, u32[]{:S(2)}, u32[]{:S(2)}) collective-permute-start(f32[16,1]{1,0:T(8,128)S(1)} %get-tuple-element.46), channel_id=1, source_target_pairs={{0,1},{1,0},{2,3},{3,2},{4,5},{5,4},{6,7},{7,6},{8,9},{9,8},{10,11... | collective-permute-start | bytes 200 | tf_op jit(solution)/shard_map/ppermute | solution.py:371
  4.3 11.1 %collective-permute-start.5 = (bf16[16,2048]{1,0:T(8,128)(2,1)S(1)}, bf16[16,2048]{1,0:T(8,128)(2,1)S(1)}, u32[]{:S(2)}, u32[]{:S(2)}) collective-permute-start(bf16[16,2048]{1,0:T(8,128)(2,1)S(1)} %get-tuple-element.45.refs_0_), channel_id=1, source_target_pairs={{0,12},{4,8},{8,4},{12,0},{1,13},{5,9},{9,5},{13,1},{2,14},{6,10},... | collective-permute-start | bytes 196616 | tf_op jit(solution)/shard_map/ppermute | solution.py:371
  8.2 7.9 %collective-permute-start.4 = (bf16[16,2048]{1,0:T(8,128)(2,1)S(1)}, bf16[16,2048]{1,0:T(8,128)(2,1)S(1)}, u32[]{:S(2)}, u32[]{:S(2)}) collective-permute-start(bf16[16,2048]{1,0:T(8,128)(2,1)S(1)} %get-tuple-element.45.refs_0_), channel_id=1, source_target_pairs={{0,8},{4,12},{8,0},{12,4},{1,9},{5,13},{9,1},{13,5},{2,10},{6,14},... | collective-permute-start | bytes 196616 | tf_op jit(solution)/shard_map/ppermute | solution.py:371
  10.7 5.4 %collective-permute-start.3 = (bf16[16,2048]{1,0:T(8,128)(2,1)S(1)}, bf16[16,2048]{1,0:T(8,128)(2,1)S(1)}, u32[]{:S(2)}, u32[]{:S(2)}) collective-permute-start(bf16[16,2048]{1,0:T(8,128)(2,1)S(1)} %get-tuple-element.45.refs_0_), channel_id=1, source_target_pairs={{0,4},{4,0},{8,12},{12,8},{1,5},{5,1},{9,13},{13,9},{2,6},{6,2},{1... | collective-permute-start | bytes 196616 | tf_op jit(solution)/shard_map/ppermute | solution.py:371
  11.5 13.7 %collective-permute-start.8 = (bf16[16,2048]{1,0:T(8,128)(2,1)S(1)}, bf16[16,2048]{1,0:T(8,128)(2,1)S(1)}, u32[]{:S(2)}, u32[]{:S(2)}) collective-permute-start(bf16[16,2048]{1,0:T(8,128)(2,1)S(1)} %multiply_convert_fusion.refs_0_), channel_id=1, source_target_pairs={{0,12},{4,8},{8,4},{12,0},{1,13},{5,9},{9,5},{13,1},{2,14},{6,10},... | collective-permute-start | bytes 196616 | tf_op jit(solution)/shard_map/ppermute | solution.py:371
  15.4 9.8 %collective-permute-start.7 = (bf16[16,2048]{1,0:T(8,128)(2,1)S(1)}, bf16[16,2048]{1,0:T(8,128)(2,1)S(1)}, u32[]{:S(2)}, u32[]{:S(2)}) collective-permute-start(bf16[16,2048]{1,0:T(8,128)(2,1)S(1)} %multiply_convert_fusion.refs_0_), channel_id=1, source_target_pairs={{0,8},{4,12},{8,0},{12,4},{1,9},{5,13},{9,1},{13,5},{2,10},{6,14},... | collective-permute-start | bytes 196616 | tf_op jit(solution)/shard_map/ppermute | solution.py:371
  15.4 9.8 %collective-permute-start.6 = (bf16[16,2048]{1,0:T(8,128)(2,1)S(1)}, bf16[16,2048]{1,0:T(8,128)(2,1)S(1)}, u32[]{:S(2)}, u32[]{:S(2)}) collective-permute-start(bf16[16,2048]{1,0:T(8,128)(2,1)S(1)} %multiply_convert_fusion.refs_0_), channel_id=1, source_target_pairs={{0,4},{4,0},{8,12},{12,8},{1,5},{5,1},{9,13},{13,9},{2,6},{6,2},{1... | collective-permute-start | bytes 196616 | tf_op jit(solution)/shard_map/ppermute | solution.py:371
  25.3 2.2 %collective-permute-start.9 = (f32[64,2560]{1,0:T(8,128)S(1)}, f32[64,2560]{1,0:T(8,128)S(1)}, u32[]{:S(2)}, u32[]{:S(2)}) collective-permute-start(f32[64,2560]{1,0:T(8,128)S(1)} %get-tuple-element.60.refs_7_), channel_id=1, source_target_pairs={{0,1},{1,0},{2,3},{3,2},{4,5},{5,4},{6,7},{7,6},{8,9},{9,8},{10,11... | collective-permute-start | bytes 1966088 | tf_op jit(solution)/shard_map/ppermute | solution.py:371
  27.5 6.9 %collective-permute-start.10 = (f32[64,2560]{1,0:T(8,128)S(1)}, f32[64,2560]{1,0:T(8,128)S(1)}, u32[]{:S(2)}, u32[]{:S(2)}) collective-permute-start(f32[64,2560]{1,0:T(8,128)S(1)} %gate_up_diagonal.1), channel_id=1, source_target_pairs={{0,1},{1,0},{2,3},{3,2},{4,5},{5,4},{6,7},{7,6},{8,9},{9,8},{10,11... | collective-permute-start | bytes 1966088 | tf_op jit(solution)/shard_map/ppermute | solution.py:371
  28.1 6.2 %collective-permute-start.11 = (bf16[64,1280]{1,0:T(8,128)(2,1)S(1)}, bf16[64,1280]{1,0:T(8,128)(2,1)S(1)}, u32[]{:S(2)}, u32[]{:S(2)}) collective-permute-start(bf16[64,1280]{1,0:T(8,128)(2,1)S(1)} %add_convert_fusion.1.refs_6_), channel_id=1, source_target_pairs={{0,2},{1,3},{2,0},{3,1},{4,6},{5,7},{6,4},{7,5},{8,10},{9,11},{10,... | collective-permute-start | bytes 491528 | tf_op jit(solution)/shard_map/ppermute | solution.py:371
  34.4 9.4 %collective-permute-start.12 = (bf16[64,2560]{1,0:T(8,128)(2,1)S(1)}, bf16[64,2560]{1,0:T(8,128)(2,1)S(1)}, u32[]{:S(2)}, u32[]{:S(2)}) collective-permute-start(bf16[64,2560]{1,0:T(8,128)(2,1)S(1)} %add_convert_fusion.refs_6_), channel_id=1, source_target_pairs={{0,2},{1,3},{2,0},{3,1},{4,6},{5,7},{6,4},{7,5},{8,10},{9,11},{10,... | collective-permute-start | bytes 983048 | tf_op jit(solution)/shard_map/ppermute | solution.py:371
  43.8 1.6 %collective-permute-start.13 = (bf16[64,2560]{1,0:T(8,128)(2,1)S(1)}, bf16[64,2560]{1,0:T(8,128)(2,1)S(1)}, u32[]{:S(2)}, u32[]{:S(2)}) collective-permute-start(bf16[64,2560]{1,0:T(8,128)(2,1)S(1)} %get-tuple-element.67), channel_id=1, source_target_pairs={{0,1},{1,0},{2,3},{3,2},{4,5},{5,4},{6,7},{7,6},{8,9},{9,8},{10,11... | collective-permute-start | bytes 983048 | tf_op jit(solution)/shard_map/ppermute | solution.py:371
  45.9 1.7 %collective-permute-start.14 = (bf16[64,2688]{1,0:T(8,128)(2,1)S(1)}, bf16[64,2688]{1,0:T(8,128)(2,1)S(1)}, u32[]{:S(2)}, u32[]{:S(2)}) collective-permute-start(bf16[64,2688]{1,0:T(8,128)(2,1)S(1)} %get-tuple-element.71.refs_0_), channel_id=1, source_target_pairs={{0,1},{1,0},{2,3},{3,2},{4,5},{5,4},{6,7},{7,6},{8,9},{9,8},{10,11... | collective-permute-start | bytes 1032200 | tf_op jit(solution)/shard_map/ppermute | solution.py:371
  46.0 10.3 %collective-permute-start.15 = (bf16[64,2688]{1,0:T(8,128)(2,1)S(1)}, bf16[64,2688]{1,0:T(8,128)(2,1)S(1)}, u32[]{:S(2)}, u32[]{:S(2)}) collective-permute-start(bf16[64,2688]{1,0:T(8,128)(2,1)S(1)} %get-tuple-element.71.refs_0_), channel_id=1, source_target_pairs={{0,2},{1,3},{2,0},{3,1},{4,6},{5,7},{6,4},{7,5},{8,10},{9,11},{10,... | collective-permute-start | bytes 1032200 | tf_op jit(solution)/shard_map/ppermute | solution.py:371
  56.4 4.2 %collective-permute-start.16 = (bf16[64,2688]{1,0:T(8,128)(2,1)S(1)}, bf16[64,2688]{1,0:T(8,128)(2,1)S(1)}, u32[]{:S(2)}, u32[]{:S(2)}) collective-permute-start(bf16[64,2688]{1,0:T(8,128)(2,1)S(1)} %collective-permute-done.15.refs_0_), channel_id=1, source_target_pairs={{0,1},{1,0},{2,3},{3,2},{4,5},{5,4},{6,7},{7,6},{8,9},{9,8},{10,11... | collective-permute-start | bytes 1032200 | tf_op jit(solution)/shard_map/ppermute | solution.py:371
  63.8 6.9 %collective-permute-start.17 = (bf16[16,2176]{1,0:T(8,128)(2,1)S(1)}, bf16[16,2176]{1,0:T(8,128)(2,1)S(1)}, u32[]{:S(2)}, u32[]{:S(2)}) collective-permute-start(bf16[16,2176]{1,0:T(8,128)(2,1)S(1)} %get-tuple-element.80), channel_id=1, source_target_pairs={{0,12},{4,8},{8,4},{12,0},{1,13},{5,9},{9,5},{13,1},{2,14},{6,10},... | collective-permute-start | bytes 208904 | tf_op jit(solution)/shard_map/ppermute | solution.py:371
  67.5 6.1 %collective-permute-start.18 = (bf16[16,2176]{1,0:T(8,128)(2,1)S(1)}, bf16[16,2176]{1,0:T(8,128)(2,1)S(1)}, u32[]{:S(2)}, u32[]{:S(2)}) collective-permute-start(bf16[16,2176]{1,0:T(8,128)(2,1)S(1)} %get-tuple-element.81), channel_id=1, source_target_pairs={{0,8},{4,12},{8,0},{12,4},{1,9},{5,13},{9,1},{13,5},{2,10},{6,14},... | collective-permute-start | bytes 208904 | tf_op jit(solution)/shard_map/ppermute | solution.py:371
  67.5 6.1 %collective-permute-start.19 = (bf16[16,2176]{1,0:T(8,128)(2,1)S(1)}, bf16[16,2176]{1,0:T(8,128)(2,1)S(1)}, u32[]{:S(2)}, u32[]{:S(2)}) collective-permute-start(bf16[16,2176]{1,0:T(8,128)(2,1)S(1)} %get-tuple-element.82), channel_id=1, source_target_pairs={{0,4},{4,0},{8,12},{12,8},{1,5},{5,1},{9,13},{13,9},{2,6},{6,2},{1... | collective-permute-start | bytes 208904 | tf_op jit(solution)/shard_map/ppermute | solution.py:371

commit v7 on v6

--- a/solution.py
+++ b/solution.py
@@ -176,7 +176,7 @@
             copy.start()
         for p, block in enumerate(block_refs):
             rows_ref[p * size : (p + 1) * size, :] = block[...]
-        n = steps(share)[0][1]
+        n = steps(share)[0][1] if picks else share
         for held_ref, out in zip(held_refs, out_refs):
 
             @pl.loop(0, share // n)

time: 74.8 us -> 74.7 us (level)
  transfers between devices with their start and end apart: 20 -> 20, of which waited for: 6 -> 7; matrix products, arithmetic and copies ran while one was open for 0% -> 0% of each run, Pallas kernels for 50% -> 50%
where the time goes in v7:
time: 74.7 us; the launch traced here: 74.5 us
  Pallas kernels  42 us (56%)
  starting transfers between devices  21.2 us (28%)
  waiting for transfers between devices  9.91 us (13%)
  other arithmetic  1.27 us (2%)
    ppermute x20, starting transfers between devices, swap(): return lax.ppermute(x, axis, [(i, i ^ k) for i in range(mesh.shape[axis])])  21.2 us
    pallas_call x3, Pallas kernels, gate_and_up(): pl.pallas_call(kernel, in_specs=[SMEM] + [VMEM] * (len(blocks) + len(give...  14.5 us
    pallas_call x3, Pallas kernels, backward(): pl.pallas_call(kernel, in_specs=[SMEM] + [VMEM] * (len(rows) + 1 + len(ex...  14.2 us
    ppermute x20, waiting for transfers between devices, swap(): return lax.ppermute(x, axis, [(i, i ^ k) for i in range(mesh.shape[axis])])  9.91 us
    pallas_call x1, Pallas kernels, hidden_gradient(): pl.pallas_call(kernel, in_specs=[SMEM] + [VMEM] * (len(blocks) + 1) + [HB...  9.17 us
    pallas_call x1, Pallas kernels, rows_ahead(): pl.pallas_call(kernel, in_specs=[SMEM, HBM], out_specs=VMEM, out_shape=pl...  2.49 us
  transfers between devices with their start and end apart: 20, of which 7 were waited for; matrix products, arithmetic and copies ran while one was open for 0% of the time, Pallas kernels for 50%

profile of v7, /device:TPU:0, one launch (start us, length us, event | category | flops | bytes accessed | tf_op | source)
XLA Modules:
  0.0 74.5 jit_solution(13976026684861979056)
XLA Ops:
  0.0 1.2 %latents.1 = (f32[16,2048]{1,0:T(8,128)S(1)}, f32[16,2048]{1,0:T(8,128)S(1)}, f32[16,1]{1,0:T(8,128)S(1)}, f32[1,2048]{1,0:T(1,128)S(1)}, bf16[16,2048]{1,0:T(8,128)(2,1)S(1)}) custom-call(bf16[16,2048]{1,0:T(8,128)(2,1)} %refs_0_.1, s32[16,2048]{1,0:T(8,128)} %refs_1_.1, f32[16,2048]{1,0:T(8,128)} %refs_2_.1, f32[1,2048]{1,0:T(1,128)} %bitcast.5, ...), custom_call_target="tpu_custom_call" | custom-call | flops 262144 | bytes 589824 | tf_op jit(solution)/shard_map/latents/pallas_call | solution.py:289
  1.2 2.4 %collective-permute-start.2 = (f32[16,1]{1,0:T(8,128)S(1)}, f32[16,1]{1,0:T(8,128)S(1)}, u32[]{:S(2)}, u32[]{:S(2)}) collective-permute-start(f32[16,1]{1,0:T(8,128)S(1)} %get-tuple-element.46), channel_id=1, source_target_pairs={{0,3},{1,2},{2,1},{3,0},{4,7},{5,6},{6,5},{7,4},{8,11},{9,10},{10,... | collective-permute-start | bytes 200 | tf_op jit(solution)/shard_map/ppermute | solution.py:371
  3.6 0.6 collective-permute-start.1
  4.3 0.0 collective-permute-start
  4.3 3.9 %collective-permute-start.5 = (bf16[16,2048]{1,0:T(8,128)(2,1)S(1)}, bf16[16,2048]{1,0:T(8,128)(2,1)S(1)}, u32[]{:S(2)}, u32[]{:S(2)}) collective-permute-start(bf16[16,2048]{1,0:T(8,128)(2,1)S(1)} %get-tuple-element.45.refs_0_), channel_id=1, source_target_pairs={{0,12},{4,8},{8,4},{12,0},{1,13},{5,9},{9,5},{13,1},{2,14},{6,10},... | collective-permute-start | bytes 196616 | tf_op jit(solution)/shard_map/ppermute | solution.py:371
  8.2 0.0 collective-permute-start.4
  8.2 2.5 %rows_ahead.1.refs_4_ = bf16[1280,2048]{1,0:T(8,128)(2,1)S(1)} custom-call(s32[1]{0:T(128)} %bitcast.1.index_ref, bf16[5120,2048]{1,0:T(8,128)(2,1)} %refs_5_.4), custom_call_target="tpu_custom_call" | custom-call | flops 41943040 | bytes 5242880 | tf_op jit(solution)/shard_map/rows_ahead/pallas_call | solution.py:87
  10.7 0.0 collective-permute-done.2
  10.7 0.6 collective-permute-start.3
  11.3 0.0 collective-permute-done.1
  11.3 0.0 collective-permute-done
  11.3 0.1 rsqrt_reduce_fusion
  11.4 0.1 multiply_convert_fusion.refs_0_
  11.5 3.9 %collective-permute-start.8 = (bf16[16,2048]{1,0:T(8,128)(2,1)S(1)}, bf16[16,2048]{1,0:T(8,128)(2,1)S(1)}, u32[]{:S(2)}, u32[]{:S(2)}) collective-permute-start(bf16[16,2048]{1,0:T(8,128)(2,1)S(1)} %multiply_convert_fusion.refs_0_), channel_id=1, source_target_pairs={{0,12},{4,8},{8,4},{12,0},{1,13},{5,9},{9,5},{13,1},{2,14},{6,10},... | collective-permute-start | bytes 196616 | tf_op jit(solution)/shard_map/ppermute | solution.py:371
  15.4 0.0 collective-permute-start.7
  15.4 0.0 collective-permute-done.5.refs_3_
  15.4 0.6 collective-permute-start.6
  16.1 0.0 collective-permute-done.3.refs_1_
  16.1 9.2 %back_hidden.1 = (f32[64,2560]{1,0:T(8,128)S(1)}, f32[64,2560]{1,0:T(8,128)S(1)}, bf16[2,2048,1280]{2,1,0:T(8,128)(2,1)S(1)}) custom-call(s32[1]{0:T(128)} %bitcast.1.index_ref, bf16[16,2048]{1,0:T(8,128)(2,1)S(1)} %get-tuple-element.45.refs_0_, bf16[16,2048]{1,0:T(8,128)(2,1)S(1)} %collective-permute-done.3.refs_1_, ...), custom_call_target="tpu_custom_call" | custom-call | flops 1342177280 | bytes 20971520 | tf_op jit(solution)/shard_map/back_hidden/pallas_call | solution.py:138
  25.2 0.0 collective-permute-done.8.refs_3_
  25.3 0.0 collective-permute-done.7.refs_2_
  25.3 0.1 collective-permute-start.9
  25.4 1.9 %gate_up_diagonal.1 = f32[64,2560]{1,0:T(8,128)S(1)} custom-call(s32[1]{0:T(128)} %bitcast.1.index_ref, bf16[16,2048]{1,0:T(8,128)(2,1)S(1)} %multiply_convert_fusion.refs_0_, bf16[16,2048]{1,0:T(8,128)(2,1)S(1)} %collective-permute-done.6.refs_1_, bf16[16,2048]{1,0:T(8,128)(2,1)S(1)} %collective-permute-done.7.refs_2_, ...), custom_call_target="tpu_custom_call" | custom-call | flops 671088640 | bytes 10485760 | tf_op jit(solution)/shard_map/gate_up_diagonal/pallas_call | solution.py:197
  27.3 0.1 collective-permute-done.9.hidden_near_ref
  27.4 0.4 collective-permute-start.10
  27.9 1.5 %collective-permute-start.11 = (bf16[64,1280]{1,0:T(8,128)(2,1)S(1)}, bf16[64,1280]{1,0:T(8,128)(2,1)S(1)}, u32[]{:S(2)}, u32[]{:S(2)}) collective-permute-start(bf16[64,1280]{1,0:T(8,128)(2,1)S(1)} %add_convert_fusion.1.refs_6_), channel_id=1, source_target_pairs={{0,2},{1,3},{2,0},{3,1},{4,6},{5,7},{6,4},{7,5},{8,10},{9,11},{10,... | collective-permute-start | bytes 491528 | tf_op jit(solution)/shard_map/ppermute | solution.py:371
  29.4 4.7 %gate_up_far.1 = f32[64,2560]{1,0:T(8,128)S(1)} custom-call(s32[1]{0:T(128)} %bitcast.1.index_ref, bf16[16,2048]{1,0:T(8,128)(2,1)S(1)} %multiply_convert_fusion.refs_0_, bf16[16,2048]{1,0:T(8,128)(2,1)S(1)} %collective-permute-done.6.refs_1_, bf16[16,2048]{1,0:T(8,128)(2,1)S(1)} %collective-permute-done.7.refs_2_, ...), custom_call_target="tpu_custom_call" | custom-call | flops 671088640 | bytes 10485760 | tf_op jit(solution)/shard_map/gate_up_far/pallas_call | solution.py:197
  34.1 0.0 collective-permute-done.11.hidden_far_ref
  34.2 0.1 add_convert_fusion.refs_6_
  34.2 1.5 %collective-permute-start.12 = (bf16[64,2560]{1,0:T(8,128)(2,1)S(1)}, bf16[64,2560]{1,0:T(8,128)(2,1)S(1)}, u32[]{:S(2)}, u32[]{:S(2)}) collective-permute-start(bf16[64,2560]{1,0:T(8,128)(2,1)S(1)} %add_convert_fusion.refs_6_), channel_id=1, source_target_pairs={{0,2},{1,3},{2,0},{3,1},{4,6},{5,7},{6,4},{7,5},{8,10},{9,11},{10,... | collective-permute-start | bytes 983048 | tf_op jit(solution)/shard_map/ppermute | solution.py:371
  35.7 7.9 %gate_up_near_own.1 = (f32[64,2560]{1,0:T(8,128)S(1)}, bf16[64,2560]{1,0:T(8,128)(2,1)S(1)}, bf16[4,2048,1280]{2,1,0:T(8,128)(2,1)S(1)}) custom-call(s32[1]{0:T(128)} %bitcast.1.index_ref, bf16[16,2048]{1,0:T(8,128)(2,1)S(1)} %multiply_convert_fusion.refs_0_, bf16[16,2048]{1,0:T(8,128)(2,1)S(1)} %collective-permute-done.6.refs_1_, ...), custom_call_target="tpu_custom_call" | custom-call | flops 1342177280 | bytes 20971520 | tf_op jit(solution)/shard_map/gate_up_near_own/pallas_call | solution.py:197
  43.6 0.1 collective-permute-done.12.far_ref
  43.7 0.0 collective-permute-start.13
  43.7 1.6 %collective-permute-done.13.near_ref = bf16[64,2560]{1,0:T(8,128)(2,1)S(1)} collective-permute-done((bf16[64,2560]{1,0:T(8,128)(2,1)S(1)}, bf16[64,2560]{1,0:T(8,128)(2,1)S(1)}, u32[]{:S(2)}, u32[]{:S(2)}) %collective-permute-start.13) | collective-permute-done | bytes 327712 | tf_op jit(solution)/shard_map/ppermute | solution.py:371
  45.4 0.4 gate.1
  45.8 0.2 collective-permute-start.14
  45.9 0.9 %collective-permute-start.15 = (bf16[64,2688]{1,0:T(8,128)(2,1)S(1)}, bf16[64,2688]{1,0:T(8,128)(2,1)S(1)}, u32[]{:S(2)}, u32[]{:S(2)}) collective-permute-start(bf16[64,2688]{1,0:T(8,128)(2,1)S(1)} %get-tuple-element.71.refs_0_), channel_id=1, source_target_pairs={{0,2},{1,3},{2,0},{3,1},{4,6},{5,7},{6,4},{7,5},{8,10},{9,11},{10,... | collective-permute-start | bytes 1032200 | tf_op jit(solution)/shard_map/ppermute | solution.py:371
  46.8 0.6 collective-permute-done.14.refs_1_
  47.4 6.8 %back_own_near.1 = (f32[64,2176]{1,0:T(8,128)S(1)}, bf16[2,2048,1280]{2,1,0:T(8,128)(2,1)S(1)}) custom-call(s32[1]{0:T(128)} %bitcast.1.index_ref, bf16[64,2688]{1,0:T(8,128)(2,1)S(1)} %get-tuple-element.71.refs_0_, bf16[64,2688]{1,0:T(8,128)(2,1)S(1)} %collective-permute-done.14.refs_1_, bf16[4,2048,1280]{2,1,0:T(8,128)(2,1)S(1)} %get-tuple-element.72.refs_2_, ...), custom_call_target="tpu_custom_call" | custom-call | flops 1342177280 | bytes 20971520 | tf_op jit(solution)/shard_map/back_own_near/pallas_call | solution.py:255
  54.3 2.0 %collective-permute-done.15.refs_0_ = bf16[64,2688]{1,0:T(8,128)(2,1)S(1)} collective-permute-done((bf16[64,2688]{1,0:T(8,128)(2,1)S(1)}, bf16[64,2688]{1,0:T(8,128)(2,1)S(1)}, u32[]{:S(2)}, u32[]{:S(2)}) %collective-permute-start.15) | collective-permute-done | bytes 344096 | tf_op jit(solution)/shard_map/ppermute | solution.py:371
  56.3 4.1 %back_far.1 = (f32[64,2176]{1,0:T(8,128)S(1)}, bf16[2,2048,1280]{2,1,0:T(8,128)(2,1)S(1)}) custom-call(s32[1]{0:T(128)} %bitcast.1.index_ref, bf16[64,2688]{1,0:T(8,128)(2,1)S(1)} %collective-permute-done.15.refs_0_, bf16[2,2048,1280]{2,1,0:T(8,128)(2,1)S(1)} %get-tuple-element.75.refs_1_, f32[64,2176]{1,0:T(8,128)S(1)} %get-tuple-element.76.refs_2_, ...), custom_call_target="tpu_custom_call" | custom-call | flops 671088640 | bytes 10485760 | tf_op jit(solution)/shard_map/back_far/pallas_call | solution.py:255
  60.4 3.3 %back_diagonal.1 = (f32[16,2176]{1,0:T(8,128)S(1)}, bf16[16,2176]{1,0:T(8,128)(2,1)S(1)}, bf16[16,2176]{1,0:T(8,128)(2,1)S(1)}, bf16[16,2176]{1,0:T(8,128)(2,1)S(1)}) custom-call(s32[1]{0:T(128)} %bitcast.1.index_ref, bf16[64,2688]{1,0:T(8,128)(2,1)S(1)} %collective-permute-done.16.refs_0_, bf16[2,2048,1280]{2,1,0:T(8,128)(2,1)S(1)} %get-tuple-element.77.refs_1_, ...), custom_call_target="tpu_custom_call" | custom-call | flops 671088640 | bytes 10485760 | tf_op jit(solution)/shard_map/back_diagonal/pallas_call | solution.py:255
  63.7 3.7 %collective-permute-start.17 = (bf16[16,2176]{1,0:T(8,128)(2,1)S(1)}, bf16[16,2176]{1,0:T(8,128)(2,1)S(1)}, u32[]{:S(2)}, u32[]{:S(2)}) collective-permute-start(bf16[16,2176]{1,0:T(8,128)(2,1)S(1)} %get-tuple-element.80), channel_id=1, source_target_pairs={{0,12},{4,8},{8,4},{12,0},{1,13},{5,9},{9,5},{13,1},{2,14},{6,10},... | collective-permute-start | bytes 208904 | tf_op jit(solution)/shard_map/ppermute | solution.py:371
  67.4 0.8 %collective-permute-start.19 = (bf16[16,2176]{1,0:T(8,128)(2,1)S(1)}, bf16[16,2176]{1,0:T(8,128)(2,1)S(1)}, u32[]{:S(2)}, u32[]{:S(2)}) collective-permute-start(bf16[16,2176]{1,0:T(8,128)(2,1)S(1)} %get-tuple-element.82), channel_id=1, source_target_pairs={{0,4},{4,0},{8,12},{12,8},{1,5},{5,1},{9,13},{13,9},{2,6},{6,2},{1... | collective-permute-start | bytes 208904 | tf_op jit(solution)/shard_map/ppermute | solution.py:371
  68.2 2.5 %collective-permute-done.17 = bf16[16,2176]{1,0:T(8,128)(2,1)S(1)} collective-permute-done((bf16[16,2176]{1,0:T(8,128)(2,1)S(1)}, bf16[16,2176]{1,0:T(8,128)(2,1)S(1)}, u32[]{:S(2)}, u32[]{:S(2)}) %collective-permute-start.17) | collective-permute-done | bytes 69664 | tf_op jit(solution)/shard_map/ppermute | solution.py:371
  70.7 2.9 %collective-permute-done.18 = bf16[16,2176]{1,0:T(8,128)(2,1)S(1)} collective-permute-done((bf16[16,2176]{1,0:T(8,128)(2,1)S(1)}, bf16[16,2176]{1,0:T(8,128)(2,1)S(1)}, u32[]{:S(2)}, u32[]{:S(2)}) %collective-permute-start.18) | collective-permute-done | bytes 69664 | tf_op jit(solution)/shard_map/ppermute | solution.py:371
  73.5 0.2 multiply_reduce_fusion
  73.7 0.8 %multiply_add_fusion = f32[16,2048]{1,0:T(8,128)} fusion(f32[16,2048]{1,0:T(8,128)S(1)} %get-tuple-element.44, f32[16,2176]{1,0:T(8,128)S(1)} %get-tuple-element.79, bf16[16,2048]{1,0:T(8,128)(2,1)S(1)} %get-tuple-element.45.refs_0_, f32[16,2048]{1,0:T(8,128)S(1)} %get-tuple-element.52, bf16[16,2176]{1,0:T(8,128)(2,1)S(1)} %collective-permute-done.19, ...), kind=kLoop, calls=%fused_computation.2 | loop fusion | flops 491520 | bytes 794752 | tf_op jit(solution)/shard_map/add | solution.py:445
  (8 shorter events, 0.1 us)
Async XLA Ops:
  1.2 9.5 %collective-permute-start.2 = (f32[16,1]{1,0:T(8,128)S(1)}, f32[16,1]{1,0:T(8,128)S(1)}, u32[]{:S(2)}, u32[]{:S(2)}) collective-permute-start(f32[16,1]{1,0:T(8,128)S(1)} %get-tuple-element.46), channel_id=1, source_target_pairs={{0,3},{1,2},{2,1},{3,0},{4,7},{5,6},{6,5},{7,4},{8,11},{9,10},{10,... | collective-permute-start | bytes 200 | tf_op jit(solution)/shard_map/ppermute | solution.py:371
  3.6 7.7 %collective-permute-start.1 = (f32[16,1]{1,0:T(8,128)S(1)}, f32[16,1]{1,0:T(8,128)S(1)}, u32[]{:S(2)}, u32[]{:S(2)}) collective-permute-start(f32[16,1]{1,0:T(8,128)S(1)} %get-tuple-element.46), channel_id=1, source_target_pairs={{0,2},{1,3},{2,0},{3,1},{4,6},{5,7},{6,4},{7,5},{8,10},{9,11},{10,... | collective-permute-start | bytes 200 | tf_op jit(solution)/shard_map/ppermute | solution.py:371
  4.3 7.0 %collective-permute-start = (f32[16,1]{1,0:T(8,128)S(1)}, f32[16,1]{1,0:T(8,128)S(1)}, u32[]{:S(2)}, u32[]{:S(2)}) collective-permute-start(f32[16,1]{1,0:T(8,128)S(1)} %get-tuple-element.46), channel_id=1, source_target_pairs={{0,1},{1,0},{2,3},{3,2},{4,5},{5,4},{6,7},{7,6},{8,9},{9,8},{10,11... | collective-permute-start | bytes 200 | tf_op jit(solution)/shard_map/ppermute | solution.py:371
  4.3 11.1 %collective-permute-start.5 = (bf16[16,2048]{1,0:T(8,128)(2,1)S(1)}, bf16[16,2048]{1,0:T(8,128)(2,1)S(1)}, u32[]{:S(2)}, u32[]{:S(2)}) collective-permute-start(bf16[16,2048]{1,0:T(8,128)(2,1)S(1)} %get-tuple-element.45.refs_0_), channel_id=1, source_target_pairs={{0,12},{4,8},{8,4},{12,0},{1,13},{5,9},{9,5},{13,1},{2,14},{6,10},... | collective-permute-start | bytes 196616 | tf_op jit(solution)/shard_map/ppermute | solution.py:371
  8.2 7.9 %collective-permute-start.4 = (bf16[16,2048]{1,0:T(8,128)(2,1)S(1)}, bf16[16,2048]{1,0:T(8,128)(2,1)S(1)}, u32[]{:S(2)}, u32[]{:S(2)}) collective-permute-start(bf16[16,2048]{1,0:T(8,128)(2,1)S(1)} %get-tuple-element.45.refs_0_), channel_id=1, source_target_pairs={{0,8},{4,12},{8,0},{12,4},{1,9},{5,13},{9,1},{13,5},{2,10},{6,14},... | collective-permute-start | bytes 196616 | tf_op jit(solution)/shard_map/ppermute | solution.py:371
  10.7 5.4 %collective-permute-start.3 = (bf16[16,2048]{1,0:T(8,128)(2,1)S(1)}, bf16[16,2048]{1,0:T(8,128)(2,1)S(1)}, u32[]{:S(2)}, u32[]{:S(2)}) collective-permute-start(bf16[16,2048]{1,0:T(8,128)(2,1)S(1)} %get-tuple-element.45.refs_0_), channel_id=1, source_target_pairs={{0,4},{4,0},{8,12},{12,8},{1,5},{5,1},{9,13},{13,9},{2,6},{6,2},{1... | collective-permute-start | bytes 196616 | tf_op jit(solution)/shard_map/ppermute | solution.py:371
  11.5 13.7 %collective-permute-start.8 = (bf16[16,2048]{1,0:T(8,128)(2,1)S(1)}, bf16[16,2048]{1,0:T(8,128)(2,1)S(1)}, u32[]{:S(2)}, u32[]{:S(2)}) collective-permute-start(bf16[16,2048]{1,0:T(8,128)(2,1)S(1)} %multiply_convert_fusion.refs_0_), channel_id=1, source_target_pairs={{0,12},{4,8},{8,4},{12,0},{1,13},{5,9},{9,5},{13,1},{2,14},{6,10},... | collective-permute-start | bytes 196616 | tf_op jit(solution)/shard_map/ppermute | solution.py:371
  15.4 9.8 %collective-permute-start.7 = (bf16[16,2048]{1,0:T(8,128)(2,1)S(1)}, bf16[16,2048]{1,0:T(8,128)(2,1)S(1)}, u32[]{:S(2)}, u32[]{:S(2)}) collective-permute-start(bf16[16,2048]{1,0:T(8,128)(2,1)S(1)} %multiply_convert_fusion.refs_0_), channel_id=1, source_target_pairs={{0,8},{4,12},{8,0},{12,4},{1,9},{5,13},{9,1},{13,5},{2,10},{6,14},... | collective-permute-start | bytes 196616 | tf_op jit(solution)/shard_map/ppermute | solution.py:371
  15.4 9.8 %collective-permute-start.6 = (bf16[16,2048]{1,0:T(8,128)(2,1)S(1)}, bf16[16,2048]{1,0:T(8,128)(2,1)S(1)}, u32[]{:S(2)}, u32[]{:S(2)}) collective-permute-start(bf16[16,2048]{1,0:T(8,128)(2,1)S(1)} %multiply_convert_fusion.refs_0_), channel_id=1, source_target_pairs={{0,4},{4,0},{8,12},{12,8},{1,5},{5,1},{9,13},{13,9},{2,6},{6,2},{1... | collective-permute-start | bytes 196616 | tf_op jit(solution)/shard_map/ppermute | solution.py:371
  25.3 2.2 %collective-permute-start.9 = (f32[64,2560]{1,0:T(8,128)S(1)}, f32[64,2560]{1,0:T(8,128)S(1)}, u32[]{:S(2)}, u32[]{:S(2)}) collective-permute-start(f32[64,2560]{1,0:T(8,128)S(1)} %get-tuple-element.60.refs_7_), channel_id=1, source_target_pairs={{0,1},{1,0},{2,3},{3,2},{4,5},{5,4},{6,7},{7,6},{8,9},{9,8},{10,11... | collective-permute-start | bytes 1966088 | tf_op jit(solution)/shard_map/ppermute | solution.py:371
  27.4 6.7 %collective-permute-start.10 = (f32[64,2560]{1,0:T(8,128)S(1)}, f32[64,2560]{1,0:T(8,128)S(1)}, u32[]{:S(2)}, u32[]{:S(2)}) collective-permute-start(f32[64,2560]{1,0:T(8,128)S(1)} %gate_up_diagonal.1), channel_id=1, source_target_pairs={{0,1},{1,0},{2,3},{3,2},{4,5},{5,4},{6,7},{7,6},{8,9},{9,8},{10,11... | collective-permute-start | bytes 1966088 | tf_op jit(solution)/shard_map/ppermute | solution.py:371
  27.9 6.3 %collective-permute-start.11 = (bf16[64,1280]{1,0:T(8,128)(2,1)S(1)}, bf16[64,1280]{1,0:T(8,128)(2,1)S(1)}, u32[]{:S(2)}, u32[]{:S(2)}) collective-permute-start(bf16[64,1280]{1,0:T(8,128)(2,1)S(1)} %add_convert_fusion.1.refs_6_), channel_id=1, source_target_pairs={{0,2},{1,3},{2,0},{3,1},{4,6},{5,7},{6,4},{7,5},{8,10},{9,11},{10,... | collective-permute-start | bytes 491528 | tf_op jit(solution)/shard_map/ppermute | solution.py:371
  34.2 9.5 %collective-permute-start.12 = (bf16[64,2560]{1,0:T(8,128)(2,1)S(1)}, bf16[64,2560]{1,0:T(8,128)(2,1)S(1)}, u32[]{:S(2)}, u32[]{:S(2)}) collective-permute-start(bf16[64,2560]{1,0:T(8,128)(2,1)S(1)} %add_convert_fusion.refs_6_), channel_id=1, source_target_pairs={{0,2},{1,3},{2,0},{3,1},{4,6},{5,7},{6,4},{7,5},{8,10},{9,11},{10,... | collective-permute-start | bytes 983048 | tf_op jit(solution)/shard_map/ppermute | solution.py:371
  43.7 1.6 %collective-permute-start.13 = (bf16[64,2560]{1,0:T(8,128)(2,1)S(1)}, bf16[64,2560]{1,0:T(8,128)(2,1)S(1)}, u32[]{:S(2)}, u32[]{:S(2)}) collective-permute-start(bf16[64,2560]{1,0:T(8,128)(2,1)S(1)} %get-tuple-element.67), channel_id=1, source_target_pairs={{0,1},{1,0},{2,3},{3,2},{4,5},{5,4},{6,7},{7,6},{8,9},{9,8},{10,11... | collective-permute-start | bytes 983048 | tf_op jit(solution)/shard_map/ppermute | solution.py:371
  45.8 1.7 %collective-permute-start.14 = (bf16[64,2688]{1,0:T(8,128)(2,1)S(1)}, bf16[64,2688]{1,0:T(8,128)(2,1)S(1)}, u32[]{:S(2)}, u32[]{:S(2)}) collective-permute-start(bf16[64,2688]{1,0:T(8,128)(2,1)S(1)} %get-tuple-element.71.refs_0_), channel_id=1, source_target_pairs={{0,1},{1,0},{2,3},{3,2},{4,5},{5,4},{6,7},{7,6},{8,9},{9,8},{10,11... | collective-permute-start | bytes 1032200 | tf_op jit(solution)/shard_map/ppermute | solution.py:371
  45.9 10.3 %collective-permute-start.15 = (bf16[64,2688]{1,0:T(8,128)(2,1)S(1)}, bf16[64,2688]{1,0:T(8,128)(2,1)S(1)}, u32[]{:S(2)}, u32[]{:S(2)}) collective-permute-start(bf16[64,2688]{1,0:T(8,128)(2,1)S(1)} %get-tuple-element.71.refs_0_), channel_id=1, source_target_pairs={{0,2},{1,3},{2,0},{3,1},{4,6},{5,7},{6,4},{7,5},{8,10},{9,11},{10,... | collective-permute-start | bytes 1032200 | tf_op jit(solution)/shard_map/ppermute | solution.py:371
  56.3 4.2 %collective-permute-start.16 = (bf16[64,2688]{1,0:T(8,128)(2,1)S(1)}, bf16[64,2688]{1,0:T(8,128)(2,1)S(1)}, u32[]{:S(2)}, u32[]{:S(2)}) collective-permute-start(bf16[64,2688]{1,0:T(8,128)(2,1)S(1)} %collective-permute-done.15.refs_0_), channel_id=1, source_target_pairs={{0,1},{1,0},{2,3},{3,2},{4,5},{5,4},{6,7},{7,6},{8,9},{9,8},{10,11... | collective-permute-start | bytes 1032200 | tf_op jit(solution)/shard_map/ppermute | solution.py:371
  63.7 6.9 %collective-permute-start.17 = (bf16[16,2176]{1,0:T(8,128)(2,1)S(1)}, bf16[16,2176]{1,0:T(8,128)(2,1)S(1)}, u32[]{:S(2)}, u32[]{:S(2)}) collective-permute-start(bf16[16,2176]{1,0:T(8,128)(2,1)S(1)} %get-tuple-element.80), channel_id=1, source_target_pairs={{0,12},{4,8},{8,4},{12,0},{1,13},{5,9},{9,5},{13,1},{2,14},{6,10},... | collective-permute-start | bytes 208904 | tf_op jit(solution)/shard_map/ppermute | solution.py:371
  67.4 6.1 %collective-permute-start.18 = (bf16[16,2176]{1,0:T(8,128)(2,1)S(1)}, bf16[16,2176]{1,0:T(8,128)(2,1)S(1)}, u32[]{:S(2)}, u32[]{:S(2)}) collective-permute-start(bf16[16,2176]{1,0:T(8,128)(2,1)S(1)} %get-tuple-element.81), channel_id=1, source_target_pairs={{0,8},{4,12},{8,0},{12,4},{1,9},{5,13},{9,1},{13,5},{2,10},{6,14},... | collective-permute-start | bytes 208904 | tf_op jit(solution)/shard_map/ppermute | solution.py:371
  67.4 6.1 %collective-permute-start.19 = (bf16[16,2176]{1,0:T(8,128)(2,1)S(1)}, bf16[16,2176]{1,0:T(8,128)(2,1)S(1)}, u32[]{:S(2)}, u32[]{:S(2)}) collective-permute-start(bf16[16,2176]{1,0:T(8,128)(2,1)S(1)} %get-tuple-element.82), channel_id=1, source_target_pairs={{0,4},{4,0},{8,12},{12,8},{1,5},{5,1},{9,13},{13,9},{2,6},{6,2},{1... | collective-permute-start | bytes 208904 | tf_op jit(solution)/shard_map/ppermute | solution.py:371
